TPU v7x, 128 devices: a whole 4x4x4 slice. The times are simulated.
128 devices in a mesh: replica: 8 (over x, y_lo), shard: 16 (over z, y_hi, core).
Axes of the slice: x: 4, y: 4 (y_hi: 2, y_lo: 2; y = y_hi * 2 + y_lo), z: 4, core: 2. Of those that a mesh axis runs over, the one named last changes fastest.
Arguments:
- tokens: bfloat16 [65536, 4096], P(('replica', 'shard')), may hold values from -6 to 6
- cotangent: bfloat16 [65536, 2048], P(('replica', 'shard')), may hold values from -6 to 6
- next_weight: bfloat16 [8, 4096, 2048], P('replica', 'shard'), may hold values from -6 to 6
- inner_weight: float32 [8, 4096, 4096], P('replica', 'shard'), may hold values from -23 to 23
- outer_weight: float32 [4096, 4096], P('shard'), may hold values from -6 to 6
- momentum: float32 [4096, 4096], P('shard', 'replica'), may hold values from -1.8 to 1.8
Outputs:
- input_grad: bfloat16 [65536, 4096], P(('replica', 'shard'))
- weight_grad: float32 [8, 4096, 2048], P('replica', 'shard')
- new_outer: float32 [4096, 4096], P('shard', 'replica')
- new_momentum: float32 [4096, 4096], P('shard', 'replica')
- new_inner: bfloat16 [4096, 4096], P('shard')
All inputs are finite; a program needn't handle non-finite values.
Results may differ from a plain program's by a relative error of at most 0.015.
Values may be sent and summed in bfloat16 or wider, within the bound.
No kernel may reach another device: no remote copies, remote signals or barrier semaphores. Data moves between devices by JAX's collectives and lax.ppermute only.
A program may use at most 192 MiB of HBM per device.

v0:
```python
import jax
import jax.numpy as jnp
from jax import lax
from jax.sharding import PartitionSpec as P


def decode_local(codes, scale_back, rows_here, full_cols):
    return (codes.astype(jnp.float32) * scale_back[:, :, None]).reshape(rows_here, full_cols)


def shards(tokens, cotangent, next_weight, inner_weight, outer_weight, momentum):
    factor = tokens.shape[1] ** (-0.5)
    whole_weight = lax.all_gather(next_weight[0], "shard", axis=0, tiled=True)
    pre = jnp.dot(tokens, whole_weight, preferred_element_type=jnp.float32) * factor
    sig = jax.nn.sigmoid(pre)
    slope = (cotangent.astype(jnp.float32) * sig * (1.0 + pre * (1.0 - sig))).astype(jnp.bfloat16)
    input_grad = (
        jnp.dot(slope, whole_weight.T, preferred_element_type=jnp.float32) * factor
    ).astype(jnp.bfloat16)
    summed = lax.psum_scatter(
        lax.dot_general(
            tokens, slope, (((0,), (0,)), ((), ())), preferred_element_type=jnp.float32
        ).astype(jnp.bfloat16),
        "shard",
        scatter_dimension=0,
        tiled=True,
    ).astype(jnp.float32)
    weight_grad = (summed * factor)[None]
    rows_here, full_cols = outer_weight.shape
    share_cols = momentum.shape[1]
    groups = full_cols // 128
    replicas = lax.axis_size("replica")
    position = lax.axis_index("replica")
    delta = (outer_weight - inner_weight[0]).reshape(rows_here, groups, 128)
    top = jnp.max(jnp.abs(delta), axis=2) + 1e-06
    scale_bf = top.astype(jnp.bfloat16)
    scale_back = lax.optimization_barrier(scale_bf).astype(jnp.float32)
    codes = (delta / scale_back[:, :, None]).astype(jnp.bfloat16)
    decoded = decode_local(codes, scale_back, rows_here, full_cols)
    total = lax.psum(decoded.astype(jnp.bfloat16), "replica").astype(jnp.float32)
    total_share = lax.dynamic_slice_in_dim(total, position * share_cols, share_cols, 1)
    average = total_share / replicas
    outer_share = lax.dynamic_slice_in_dim(outer_weight, position * share_cols, share_cols, 1)
    new_momentum = 0.9 * momentum + average
    new_outer = outer_share - 0.7 * (average + 0.9 * new_momentum)
    new_inner = lax.all_gather(new_outer.astype(jnp.bfloat16), "replica", axis=1, tiled=True)
    return (input_grad, weight_grad, new_outer, new_momentum, new_inner)


def solution(mesh):
    return jax.shard_map(
        shards,
        mesh=mesh,
        in_specs=(
            P(("replica", "shard"), None),
            P(("replica", "shard"), None),
            P("replica", "shard", None),
            P("replica", "shard", None),
            P("shard", None),
            P("shard", "replica"),
        ),
        out_specs=(
            P(("replica", "shard"), None),
            P("replica", "shard", None),
            P("shard", "replica"),
            P("shard", "replica"),
            P("shard", None),
        ),
        check_vma=False,
    )
```

profile of v0, /device:TPU:1, one launch (start us, length us, event | category | flops | bytes accessed | tf_op | source)
XLA Modules:
  0.0 409.7 jit_solution(9290833359949838054)
XLA Ops:
  8.0 0.0 all-reduce.2.cloned.1.call-start
  8.0 4.1 abs_bitcast_fusion
  12.1 2.8 copy.12
  14.9 3.3 reduce_max.9
  18.2 0.0 copy-start
  18.2 1.1 div.21
  19.4 1.0 copy-done
  20.4 0.0 copy-start.1
  20.4 7.0 %fusion.7 = bf16[256,4096]{1,0:T(8,128)(2,1)} fusion(f32[32,8,32,128]{3,2,1,0:T(8,128)S(1)} %bitcast.32, f32[256,4096]{1,0:T(8,128)S(1)} %copy-done, f32[1,256,4096]{2,1,0:T(8,128)} %param.9), kind=kLoop, calls=%fused_computation.9 | loop fusion | flops 6291456 | bytes 14680064 | tf_op jit(solution)/shard_map/convert_element_type | solution.py:40
  27.4 0.0 all-reduce.2.cloned.1.call-update
  27.4 0.0 all-gather.6.cloned.1.call-start
  27.5 0.5 all-gather.6.cloned.1.call-update
  28.0 0.0 all-gather.4.cloned.1.call-start
  28.1 162.3 %all-reduce.2.cloned.1.call-done = bf16[256,4096]{1,0:T(8,128)(2,1)} async-done(((bf16[256,4096]{1,0:T(8,128)(2,1)}), bf16[256,4096]{1,0:T(8,128)(2,1)}) %all-reduce.2.cloned.1.call-update) | async-done | bytes 2097168 | tf_op jit(solution)/shard_map/psum | solution.py:40
  190.3 0.0 copy-done.1
  190.3 2.3 fusion.18
  192.7 0.0 all-gather.4.cloned.1.call-update
  192.7 0.0 copy-start.3
  192.7 0.2 reduce-scatter.2.cloned.1.call-start
  193.0 0.0 all-gather.6.cloned.1.call-done
  193.0 0.0 copy-start.2
  193.0 15.2 %fusion.2 = f32[512,2048]{1,0:T(8,128)} fusion(bf16[512,4096]{1,0:T(8,128)(2,1)} %param.6, bf16[1,4096,2048]{2,1,0:T(8,128)(2,1)} %all-gather.6.cloned.1.call-done), kind=kOutput, calls=%fused_computation.2 | convolution fusion | flops 8589934592 | bytes 25165824 | tf_op jit(solution)/shard_map/dot_general | solution.py:14
  208.2 0.0 copy-done.3
  208.2 0.0 copy-done.2
  208.2 17.5 %convert_bitcast_fusion = bf16[4096,2048]{0,1:T(8,128)(2,1)} fusion(bf16[512,4096]{1,0:T(8,128)(2,1)S(1)} %copy-done.2, f32[512,2048]{1,0:T(8,128)} %fusion.2, bf16[512,2048]{1,0:T(8,128)(2,1)S(1)} %copy-done.3), kind=kOutput, calls=%fused_computation.4 | convolution fusion | flops 8609857536 | bytes 27262976 | tf_op jit(solution)/shard_map/dot_general | solution.py:21
  225.7 0.0 reduce-scatter.2.cloned.1.call-update
  225.7 19.4 %all-gather.4.cloned.1.call-done = bf16[256,4096]{1,0:T(8,128)(2,1)} async-done(((bf16[256,512]{1,0:T(8,128)(2,1)}), bf16[256,4096]{1,0:T(8,128)(2,1)}) %all-gather.4.cloned.1.call-update) | async-done | bytes 2097168 | tf_op jit(solution)/shard_map/all_gather | solution.py:46
  245.1 16.4 %multiply_convert_fusion = bf16[512,4096]{1,0:T(8,128)(2,1)} fusion(bf16[1,4096,2048]{2,1,0:T(8,128)(2,1)} %all-gather.6.cloned.1.call-done, f32[512,2048]{1,0:T(8,128)} %fusion.2, bf16[512,2048]{1,0:T(8,128)(2,1)S(1)} %copy-done.3), kind=kOutput, calls=%fused_computation.5 | convolution fusion | flops 8605663232 | bytes 27262976 | tf_op jit(solution)/shard_map/dot_general | solution.py:18
  261.6 134.2 %reduce-scatter.2.cloned.1.call-done = bf16[256,2048]{0,1:T(8,128)(2,1)} async-done(((bf16[4096,2048]{0,1:T(8,128)(2,1)}), bf16[256,2048]{0,1:T(8,128)(2,1)}) %reduce-scatter.2.cloned.1.call-update) | async-done | bytes 1048592 | tf_op jit(solution)/shard_map/reduce_scatter | solution.py:20
  395.8 1.4 multiply_bitcast_fusion
  397.1 1.8 copy.11
  399.0 3.1 copy.20
  (1 shorter events, 0.0 us)
Async XLA Ops:
  8.0 182.3 %all-reduce.2.cloned.1.call-start = ((), (), s32[]{:S(2)}) async-start(), calls=%async_computation.2 | async-start | bytes 4194304 | tf_op jit(solution)/shard_map/psum | solution.py:40
  18.2 2.2 copy-start
  20.4 169.9 %copy-start.1 = (f32[256,512]{1,0:T(8,128)S(1)}, f32[256,512]{1,0:T(8,128)}, u32[]{:S(2)}) copy-start(f32[256,512]{1,0:T(8,128)} %param.11) | copy-start | bytes 1572868
  27.4 165.6 %all-gather.6.cloned.1.call-start = ((), (), s32[]{:S(2)}) async-start(), calls=%async_computation.4 | async-start | bytes 17825792 | tf_op jit(solution)/shard_map/all_gather | solution.py:13
  28.0 217.1 %all-gather.4.cloned.1.call-start = ((), (), s32[]{:S(2)}) async-start(), calls=%async_computation.3 | async-start | bytes 2359296 | tf_op jit(solution)/shard_map/all_gather | solution.py:46
  192.7 15.5 %copy-start.3 = (bf16[512,2048]{1,0:T(8,128)(2,1)S(1)}, bf16[512,2048]{1,0:T(8,128)(2,1)}, u32[]{:S(2)}) copy-start(bf16[512,2048]{1,0:T(8,128)(2,1)} %param.7) | copy-start | bytes 6291460
  192.7 203.1 %reduce-scatter.2.cloned.1.call-start = ((), (), s32[]{:S(2)}) async-start(), calls=%async_computation.1 | async-start | bytes 17825792 | tf_op jit(solution)/shard_map/reduce_scatter | solution.py:20
  193.0 15.2 %copy-start.2 = (bf16[512,4096]{1,0:T(8,128)(2,1)S(1)}, bf16[512,4096]{1,0:T(8,128)(2,1)}, u32[]{:S(2)}) copy-start(bf16[512,4096]{1,0:T(8,128)(2,1)} %param.6) | copy-start | bytes 12582916
Sparse Core Ops, SparseCore 0:
  27.5 162.7 all-reduce.1
Sparse Core Ops, SparseCore 1:
  30.4 121.2 all-gather.5
  192.8 52.3 all-gather.3
  249.3 146.4 reduce-scatter.1
where the time goes:
time: 410 us
  waiting for transfers between devices  317 us (77%)
  matrix products  49.1 us (12%)
  other arithmetic  18.1 us (4%)
  between operations  15.7 us (4%)
  local copies, waits for them, and re-layouts  9.87 us (2%)
    psum x1, waiting for transfers between devices, shards(): lax.psum(decoded.astype(jnp.bfloat16), 'replica').astype(jnp.float32)  162 us
    reduce_scatter x1, waiting for transfers between devices, shards(): lax.psum_scatter(lax.dot_general(tokens, slope, (((0,), (0,)), ((), ())),...  134 us
    all_gather x1, waiting for transfers between devices, shards(): lax.all_gather(new_outer.astype(jnp.bfloat16), 'replica', axis=1, tiled=T...  19.4 us
    dot_general x1, matrix products, shards(): lax.dot_general(tokens, slope, (((0,), (0,)), ((), ())), preferred_elemen...  17.5 us
    dot_general x1, matrix products, shards(): jnp.dot(slope, whole_weight.T, preferred_element_type=jnp.float32) * factor  16.4 us
    dot_general x1, matrix products, shards(): jnp.dot(tokens, whole_weight, preferred_element_type=jnp.float32) * factor  15.2 us
    unnamed x11, local copies, waits for them, and re-layouts  8.73 us
  transfers between devices with their start and end apart: 4, of which 3 were waited for; matrix products, arithmetic and copies ran while one was open for 13% of the time, Pallas kernels for 0%

commit v1 on v0

v1 whole, which is shorter than its diff:
```python
import functools

import jax
import jax.numpy as jnp
from jax import lax
from jax.experimental import pallas as pl
from jax.experimental.pallas import tpu as pltpu
from jax.sharding import PartitionSpec as P

F32 = jnp.float32
BF16 = jnp.bfloat16
MIB = 1 << 20

NZ, NY, NC, NX, NL = 4, 2, 2, 4, 2
DIRS = [(dz, dy) for dz in range(NZ) for dy in range(NY)]


def shard_perm(dz, dy, dc):
    perm = []
    for i in range(NZ * NY * NC):
        z, y, c = i // (NY * NC), (i // NC) % NY, i % NC
        j = ((z + dz) % NZ) * NY * NC + ((y + dy) % NY) * NC + (c + dc) % NC
        perm.append((i, j))
    return perm


def replica_perm(dx, dl):
    perm = []
    for i in range(NX * NL):
        x, w = i // NL, i % NL
        perm.append((i, ((x + dx) % NX) * NL + (w + dl) % NL))
    return perm


def to_zp(a):
    return lax.ppermute(a, "shard", shard_perm(1, 0, 0))


def to_zm(a):
    return lax.ppermute(a, "shard", shard_perm(-1, 0, 0))


def to_y(a):
    return lax.ppermute(a, "shard", shard_perm(0, 1, 0))


def to_core(a):
    return lax.ppermute(a, "shard", shard_perm(0, 0, 1))


def to_x(a, dx):
    return lax.ppermute(a, "replica", replica_perm(dx, 0))


def to_l(a):
    return lax.ppermute(a, "replica", replica_perm(0, 1))


def add(*terms):
    total = terms[0].astype(F32)
    for term in terms[1:]:
        total = total + term.astype(F32)
    return total


def whole(shape):
    return pl.BlockSpec(shape, lambda i, *_: (0,) * len(shape))


def cost(flops, nbytes, trans=0):
    return pl.CostEstimate(flops=int(flops), bytes_accessed=int(nbytes), transcendentals=int(trans))


def params(mib):
    return pltpu.CompilerParams(vmem_limit_bytes=mib * MIB)


def decode_kernel(pos_ref, outer_ref, inner_ref, *out_refs):
    dx = pl.program_id(0)
    width = outer_ref.shape[1]
    for g in range(width // 128):
        cols = slice(g * 128, (g + 1) * 128)
        delta = outer_ref[:, cols] - inner_ref[0, :, cols]
        top = jnp.max(jnp.abs(delta), axis=1, keepdims=True) + 1e-06
        scale = top.astype(BF16).astype(F32)
        code = (delta / scale).astype(BF16).astype(F32)
        decoded = (code * scale).astype(BF16)
        for k, out_ref in enumerate(out_refs):
            @pl.when(dx == k)
            def _(out_ref=out_ref, decoded=decoded, cols=cols):
                out_ref[:, cols] = decoded


def decode(x_pos, outer, inner):
    rows, cols = outer.shape
    width = cols // NX
    return pl.pallas_call(
        decode_kernel,
        grid_spec=pltpu.PrefetchScalarGridSpec(
            num_scalar_prefetch=1,
            grid=(NX,),
            in_specs=[
                pl.BlockSpec((rows, width), lambda i, p: (0, lax.rem(p[0] + i, NX))),
                pl.BlockSpec((1, rows, width), lambda i, p: (0, 0, lax.rem(p[0] + i, NX))),
            ],
            out_specs=[whole((rows, width))] * NX,
        ),
        out_shape=[jax.ShapeDtypeStruct((rows, width), BF16)] * NX,
        compiler_params=params(32),
        cost_estimate=cost(10 * rows * cols, 10 * rows * cols),
        name="decode",
    )(x_pos, outer, inner)


def slope_kernel(factor, npieces, off_ref, xo_ref, xp_ref, co_ref, cp_ref, *refs):
    piece_refs, so_ref, sp_ref = refs[:npieces], refs[npieces], refs[npieces + 1]
    for x_ref, cot_ref, out_ref in ((xo_ref, co_ref, so_ref), (xp_ref, cp_ref, sp_ref)):
        pre = None
        for k in range(npieces):
            depth = piece_refs[k].shape[0]
            cols = pl.ds(pl.multiple_of(off_ref[k], 256), depth)
            term = jnp.dot(x_ref[:, cols], piece_refs[k][...], preferred_element_type=F32)
            pre = term if pre is None else pre + term
        pre = pre * factor
        sig = 1.0 / (1.0 + jnp.exp(-pre))
        out_ref[...] = (cot_ref[...].astype(F32) * sig * (1.0 + pre * (1.0 - sig))).astype(BF16)


def slope_of(factor, offs, cot_block, x_own, x_par, cot_own, cot_par, j, pieces):
    toks, feats = x_own.shape
    width = pieces[0].shape[1]
    tile = 256
    n = len(pieces)
    scalars = jnp.concatenate([offs, cot_block[None]]).astype(jnp.int32)
    return pl.pallas_call(
        functools.partial(slope_kernel, factor, n),
        grid_spec=pltpu.PrefetchScalarGridSpec(
            num_scalar_prefetch=1,
            grid=(toks // tile,),
            in_specs=[
                pl.BlockSpec((tile, feats), lambda i, s: (i, 0)),
                pl.BlockSpec((tile, feats), lambda i, s: (i, 0)),
                pl.BlockSpec((tile, width), lambda i, s: (i, s[n])),
                pl.BlockSpec((tile, width), lambda i, s: (i, j)),
            ] + [whole(p.shape) for p in pieces],
            out_specs=[pl.BlockSpec((tile, width), lambda i, s: (i, 0))] * 2,
        ),
        out_shape=[jax.ShapeDtypeStruct((toks, width), BF16)] * 2,
        compiler_params=params(48),
        cost_estimate=cost(4 * toks * feats * width, 4 * toks * feats + 2 * feats * width, 2 * toks * width),
        name="slope",
    )(scalars, x_own, x_par, cot_own, cot_par, *pieces)


def wgrad_kernel(blk_ref, xo_ref, xp_ref, so_ref, sp_ref, *out_refs):
    d = pl.program_id(0)
    dims = (((0,), (0,)), ((), ()))
    term = lax.dot_general(xo_ref[...], so_ref[...], dims, preferred_element_type=F32)
    term = term + lax.dot_general(xp_ref[...], sp_ref[...], dims, preferred_element_type=F32)
    term = term.astype(BF16)
    for k, out_ref in enumerate(out_refs):
        @pl.when(d == k)
        def _(out_ref=out_ref):
            out_ref[...] = term


def wgrad_of(blks, x_own, x_par, s_own, s_par):
    toks, feats = x_own.shape
    width = s_own.shape[1]
    n = blks.shape[0]
    rows = feats // (NZ * NY)
    return pl.pallas_call(
        wgrad_kernel,
        grid_spec=pltpu.PrefetchScalarGridSpec(
            num_scalar_prefetch=1,
            grid=(n,),
            in_specs=[
                pl.BlockSpec((toks, rows), lambda i, b: (0, b[i])),
                pl.BlockSpec((toks, rows), lambda i, b: (0, b[i])),
                whole((toks, width)),
                whole((toks, width)),
            ],
            out_specs=[whole((rows, width))] * n,
        ),
        out_shape=[jax.ShapeDtypeStruct((rows, width), BF16)] * n,
        compiler_params=params(32),
        cost_estimate=cost(4 * toks * n * rows * width, 4 * toks * n * rows + 2 * n * rows * width),
        name="wgrad",
    )(blks, x_own, x_par, s_own, s_par)


def igrad_kernel(factor, na, nb, has_term, off_ref, sa_ref, sb_ref, *refs):
    a_refs, b_refs = refs[:na], refs[na:na + nb]
    term_ref = refs[na + nb] if has_term else None
    out_ref = refs[-1]
    dims = (((1,), (1,)), ((), ()))
    sa, sb = sa_ref[...], sb_ref[...]
    k = 0
    for a_ref in a_refs:
        depth = a_ref.shape[0]
        cols = pl.ds(pl.multiple_of(off_ref[k], 256), depth)
        total = lax.dot_general(sa, a_ref[...], dims, preferred_element_type=F32)
        if has_term:
            total = total + term_ref[:, cols].astype(F32)
        first, filled = k, 0
        parts = []
        while filled < depth:
            b_ref = b_refs[k]
            parts.append(lax.dot_general(sb, b_ref[...], dims, preferred_element_type=F32))
            filled += b_ref.shape[0]
            k += 1
        total = total + (parts[0] if len(parts) == 1 else jnp.concatenate(parts, axis=1))
        if has_term:
            total = total * factor
        out_ref[:, cols] = total.astype(BF16)


def igrad_of(factor, offs, s_a, s_b, a, b, term):
    toks, width = s_a.shape
    feats = sum(p.shape[0] for p in a)
    tile = 256
    extra = [] if term is None else [term]
    return pl.pallas_call(
        functools.partial(igrad_kernel, factor, len(a), len(b), term is not None),
        grid_spec=pltpu.PrefetchScalarGridSpec(
            num_scalar_prefetch=1,
            grid=(toks // tile,),
            in_specs=[pl.BlockSpec((tile, width), lambda i, s: (i, 0))] * 2
            + [whole(p.shape) for p in list(a) + list(b)]
            + [pl.BlockSpec((tile, feats), lambda i, s: (i, 0)) for _ in extra],
            out_specs=pl.BlockSpec((tile, feats), lambda i, s: (i, 0)),
        ),
        out_shape=jax.ShapeDtypeStruct((toks, feats), BF16),
        compiler_params=params(48),
        cost_estimate=cost(4 * toks * feats * width, 2 * toks * feats + 4 * feats * width),
        name="igrad",
    )(offs, s_a, s_b, *a, *b, *extra)


def by_core(core, mine, other, axis):
    return jnp.where(
        core == 0,
        jnp.concatenate([mine, other], axis=axis),
        jnp.concatenate([other, mine], axis=axis),
    )


def shards(tokens, cotangent, next_weight, inner_weight, outer_weight, momentum):
    toks, feats = tokens.shape
    factor = feats ** (-0.5)
    me = lax.axis_index("shard")
    z, y, core = me // (NY * NC), (me // NC) % NY, me % NC
    pos = lax.axis_index("replica")
    x, low = pos // NL, pos % NL

    blk = {(dz, dy): ((z + dz) % NZ) * NY + (y + dy) % NY for dz, dy in DIRS}
    rows = feats // (NZ * NY)
    half = rows // 2
    cols = next_weight.shape[2] // NC
    chunk = cols // 2
    my_rows = next_weight[0]

    keep = lax.dynamic_slice_in_dim(my_rows, core * cols, cols, 1)
    give = lax.dynamic_slice_in_dim(my_rows, (1 - core) * cols, cols, 1)
    got = to_core(give)
    a0 = by_core(core, keep[:, :chunk], got[:, :chunk], 0)
    b0 = by_core(core, keep[:, chunk:], got[:, chunk:], 0)

    a, b = {(0, 0): a0}, {(0, 0): [b0]}
    a[0, 1] = to_y(a0)
    b[3, 0] = [to_zp(b0)]
    b[1, 0] = [to_zm(b0)]
    a[3, 0] = to_zp(a0)
    a[1, 0] = to_zm(a0)
    b[2, 0] = [to_zp(b[3, 0][0][:half]), to_zm(b[1, 0][0][half:])]
    a[3, 1] = to_zp(a[0, 1])
    a[1, 1] = to_zm(a[0, 1])
    a[2, 0] = to_zp(a[3, 0])
    a[2, 1] = to_zm(a[1, 1])
    for dz in (0, 3, 1, 2):
        b[dz, 1] = [to_y(part) for part in b[dz, 0]]

    x_par = to_core(tokens)
    cot_par = to_core(lax.dynamic_slice_in_dim(cotangent, (1 - core) * cols, cols, 1))

    a_list = [a[d] for d in DIRS]
    b_list = [part for d in DIRS for part in b[d]]
    a_offs = jnp.stack([blk[d] * rows for d in DIRS]).astype(jnp.int32)
    b_offs = jnp.stack(
        [blk[d] * rows + (h * half) for d in DIRS for h in range(len(b[d]))]
    ).astype(jnp.int32)
    blks = jnp.stack([blk[d] for d in DIRS]).astype(jnp.int32)

    dec = decode(x[None].astype(jnp.int32), outer_weight, inner_weight)
    rec = [to_x(dec[dx], dx) for dx in (1, 2, 3)]
    x_sum = add(dec[0], *rec)
    share = momentum.shape[1]
    mine = lax.dynamic_slice_in_dim(x_sum, low * share, share, 1)
    other = lax.dynamic_slice_in_dim(x_sum, (1 - low) * share, share, 1)
    total = mine + to_l(other.astype(BF16)).astype(F32)
    average = total / (NX * NL)
    outer_share = lax.dynamic_slice_in_dim(outer_weight, pos * share, share, 1)
    new_momentum = 0.9 * momentum + average
    new_outer = outer_share - 0.7 * (average + 0.9 * new_momentum)
    inner_share = new_outer.astype(BF16)
    inner_pair = by_core(low, inner_share, to_l(inner_share), 1)
    new_inner = jnp.zeros(outer_weight.shape, BF16)
    for dx in range(NX):
        part = inner_pair if dx == 0 else to_x(inner_pair, dx)
        at = ((x - dx) % NX) * (share * NL)
        new_inner = lax.dynamic_update_slice_in_dim(new_inner, part, at, 1)

    sa_own, sa_par = slope_of(
        factor, a_offs, core * 2, tokens, x_par, cotangent, cot_par, 0, a_list
    )
    ga = dict(zip(DIRS, wgrad_of(blks, tokens, x_par, sa_own, sa_par)))
    sb_own, sb_par = slope_of(
        factor, b_offs, core * 2 + 1, tokens, x_par, cotangent, cot_par, 1, b_list
    )
    gb = dict(zip(DIRS, wgrad_of(blks, tokens, x_par, sb_own, sb_par)))

    t0 = to_zm(ga[2, 0])
    t1 = to_zp(ga[2, 1])
    up0 = to_zp(ga[1, 0])
    down1 = to_zm(ga[3, 1])
    down0 = to_zm(add(ga[3, 0], t0).astype(BF16))
    up1 = to_zp(add(ga[1, 1], t1).astype(BF16))
    sum1 = add(ga[0, 1], down1, up1).astype(BF16)
    a_sum = add(ga[0, 0], down0, up0, to_y(sum1))

    hb = {dz: add(gb[dz, 0], to_y(gb[dz, 1])) for dz in (2, 3, 1, 0)}
    top = to_zm(hb[2][:half].astype(BF16))
    bot = to_zp(hb[2][half:].astype(BF16))
    down = to_zm(
        jnp.concatenate([add(hb[3][:half], top), hb[3][half:]], axis=0).astype(BF16)
    )
    up = to_zp(
        jnp.concatenate([hb[1][:half], add(hb[1][half:], bot)], axis=0).astype(BF16)
    )
    b_sum = add(hb[0], down, up)

    def split(total_sum):
        keep_rows = lax.dynamic_slice_in_dim(total_sum, core * half, half, 0)
        give_rows = lax.dynamic_slice_in_dim(total_sum, (1 - core) * half, half, 0)
        return keep_rows * factor, to_core(give_rows) * factor

    a_mine, a_got = split(a_sum)
    b_mine, b_got = split(b_sum)
    weight_grad = by_core(
        core,
        jnp.concatenate([a_mine, b_mine], axis=1),
        jnp.concatenate([a_got, b_got], axis=1),
        1,
    )[None]

    part = igrad_of(factor, b_offs, sa_par, sb_par, a_list, b_list, None)
    input_grad = igrad_of(factor, b_offs, sa_own, sb_own, a_list, b_list, to_core(part))
    return (input_grad, weight_grad, new_outer, new_momentum, new_inner)


def solution(mesh):
    return jax.shard_map(
        shards,
        mesh=mesh,
        in_specs=(
            P(("replica", "shard"), None),
            P(("replica", "shard"), None),
            P("replica", "shard", None),
            P("replica", "shard", None),
            P("shard", None),
            P("shard", "replica"),
        ),
        out_specs=(
            P(("replica", "shard"), None),
            P("replica", "shard", None),
            P("shard", "replica"),
            P("shard", "replica"),
            P("shard", None),
        ),
        check_vma=False,
    )
```

time: 410 us -> 259 us (0.63)
  waiting for transfers between devices: 317 us -> 94.7 us
  starting transfers between devices: 0.35 us -> 73.2 us
  Pallas kernels: 0 us -> 63.6 us
  matrix products: 49.1 us -> 0 us
  between operations: 15.7 us -> 1.12 us
  other arithmetic: 18.1 us -> 9.77 us
    psum x1 -> x0, waiting for transfers between devices: 162 us -> none  [shards(): lax.psum(decoded.astype(jnp.bfloat16), 'replica').astype(jnp.float32)]
    reduce_scatter x1 -> x0, waiting for transfers between devices: 134 us -> none  [shards(): lax.psum_scatter(lax.dot_general(tokens, slope, (((0,), (0,)), ((), ())),...]
    ppermute x0 -> x45, waiting for transfers between devices: none -> 94.7 us  [the longest x10 34.7 us: to_zp(): return lax.ppermute(a, 'shard', shard_perm(1, 0, 0))]
    ppermute x0 -> x45, starting transfers between devices: none -> 73.2 us  [the longest x11 19.7 us: to_y(): return lax.ppermute(a, 'shard', shard_perm(0, 1, 0))]
    pallas_call x0 -> x7, Pallas kernels: none -> 63.6 us  [the longest x2 20.4 us: wgrad_of(): pl.pallas_call(wgrad_kernel, grid_spec=pltpu.PrefetchScalarGridSpec(num_s...]
    dot_general x3 -> x0, matrix products: 49.1 us -> none  [the longest x1 17.5 us: shards(): lax.dot_general(tokens, slope, (((0,), (0,)), ((), ())), preferred_elemen...]
    all_gather x2 -> x0, waiting for transfers between devices: 19.5 us -> none  [the longest x1 19.4 us: shards(): lax.all_gather(new_outer.astype(jnp.bfloat16), 'replica', axis=1, tiled=T...]
    convert_element_type x3 -> x4, other arithmetic: 9.36 us -> 3.18 us  [the longest x1 2.72 us: shards(): inner_share = new_outer.astype(BF16)]
  transfers between devices with their start and end apart: 4 -> 45, of which waited for: 3 -> 17; matrix products, arithmetic and copies ran while one was open for 13% -> 6% of each run, Pallas kernels for 0% -> 21%
where the time goes in v1:
time: 259 us; the launch traced here: 255 us
  waiting for transfers between devices  94.7 us (37%)
  starting transfers between devices  73.2 us (28%)
  Pallas kernels  63.6 us (25%)
  local copies, waits for them, and re-layouts  12.9 us (5%)
  other arithmetic  9.77 us (4%)
    ppermute x10, waiting for transfers between devices, to_zp(): return lax.ppermute(a, 'shard', shard_perm(1, 0, 0))  34.7 us
    ppermute x6, waiting for transfers between devices, to_x(): return lax.ppermute(a, 'replica', replica_perm(dx, 0))  23.2 us
    pallas_call x2, Pallas kernels, wgrad_of(): pl.pallas_call(wgrad_kernel, grid_spec=pltpu.PrefetchScalarGridSpec(num_s...  20.4 us
    ppermute x11, starting transfers between devices, to_y(): return lax.ppermute(a, 'shard', shard_perm(0, 1, 0))  19.7 us
    pallas_call x2, Pallas kernels, slope_of(): pl.pallas_call(functools.partial(slope_kernel, factor, n), grid_spec=pltp...  19.6 us
    ppermute x6, starting transfers between devices, to_core(): return lax.ppermute(a, 'shard', shard_perm(0, 0, 1))  19.3 us
    ppermute x11, waiting for transfers between devices, to_y(): return lax.ppermute(a, 'shard', shard_perm(0, 1, 0))  18.5 us
    pallas_call x2, Pallas kernels, igrad_of(): pl.pallas_call(functools.partial(igrad_kernel, factor, len(a), len(b), te...  18.4 us
  transfers between devices with their start and end apart: 45, of which 17 were waited for; matrix products, arithmetic and copies ran while one was open for 6% of the time, Pallas kernels for 21%

profile of v1, /device:TPU:1, one launch (start us, length us, event | category | flops | bytes accessed | tf_op | source)
XLA Modules:
  0.0 255.3 jit_solution(14020640195137888835)
XLA Ops:
  0.6 1.5 collective-permute-start
  2.1 2.1 dynamic-slice_bitcast_fusion.1
  4.2 2.2 copy-done
  6.4 2.2 copy-done.1
  8.6 5.2 %decode.1 = (bf16[256,1024]{1,0:T(8,128)(2,1)S(1)}, bf16[256,1024]{1,0:T(8,128)(2,1)S(1)}, bf16[256,1024]{1,0:T(8,128)(2,1)S(1)}, bf16[256,1024]{1,0:T(8,128)(2,1)S(1)}) custom-call(s32[1]{0:T(128)} %bitcast.26.pos_ref, f32[256,4096]{1,0:T(8,128)S(1)} %copy-done, f32[1,256,4096]{2,1,0:T(8,128)S(1)} %copy-done.1), custom_call_target="tpu_custom_call" | custom-call | flops 10485760 | bytes 10485760 | tf_op jit(solution)/shard_map/decode/pallas_call | solution.py:97
  13.8 1.4 collective-permute-start.37
  15.1 2.5 collective-permute-start.38
  17.6 1.2 collective-permute-start.39
  19.5 1.3 constant_dynamic-slice_fusion.2
  20.8 1.4 collective-permute-start.1
  22.2 1.1 fusion.5
  23.5 4.7 %collective-permute-done.37 = bf16[256,1024]{1,0:T(8,128)(2,1)} collective-permute-done((bf16[256,1024]{1,0:T(8,128)(2,1)S(1)}, bf16[256,1024]{1,0:T(8,128)(2,1)}, u32[]{:S(2)}, u32[]{:S(2)}) %collective-permute-start.37) | collective-permute-done | bytes 524320 | tf_op jit(solution)/shard_map/ppermute | solution.py:52
  28.2 3.0 %collective-permute-start.3 = (bf16[512,512]{1,0:T(8,128)(2,1)S(1)}, bf16[512,512]{1,0:T(8,128)(2,1)S(1)}, u32[]{:S(2)}, u32[]{:S(2)}) collective-permute-start(bf16[512,512]{1,0:T(8,128)(2,1)S(1)} %maximum_select_fusion.1.refs_0_), channel_id=1, source_target_pairs={{0,2},{1,3},{2,0},{3,1},{4,6},{5,7},{6,4},{7,5},{8,10},{9,11},{10,... | collective-permute-start | bytes 1572872 | tf_op jit(solution)/shard_map/ppermute | solution.py:44
  31.2 9.3 %collective-permute-done.38 = bf16[256,1024]{1,0:T(8,128)(2,1)} collective-permute-done((bf16[256,1024]{1,0:T(8,128)(2,1)S(1)}, bf16[256,1024]{1,0:T(8,128)(2,1)}, u32[]{:S(2)}, u32[]{:S(2)}) %collective-permute-start.38) | collective-permute-done | bytes 524320 | tf_op jit(solution)/shard_map/ppermute | solution.py:52
  40.5 1.7 convert_add_fusion
  42.3 1.4 collective-permute-start.40
  43.6 1.6 collective-permute-start.6
  45.5 3.3 %collective-permute-done.40 = bf16[256,512]{1,0:T(8,128)(2,1)S(1)} collective-permute-done((bf16[256,512]{1,0:T(8,128)(2,1)S(1)}, bf16[256,512]{1,0:T(8,128)(2,1)S(1)}, u32[]{:S(2)}, u32[]{:S(2)}) %collective-permute-start.40) | collective-permute-done | bytes 262176 | tf_op jit(solution)/shard_map/ppermute | solution.py:56
  48.8 1.6 collective-permute-start.13
  50.5 2.2 collective-permute-start.11
  52.7 5.4 %collective-permute-done.6.refs_6_ = bf16[512,512]{1,0:T(8,128)(2,1)S(1)} collective-permute-done((bf16[512,512]{1,0:T(8,128)(2,1)S(1)}, bf16[512,512]{1,0:T(8,128)(2,1)S(1)}, u32[]{:S(2)}, u32[]{:S(2)}) %collective-permute-start.6) | collective-permute-done | bytes 524320 | tf_op jit(solution)/shard_map/ppermute | solution.py:36
  58.0 2.6 %collective-permute-start.10 = (bf16[512,512]{1,0:T(8,128)(2,1)S(1)}, bf16[512,512]{1,0:T(8,128)(2,1)S(1)}, u32[]{:S(2)}, u32[]{:S(2)}) collective-permute-start(bf16[512,512]{1,0:T(8,128)(2,1)S(1)} %maximum_select_fusion.2.refs_0_.refs_8_), channel_id=1, source_target_pairs={{0,2},{1,3},{2,0},{3,1},{4,6},{5,7},{6,4},{7,5},{8,10},{9,11},{10,... | collective-permute-start | bytes 1572872 | tf_op jit(solution)/shard_map/ppermute | solution.py:44
  60.7 8.6 %collective-permute-done.13.refs_8_.refs_16_ = bf16[512,512]{1,0:T(8,128)(2,1)S(1)} collective-permute-done((bf16[512,512]{1,0:T(8,128)(2,1)S(1)}, bf16[512,512]{1,0:T(8,128)(2,1)S(1)}, u32[]{:S(2)}, u32[]{:S(2)}) %collective-permute-start.13) | collective-permute-done | bytes 524320 | tf_op jit(solution)/shard_map/ppermute | solution.py:36
  69.3 1.2 collective-permute-start.5
  71.6 2.4 collective-permute-start.15
  74.8 2.6 %collective-permute-start.12 = (bf16[512,512]{1,0:T(8,128)(2,1)S(1)}, bf16[512,512]{1,0:T(8,128)(2,1)}, u32[]{:S(2)}, u32[]{:S(2)}) collective-permute-start(bf16[512,512]{1,0:T(8,128)(2,1)S(1)} %collective-permute-done.11.refs_2_.refs_10_), channel_id=1, source_target_pairs={{0,2},{1,3},{2,0},{3,1},{4,6},{5,7},{6,4},{7,5},{8,10},{9,11},{10,... | collective-permute-start | bytes 1572872 | tf_op jit(solution)/shard_map/ppermute | solution.py:44
  77.4 2.2 collective-permute-start.18
  80.0 6.2 %collective-permute-done.15.refs_5_.refs_13_ = bf16[256,512]{1,0:T(8,128)(2,1)} collective-permute-done((bf16[256,512]{1,0:T(8,128)(2,1)}, bf16[256,512]{1,0:T(8,128)(2,1)}, u32[]{:S(2)}, u32[]{:S(2)}) %collective-permute-start.15) | collective-permute-done | bytes 262176 | tf_op jit(solution)/shard_map/ppermute | solution.py:40
  86.2 2.6 %collective-permute-start.16 = (bf16[256,512]{1,0:T(8,128)(2,1)S(1)}, bf16[256,512]{1,0:T(8,128)(2,1)S(1)}, u32[]{:S(2)}, u32[]{:S(2)}) collective-permute-start(bf16[256,512]{1,0:T(8,128)(2,1)S(1)} %collective-permute-done.14.refs_4_.refs_12_), channel_id=1, source_target_pairs={{0,2},{1,3},{2,0},{3,1},{4,6},{5,7},{6,4},{7,5},{8,10},{9,11},{10,... | collective-permute-start | bytes 786440 | tf_op jit(solution)/shard_map/ppermute | solution.py:44
  89.2 2.7 %fusion.2 = (bf16[256,512]{1,0:T(8,128)(2,1)}, f32[256,512]{1,0:T(8,128)}, f32[256,512]{1,0:T(8,128)}) fusion(bf16[256,512]{1,0:T(8,128)(2,1)} %copy-done.18, f32[256,1024]{1,0:T(8,128)} %copy-done.14, s32[]{:T(128)S(6)} %select_n.178, f32[256,4096]{1,0:T(8,128)} %outer_ref.1, s32[]{:T(128)S(6)} %select_n.175, f32[256,512]{1,0:T(8,128)} %param.11), kind=kLoop, calls=%fused_computation.38 | loop fusion | flops 1310720 | bytes 3145736 | tf_op jit(solution)/shard_map/convert_element_type | solution.py:305
  91.9 2.1 collective-permute-start.4
  94.0 3.7 %collective-permute-done.18.refs_9_.refs_17_ = bf16[512,512]{1,0:T(8,128)(2,1)} collective-permute-done((bf16[512,512]{1,0:T(8,128)(2,1)S(1)}, bf16[512,512]{1,0:T(8,128)(2,1)}, u32[]{:S(2)}, u32[]{:S(2)}) %collective-permute-start.18) | collective-permute-done | bytes 524320 | tf_op jit(solution)/shard_map/ppermute | solution.py:44
  97.7 5.6 %collective-permute-done.16.refs_6_.refs_14_ = bf16[256,512]{1,0:T(8,128)(2,1)S(1)} collective-permute-done((bf16[256,512]{1,0:T(8,128)(2,1)S(1)}, bf16[256,512]{1,0:T(8,128)(2,1)S(1)}, u32[]{:S(2)}, u32[]{:S(2)}) %collective-permute-start.16) | collective-permute-done | bytes 262176 | tf_op jit(solution)/shard_map/ppermute | solution.py:44
  103.3 5.5 %collective-permute-done.17.refs_7_.refs_15_ = bf16[256,512]{1,0:T(8,128)(2,1)S(1)} collective-permute-done((bf16[256,512]{1,0:T(8,128)(2,1)}, bf16[256,512]{1,0:T(8,128)(2,1)S(1)}, u32[]{:S(2)}, u32[]{:S(2)}) %collective-permute-start.17) | collective-permute-done | bytes 262176 | tf_op jit(solution)/shard_map/ppermute | solution.py:44
  109.2 9.9 %slope.3 = (bf16[512,512]{1,0:T(8,128)(2,1)S(1)}, bf16[512,512]{1,0:T(8,128)(2,1)S(1)}) custom-call(s32[11]{0:T(128)S(1)} %concatenate.68.off_ref, bf16[512,4096]{1,0:T(8,128)(2,1)} %xo_ref.7, bf16[512,4096]{1,0:T(8,128)(2,1)} %collective-permute-done.xp_ref, bf16[512,2048]{1,0:T(8,128)(2,1)} %co_ref.3, bf16[512,1024]{1,0:T(8,128)(2,1)} %copy-done.19, ...), custom_call_target="tpu_custom_call" | custom-call | flops 4294967296 | bytes 12582912 | tf_op jit(solution)/shard_map/slope/pallas_call | solution.py:135
  119.2 10.1 %wgrad.3 = (bf16[512,512]{1,0:T(8,128)(2,1)S(1)}, bf16[512,512]{1,0:T(8,128)(2,1)S(1)}, bf16[512,512]{1,0:T(8,128)(2,1)S(1)}, bf16[512,512]{1,0:T(8,128)(2,1)S(1...) custom-call(s32[8]{0:T(128)S(1)} %stack.87.blk_ref, ...), custom_call_target="tpu_custom_call" | custom-call | flops 4294967296 | bytes 12582912 | tf_op jit(solution)/shard_map/wgrad/pallas_call | solution.py:172
  130.1 2.6 %collective-permute-start.28 = (bf16[512,512]{1,0:T(8,128)(2,1)}, bf16[512,512]{1,0:T(8,128)(2,1)}, u32[]{:S(2)}, u32[]{:S(2)}) collective-permute-start(bf16[512,512]{1,0:T(8,128)(2,1)} %get-tuple-element.44), channel_id=1, source_target_pairs={{0,2},{1,3},{2,0},{3,1},{4,6},{5,7},{6,4},{7,5},{8,10},{9,11},{10,... | collective-permute-start | bytes 1572872 | tf_op jit(solution)/shard_map/ppermute | solution.py:44
  132.8 9.7 %slope.2 = (bf16[512,512]{1,0:T(8,128)(2,1)S(1)}, bf16[512,512]{1,0:T(8,128)(2,1)S(1)}) custom-call(s32[9]{0:T(128)S(1)} %concatenate.65.off_ref, bf16[512,4096]{1,0:T(8,128)(2,1)} %xo_ref.7, bf16[512,4096]{1,0:T(8,128)(2,1)} %collective-permute-done.xp_ref, bf16[512,2048]{1,0:T(8,128)(2,1)} %co_ref.3, bf16[512,1024]{1,0:T(8,128)(2,1)} %copy-done.19, ...), custom_call_target="tpu_custom_call" | custom-call | flops 4294967296 | bytes 12582912 | tf_op jit(solution)/shard_map/slope/pallas_call | solution.py:135
  142.5 10.3 %wgrad.2 = (bf16[512,512]{1,0:T(8,128)(2,1)S(1)}, bf16[512,512]{1,0:T(8,128)(2,1)S(1)}, bf16[512,512]{1,0:T(8,128)(2,1)S(1)}, bf16[512,512]{1,0:T(8,128)(2,1)S(1...) custom-call(s32[8]{0:T(128)S(1)} %stack.87.blk_ref, ...), custom_call_target="tpu_custom_call" | custom-call | flops 4294967296 | bytes 12582912 | tf_op jit(solution)/shard_map/wgrad/pallas_call | solution.py:172
  152.8 1.4 collective-permute-start.24
  154.3 1.2 collective-permute-start.23
  155.5 0.8 collective-permute-start.29
  156.3 8.9 %igrad.2 = bf16[512,4096]{1,0:T(8,128)(2,1)} custom-call(s32[10]{0:T(128)S(1)} %stack.78.off_ref, bf16[512,512]{1,0:T(8,128)(2,1)S(1)} %get-tuple-element.31.sa_ref.sp_ref, bf16[512,512]{1,0:T(8,128)(2,1)S(1)} %copy-done.13, bf16[512,512]{1,0:T(8,128)(2,1)S(1)} %maximum_select_fusion.1.refs_0_, bf16[512,512]{1,0:T(8,128)(2,1)S(1)} %collective-permute-done.3.refs_1_, ...), custom_call_target="tpu_custom_call" | custom-call | flops 4294967296 | bytes 12582912 | tf_op jit(solution)/shard_map/igrad/pallas_call | solution.py:223
  165.2 2.2 collective-permute-start.32
  167.4 1.2 convert_add_fusion.3
  168.6 5.8 %collective-permute-start.19 = (bf16[512,4096]{1,0:T(8,128)(2,1)}, bf16[512,4096]{1,0:T(8,128)(2,1)}, u32[]{:S(2)}, u32[]{:S(2)}) collective-permute-start(bf16[512,4096]{1,0:T(8,128)(2,1)} %igrad.2), channel_id=1, source_target_pairs={{0,1},{1,0},{2,3},{3,2},{4,5},{5,4},{6,7},{7,6},{8,9},{9,8},{10,11... | collective-permute-start | bytes 12582920 | tf_op jit(solution)/shard_map/ppermute | solution.py:48
  174.7 3.7 %collective-permute-done.32 = bf16[512,512]{1,0:T(8,128)(2,1)S(1)} collective-permute-done((bf16[512,512]{1,0:T(8,128)(2,1)S(1)}, bf16[512,512]{1,0:T(8,128)(2,1)S(1)}, u32[]{:S(2)}, u32[]{:S(2)}) %collective-permute-start.32) | collective-permute-done | bytes 524320 | tf_op jit(solution)/shard_map/ppermute | solution.py:44
  179.2 0.8 collective-permute-start.33
  180.3 3.3 %collective-permute-done.30 = bf16[256,512]{1,0:T(8,128)(2,1)S(1)} collective-permute-done((bf16[256,512]{1,0:T(8,128)(2,1)S(1)}, bf16[256,512]{1,0:T(8,128)(2,1)S(1)}, u32[]{:S(2)}, u32[]{:S(2)}) %collective-permute-start.30) | collective-permute-done | bytes 262176 | tf_op jit(solution)/shard_map/ppermute | solution.py:40
  183.7 2.1 collective-permute-done.33
  185.9 3.0 %collective-permute-start.31 = (bf16[512,512]{1,0:T(8,128)(2,1)S(1)}, bf16[512,512]{1,0:T(8,128)(2,1)S(1)}, u32[]{:S(2)}, u32[]{:S(2)}) collective-permute-start(bf16[512,512]{1,0:T(8,128)(2,1)S(1)} %pad_maximum_fusion), channel_id=1, source_target_pairs={{0,12},{1,13},{2,14},{3,15},{4,0},{5,1},{6,2},{7,3},{8,4},{9,5},{1... | collective-permute-start | bytes 1572872 | tf_op jit(solution)/shard_map/ppermute | solution.py:40
  189.0 7.8 %collective-permute-done.25 = bf16[512,512]{1,0:T(8,128)(2,1)S(1)} collective-permute-done((bf16[512,512]{1,0:T(8,128)(2,1)S(1)}, bf16[512,512]{1,0:T(8,128)(2,1)S(1)}, u32[]{:S(2)}, u32[]{:S(2)}) %collective-permute-start.25) | collective-permute-done | bytes 524320 | tf_op jit(solution)/shard_map/ppermute | solution.py:36
  197.0 5.3 %collective-permute-done.41 = bf16[256,512]{1,0:T(8,128)(2,1)S(1)} collective-permute-done((bf16[256,512]{1,0:T(8,128)(2,1)S(1)}, bf16[256,512]{1,0:T(8,128)(2,1)S(1)}, u32[]{:S(2)}, u32[]{:S(2)}) %collective-permute-start.41) | collective-permute-done | bytes 262176 | tf_op jit(solution)/shard_map/ppermute | solution.py:56
  202.4 2.7 %collective-permute-start.21 = (bf16[512,512]{1,0:T(8,128)(2,1)S(1)}, bf16[512,512]{1,0:T(8,128)(2,1)S(1)}, u32[]{:S(2)}, u32[]{:S(2)}) collective-permute-start(bf16[512,512]{1,0:T(8,128)(2,1)S(1)} %add_convert_fusion.3), channel_id=1, source_target_pairs={{0,12},{1,13},{2,14},{3,15},{4,0},{5,1},{6,2},{7,3},{8,4},{9,5},{1... | collective-permute-start | bytes 1572872 | tf_op jit(solution)/shard_map/ppermute | solution.py:40
  206.1 1.2 collective-permute-done.34
  207.3 1.2 collective-permute-start.42
  208.9 9.7 %collective-permute-done.22 = bf16[512,512]{1,0:T(8,128)(2,1)S(1)} collective-permute-done((bf16[512,512]{1,0:T(8,128)(2,1)S(1)}, bf16[512,512]{1,0:T(8,128)(2,1)S(1)}, u32[]{:S(2)}, u32[]{:S(2)}) %collective-permute-start.22) | collective-permute-done | bytes 524320 | tf_op jit(solution)/shard_map/ppermute | solution.py:36
  218.5 1.9 collective-permute-start.43
  220.4 3.0 %collective-permute-start.44 = (bf16[256,1024]{1,0:T(8,128)(2,1)S(1)}, bf16[256,1024]{1,0:T(8,128)(2,1)S(1)}, u32[]{:S(2)}, u32[]{:S(2)}) collective-permute-start(bf16[256,1024]{1,0:T(8,128)(2,1)S(1)} %get-tuple-element.54), channel_id=1, source_target_pairs={{0,96},{16,112},{32,0},{48,16},{64,32},{80,48},{96,64},{112,80},{1... | collective-permute-start | bytes 1572872 | tf_op jit(solution)/shard_map/ppermute | solution.py:52
  223.4 8.0 %collective-permute-start.36 = (f32[256,512]{1,0:T(8,128)S(1)}, f32[256,512]{1,0:T(8,128)S(1)}, u32[]{:S(2)}, u32[]{:S(2)}) collective-permute-start(f32[256,512]{1,0:T(8,128)S(1)} %get-tuple-element.61), channel_id=1, source_target_pairs={{0,1},{1,0},{2,3},{3,2},{4,5},{5,4},{6,7},{7,6},{8,9},{9,8},{10,11... | collective-permute-start | bytes 1572872 | tf_op jit(solution)/shard_map/ppermute | solution.py:48
  231.9 2.5 collective-permute-start.35
  234.5 9.3 %collective-permute-done.44 = bf16[256,1024]{1,0:T(8,128)(2,1)S(1)} collective-permute-done((bf16[256,1024]{1,0:T(8,128)(2,1)S(1)}, bf16[256,1024]{1,0:T(8,128)(2,1)S(1)}, u32[]{:S(2)}, u32[]{:S(2)}) %collective-permute-start.44) | collective-permute-done | bytes 524320 | tf_op jit(solution)/shard_map/ppermute | solution.py:52
  243.9 1.8 maximum_select_fusion
  245.8 9.5 %igrad.3 = bf16[512,4096]{1,0:T(8,128)(2,1)} custom-call(s32[10]{0:T(128)S(1)} %stack.78.off_ref, bf16[512,512]{1,0:T(8,128)(2,1)S(1)} %get-tuple-element.29.sa_ref.so_ref, bf16[512,512]{1,0:T(8,128)(2,1)S(1)} %get-tuple-element.30.sb_ref.so_ref, bf16[512,512]{1,0:T(8,128)(2,1)S(1)} %maximum_select_fusion.1.refs_0_, ...), custom_call_target="tpu_custom_call" | custom-call | flops 4294967296 | bytes 12582912 | tf_op jit(solution)/shard_map/igrad/pallas_call | solution.py:223
  (113 shorter events, 9.0 us)
Async XLA Ops:
  0.6 108.5 %collective-permute-start = (bf16[512,4096]{1,0:T(8,128)(2,1)}, bf16[512,4096]{1,0:T(8,128)(2,1)}, u32[]{:S(2)}, u32[]{:S(2)}) collective-permute-start(bf16[512,4096]{1,0:T(8,128)(2,1)} %xo_ref.7), channel_id=1, source_target_pairs={{0,1},{1,0},{2,3},{3,2},{4,5},{5,4},{6,7},{7,6},{8,9},{9,8},{10,11... | collective-permute-start | bytes 12582920 | tf_op jit(solution)/shard_map/ppermute | solution.py:48
  4.2 16.6 %collective-permute-start.2 = (bf16[256,1024]{1,0:T(8,128)(2,1)}, bf16[256,1024]{1,0:T(8,128)(2,1)}, u32[]{:S(2)}, u32[]{:S(2)}) collective-permute-start(bf16[256,1024]{1,0:T(8,128)(2,1)} %get-tuple-element.63), channel_id=1, source_target_pairs={{0,1},{1,0},{2,3},{3,2},{4,5},{5,4},{6,7},{7,6},{8,9},{9,8},{10,11... | collective-permute-start | bytes 1572872 | tf_op jit(solution)/shard_map/ppermute | solution.py:48
  4.2 2.2 copy-start
  6.4 2.2 copy-start.1
  13.8 14.4 %collective-permute-start.37 = (bf16[256,1024]{1,0:T(8,128)(2,1)S(1)}, bf16[256,1024]{1,0:T(8,128)(2,1)}, u32[]{:S(2)}, u32[]{:S(2)}) collective-permute-start(bf16[256,1024]{1,0:T(8,128)(2,1)S(1)} %get-tuple-element.50), channel_id=1, source_target_pairs={{0,32},{16,48},{32,64},{48,80},{64,96},{80,112},{96,0},{112,16},{1... | collective-permute-start | bytes 1572872 | tf_op jit(solution)/shard_map/ppermute | solution.py:52
  15.1 25.4 %collective-permute-start.38 = (bf16[256,1024]{1,0:T(8,128)(2,1)S(1)}, bf16[256,1024]{1,0:T(8,128)(2,1)}, u32[]{:S(2)}, u32[]{:S(2)}) collective-permute-start(bf16[256,1024]{1,0:T(8,128)(2,1)S(1)} %get-tuple-element.51), channel_id=1, source_target_pairs={{0,64},{16,80},{32,96},{48,112},{64,0},{80,16},{96,32},{112,48},{1... | collective-permute-start | bytes 1572872 | tf_op jit(solution)/shard_map/ppermute | solution.py:52
  17.6 22.9 %collective-permute-start.39 = (bf16[256,1024]{1,0:T(8,128)(2,1)S(1)}, bf16[256,1024]{1,0:T(8,128)(2,1)}, u32[]{:S(2)}, u32[]{:S(2)}) collective-permute-start(bf16[256,1024]{1,0:T(8,128)(2,1)S(1)} %get-tuple-element.52), channel_id=1, source_target_pairs={{0,96},{16,112},{32,0},{48,16},{64,32},{80,48},{96,64},{112,80},{1... | collective-permute-start | bytes 1572872 | tf_op jit(solution)/shard_map/ppermute | solution.py:52
  19.5 3.8 %copy-start.17 = (bf16[256,512]{1,0:T(8,128)(2,1)S(1)}, bf16[256,512]{1,0:T(8,128)(2,1)}, u32[]{:S(2)}) copy-start(bf16[256,512]{1,0:T(8,128)(2,1)} %get-tuple-element.67) | copy-start | bytes 786436
  20.8 50.7 %collective-permute-start.1 = (bf16[512,1024]{1,0:T(8,128)(2,1)S(1)}, bf16[512,1024]{1,0:T(8,128)(2,1)S(1)}, u32[]{:S(2)}, u32[]{:S(2)}) collective-permute-start(bf16[512,1024]{1,0:T(8,128)(2,1)S(1)} %constant_dynamic-slice_fusion.2), channel_id=1, source_target_pairs={{0,1},{1,0},{2,3},{3,2},{4,5},{5,4},{6,7},{7,6},{8,9},{9,8},{10,11... | collective-permute-start | bytes 3145736 | tf_op jit(solution)/shard_map/ppermute | solution.py:48
  28.2 22.3 %collective-permute-start.3 = (bf16[512,512]{1,0:T(8,128)(2,1)S(1)}, bf16[512,512]{1,0:T(8,128)(2,1)S(1)}, u32[]{:S(2)}, u32[]{:S(2)}) collective-permute-start(bf16[512,512]{1,0:T(8,128)(2,1)S(1)} %maximum_select_fusion.1.refs_0_), channel_id=1, source_target_pairs={{0,2},{1,3},{2,0},{3,1},{4,6},{5,7},{6,4},{7,5},{8,10},{9,11},{10,... | collective-permute-start | bytes 1572872 | tf_op jit(solution)/shard_map/ppermute | solution.py:44
  42.2 3.1 %copy-start.14 = (f32[256,1024]{1,0:T(8,128)}, f32[256,1024]{1,0:T(8,128)S(1)}, u32[]{:S(2)}) copy-start(f32[256,1024]{1,0:T(8,128)S(1)} %convert_add_fusion) | copy-start | bytes 3145732
  42.3 6.6 %collective-permute-start.40 = (bf16[256,512]{1,0:T(8,128)(2,1)S(1)}, bf16[256,512]{1,0:T(8,128)(2,1)S(1)}, u32[]{:S(2)}, u32[]{:S(2)}) collective-permute-start(bf16[256,512]{1,0:T(8,128)(2,1)S(1)} %dynamic-slice_convert_fusion), channel_id=1, source_target_pairs={{0,16},{16,0},{32,48},{48,32},{64,80},{80,64},{96,112},{112,96},{1... | collective-permute-start | bytes 786440 | tf_op jit(solution)/shard_map/ppermute | solution.py:56
  43.6 14.4 %collective-permute-start.6 = (bf16[512,512]{1,0:T(8,128)(2,1)S(1)}, bf16[512,512]{1,0:T(8,128)(2,1)S(1)}, u32[]{:S(2)}, u32[]{:S(2)}) collective-permute-start(bf16[512,512]{1,0:T(8,128)(2,1)S(1)} %maximum_select_fusion.1.refs_0_), channel_id=1, source_target_pairs={{0,4},{1,5},{2,6},{3,7},{4,8},{5,9},{6,10},{7,11},{8,12},{9,13},{1... | collective-permute-start | bytes 1572872 | tf_op jit(solution)/shard_map/ppermute | solution.py:36
  45.5 63.7 %copy-start.2 = (bf16[512,512]{1,0:T(8,128)(2,1)}, bf16[512,512]{1,0:T(8,128)(2,1)S(1)}, u32[]{:S(2)}) copy-start(bf16[512,512]{1,0:T(8,128)(2,1)S(1)} %maximum_select_fusion.2.refs_0_.refs_8_) | copy-start | bytes 1572868
  48.8 21.7 %copy-start.18 = (bf16[256,512]{1,0:T(8,128)(2,1)}, bf16[256,512]{1,0:T(8,128)(2,1)S(1)}, u32[]{:S(2)}) copy-start(bf16[256,512]{1,0:T(8,128)(2,1)S(1)} %collective-permute-done.40) | copy-start | bytes 786436
  48.8 20.4 %collective-permute-start.13 = (bf16[512,512]{1,0:T(8,128)(2,1)S(1)}, bf16[512,512]{1,0:T(8,128)(2,1)S(1)}, u32[]{:S(2)}, u32[]{:S(2)}) collective-permute-start(bf16[512,512]{1,0:T(8,128)(2,1)S(1)} %maximum_select_fusion.2.refs_0_.refs_8_), channel_id=1, source_target_pairs={{0,4},{1,5},{2,6},{3,7},{4,8},{5,9},{6,10},{7,11},{8,12},{9,13},{1... | collective-permute-start | bytes 1572872 | tf_op jit(solution)/shard_map/ppermute | solution.py:36
  50.5 20.0 %collective-permute-start.11 = (bf16[512,512]{1,0:T(8,128)(2,1)S(1)}, bf16[512,512]{1,0:T(8,128)(2,1)S(1)}, u32[]{:S(2)}, u32[]{:S(2)}) collective-permute-start(bf16[512,512]{1,0:T(8,128)(2,1)S(1)} %maximum_select_fusion.2.refs_0_.refs_8_), channel_id=1, source_target_pairs={{0,12},{1,13},{2,14},{3,15},{4,0},{5,1},{6,2},{7,3},{8,4},{9,5},{1... | collective-permute-start | bytes 1572872 | tf_op jit(solution)/shard_map/ppermute | solution.py:40
  58.0 15.9 %collective-permute-start.10 = (bf16[512,512]{1,0:T(8,128)(2,1)S(1)}, bf16[512,512]{1,0:T(8,128)(2,1)S(1)}, u32[]{:S(2)}, u32[]{:S(2)}) collective-permute-start(bf16[512,512]{1,0:T(8,128)(2,1)S(1)} %maximum_select_fusion.2.refs_0_.refs_8_), channel_id=1, source_target_pairs={{0,2},{1,3},{2,0},{3,1},{4,6},{5,7},{6,4},{7,5},{8,10},{9,11},{10,... | collective-permute-start | bytes 1572872 | tf_op jit(solution)/shard_map/ppermute | solution.py:44
  69.3 39.9 %copy-start.3 = (bf16[512,512]{1,0:T(8,128)(2,1)}, bf16[512,512]{1,0:T(8,128)(2,1)S(1)}, u32[]{:S(2)}) copy-start(bf16[512,512]{1,0:T(8,128)(2,1)S(1)} %collective-permute-done.13.refs_8_.refs_16_) | copy-start | bytes 1572868
  69.3 19.5 %collective-permute-start.5 = (bf16[512,512]{1,0:T(8,128)(2,1)S(1)}, bf16[512,512]{1,0:T(8,128)(2,1)}, u32[]{:S(2)}, u32[]{:S(2)}) collective-permute-start(bf16[512,512]{1,0:T(8,128)(2,1)S(1)} %collective-permute-done.3.refs_1_), channel_id=1, source_target_pairs={{0,12},{1,13},{2,14},{3,15},{4,0},{5,1},{6,2},{7,3},{8,4},{9,5},{1... | collective-permute-start | bytes 1572872 | tf_op jit(solution)/shard_map/ppermute | solution.py:40
  70.5 48.6 %copy-start.4 = (bf16[512,512]{1,0:T(8,128)(2,1)}, bf16[512,512]{1,0:T(8,128)(2,1)S(1)}, u32[]{:S(2)}) copy-start(bf16[512,512]{1,0:T(8,128)(2,1)S(1)} %collective-permute-done.11.refs_2_.refs_10_) | copy-start | bytes 1572868
  70.5 6.9 %collective-permute-start.14 = (bf16[256,512]{1,0:T(8,128)(2,1)S(1)}, bf16[256,512]{1,0:T(8,128)(2,1)S(1)}, u32[]{:S(2)}, u32[]{:S(2)}) collective-permute-start(bf16[256,512]{1,0:T(8,128)(2,1)S(1)} %slice.56), channel_id=1, source_target_pairs={{0,4},{1,5},{2,6},{3,7},{4,8},{5,9},{6,10},{7,11},{8,12},{9,13},{1... | collective-permute-start | bytes 786440 | tf_op jit(solution)/shard_map/ppermute | solution.py:36
  71.6 5.8 %copy-start.19 = (bf16[512,1024]{1,0:T(8,128)(2,1)}, bf16[512,1024]{1,0:T(8,128)(2,1)S(1)}, u32[]{:S(2)}) copy-start(bf16[512,1024]{1,0:T(8,128)(2,1)S(1)} %collective-permute-done.1.cp_ref) | copy-start | bytes 3145732
  71.6 14.6 %collective-permute-start.15 = (bf16[256,512]{1,0:T(8,128)(2,1)}, bf16[256,512]{1,0:T(8,128)(2,1)}, u32[]{:S(2)}, u32[]{:S(2)}) collective-permute-start(bf16[256,512]{1,0:T(8,128)(2,1)} %slice.57), channel_id=1, source_target_pairs={{0,12},{1,13},{2,14},{3,15},{4,0},{5,1},{6,2},{7,3},{8,4},{9,5},{1... | collective-permute-start | bytes 786440 | tf_op jit(solution)/shard_map/ppermute | solution.py:40
  74.8 17.1 %collective-permute-start.12 = (bf16[512,512]{1,0:T(8,128)(2,1)S(1)}, bf16[512,512]{1,0:T(8,128)(2,1)}, u32[]{:S(2)}, u32[]{:S(2)}) collective-permute-start(bf16[512,512]{1,0:T(8,128)(2,1)S(1)} %collective-permute-done.11.refs_2_.refs_10_), channel_id=1, source_target_pairs={{0,2},{1,3},{2,0},{3,1},{4,6},{5,7},{6,4},{7,5},{8,10},{9,11},{10,... | collective-permute-start | bytes 1572872 | tf_op jit(solution)/shard_map/ppermute | solution.py:44
  77.4 20.3 %collective-permute-start.18 = (bf16[512,512]{1,0:T(8,128)(2,1)S(1)}, bf16[512,512]{1,0:T(8,128)(2,1)}, u32[]{:S(2)}, u32[]{:S(2)}) collective-permute-start(bf16[512,512]{1,0:T(8,128)(2,1)S(1)} %collective-permute-done.13.refs_8_.refs_16_), channel_id=1, source_target_pairs={{0,2},{1,3},{2,0},{3,1},{4,6},{5,7},{6,4},{7,5},{8,10},{9,11},{10,... | collective-permute-start | bytes 1572872 | tf_op jit(solution)/shard_map/ppermute | solution.py:44
  80.0 29.2 %copy-start.6 = (bf16[512,512]{1,0:T(8,128)(2,1)S(1)}, bf16[512,512]{1,0:T(8,128)(2,1)}, u32[]{:S(2)}) copy-start(bf16[512,512]{1,0:T(8,128)(2,1)} %copy-done.5) | copy-start | bytes 1572868
  86.2 17.1 %collective-permute-start.16 = (bf16[256,512]{1,0:T(8,128)(2,1)S(1)}, bf16[256,512]{1,0:T(8,128)(2,1)S(1)}, u32[]{:S(2)}, u32[]{:S(2)}) collective-permute-start(bf16[256,512]{1,0:T(8,128)(2,1)S(1)} %collective-permute-done.14.refs_4_.refs_12_), channel_id=1, source_target_pairs={{0,2},{1,3},{2,0},{3,1},{4,6},{5,7},{6,4},{7,5},{8,10},{9,11},{10,... | collective-permute-start | bytes 786440 | tf_op jit(solution)/shard_map/ppermute | solution.py:44
  88.8 20.0 %collective-permute-start.17 = (bf16[256,512]{1,0:T(8,128)(2,1)}, bf16[256,512]{1,0:T(8,128)(2,1)S(1)}, u32[]{:S(2)}, u32[]{:S(2)}) collective-permute-start(bf16[256,512]{1,0:T(8,128)(2,1)} %collective-permute-done.15.refs_5_.refs_13_), channel_id=1, source_target_pairs={{0,2},{1,3},{2,0},{3,1},{4,6},{5,7},{6,4},{7,5},{8,10},{9,11},{10,... | collective-permute-start | bytes 786440 | tf_op jit(solution)/shard_map/ppermute | solution.py:44
  91.9 27.3 %copy-start.8 = (bf16[512,4096]{1,0:T(8,128)(2,1)S(1)}, bf16[512,4096]{1,0:T(8,128)(2,1)}, u32[]{:S(2)}) copy-start(bf16[512,4096]{1,0:T(8,128)(2,1)} %xo_ref.7) | copy-start | bytes 12582916
  91.9 40.8 %collective-permute-start.4 = (bf16[512,512]{1,0:T(8,128)(2,1)S(1)}, bf16[512,512]{1,0:T(8,128)(2,1)S(1)}, u32[]{:S(2)}, u32[]{:S(2)}) collective-permute-start(bf16[512,512]{1,0:T(8,128)(2,1)S(1)} %maximum_select_fusion.1.refs_0_), channel_id=1, source_target_pairs={{0,12},{1,13},{2,14},{3,15},{4,0},{5,1},{6,2},{7,3},{8,4},{9,5},{1... | collective-permute-start | bytes 1572872 | tf_op jit(solution)/shard_map/ppermute | solution.py:40
  97.7 35.0 %collective-permute-start.9 = (bf16[512,512]{1,0:T(8,128)(2,1)S(1)}, bf16[512,512]{1,0:T(8,128)(2,1)S(1)}, u32[]{:S(2)}, u32[]{:S(2)}) collective-permute-start(bf16[512,512]{1,0:T(8,128)(2,1)S(1)} %collective-permute-done.3.refs_1_), channel_id=1, source_target_pairs={{0,4},{1,5},{2,6},{3,7},{4,8},{5,9},{6,10},{7,11},{8,12},{9,13},{1... | collective-permute-start | bytes 1572872 | tf_op jit(solution)/shard_map/ppermute | solution.py:36
  103.3 29.4 %collective-permute-start.7 = (bf16[512,512]{1,0:T(8,128)(2,1)S(1)}, bf16[512,512]{1,0:T(8,128)(2,1)S(1)}, u32[]{:S(2)}, u32[]{:S(2)}) collective-permute-start(bf16[512,512]{1,0:T(8,128)(2,1)S(1)} %collective-permute-done.6.refs_6_), channel_id=1, source_target_pairs={{0,4},{1,5},{2,6},{3,7},{4,8},{5,9},{6,10},{7,11},{8,12},{9,13},{1... | collective-permute-start | bytes 1572872 | tf_op jit(solution)/shard_map/ppermute | solution.py:36
  108.8 23.9 %collective-permute-start.8 = (bf16[512,512]{1,0:T(8,128)(2,1)}, bf16[512,512]{1,0:T(8,128)(2,1)S(1)}, u32[]{:S(2)}, u32[]{:S(2)}) collective-permute-start(bf16[512,512]{1,0:T(8,128)(2,1)} %collective-permute-done.5.refs_3_), channel_id=1, source_target_pairs={{0,12},{1,13},{2,14},{3,15},{4,0},{5,1},{6,2},{7,3},{8,4},{9,5},{1... | collective-permute-start | bytes 1572872 | tf_op jit(solution)/shard_map/ppermute | solution.py:40
  119.1 10.1 %copy-start.12 = (bf16[512,512]{1,0:T(8,128)(2,1)}, bf16[512,512]{1,0:T(8,128)(2,1)S(1)}, u32[]{:S(2)}) copy-start(bf16[512,512]{1,0:T(8,128)(2,1)S(1)} %get-tuple-element.32.sb_ref.sp_ref) | copy-start | bytes 1572868
  129.3 0.8 copy-start.10
  130.1 12.4 %copy-start.9 = (bf16[512,4096]{1,0:T(8,128)(2,1)S(1)}, bf16[512,4096]{1,0:T(8,128)(2,1)}, u32[]{:S(2)}) copy-start(bf16[512,4096]{1,0:T(8,128)(2,1)} %xo_ref.7) | copy-start | bytes 12582916
  130.1 35.1 %collective-permute-start.28 = (bf16[512,512]{1,0:T(8,128)(2,1)}, bf16[512,512]{1,0:T(8,128)(2,1)}, u32[]{:S(2)}, u32[]{:S(2)}) collective-permute-start(bf16[512,512]{1,0:T(8,128)(2,1)} %get-tuple-element.44), channel_id=1, source_target_pairs={{0,2},{1,3},{2,0},{3,1},{4,6},{5,7},{6,4},{7,5},{8,10},{9,11},{10,... | collective-permute-start | bytes 1572872 | tf_op jit(solution)/shard_map/ppermute | solution.py:44
  132.7 9.7 %copy-start.7 = (bf16[512,512]{1,0:T(8,128)(2,1)}, bf16[512,512]{1,0:T(8,128)(2,1)S(1)}, u32[]{:S(2)}) copy-start(bf16[512,512]{1,0:T(8,128)(2,1)S(1)} %collective-permute-done.9.refs_7_) | copy-start | bytes 1572868
  142.5 13.8 %copy-start.13 = (bf16[512,512]{1,0:T(8,128)(2,1)S(1)}, bf16[512,512]{1,0:T(8,128)(2,1)}, u32[]{:S(2)}) copy-start(bf16[512,512]{1,0:T(8,128)(2,1)} %copy-done.12) | copy-start | bytes 1572868
  152.8 33.1 %collective-permute-start.20 = (bf16[512,512]{1,0:T(8,128)(2,1)}, bf16[512,512]{1,0:T(8,128)(2,1)S(1)}, u32[]{:S(2)}, u32[]{:S(2)}) collective-permute-start(bf16[512,512]{1,0:T(8,128)(2,1)} %get-tuple-element.35), channel_id=1, source_target_pairs={{0,12},{1,13},{2,14},{3,15},{4,0},{5,1},{6,2},{7,3},{8,4},{9,5},{1... | collective-permute-start | bytes 1572872 | tf_op jit(solution)/shard_map/ppermute | solution.py:40
  152.8 26.4 %collective-permute-start.24 = (bf16[512,512]{1,0:T(8,128)(2,1)}, bf16[512,512]{1,0:T(8,128)(2,1)S(1)}, u32[]{:S(2)}, u32[]{:S(2)}) collective-permute-start(bf16[512,512]{1,0:T(8,128)(2,1)} %get-tuple-element.40), channel_id=1, source_target_pairs={{0,4},{1,5},{2,6},{3,7},{4,8},{5,9},{6,10},{7,11},{8,12},{9,13},{1... | collective-permute-start | bytes 1572872 | tf_op jit(solution)/shard_map/ppermute | solution.py:36
  154.3 34.6 %collective-permute-start.23 = (bf16[512,512]{1,0:T(8,128)(2,1)}, bf16[512,512]{1,0:T(8,128)(2,1)S(1)}, u32[]{:S(2)}, u32[]{:S(2)}) collective-permute-start(bf16[512,512]{1,0:T(8,128)(2,1)} %get-tuple-element.38), channel_id=1, source_target_pairs={{0,12},{1,13},{2,14},{3,15},{4,0},{5,1},{6,2},{7,3},{8,4},{9,5},{1... | collective-permute-start | bytes 1572872 | tf_op jit(solution)/shard_map/ppermute | solution.py:40
  155.5 9.7 %copy-start.11 = (bf16[512,512]{1,0:T(8,128)(2,1)S(1)}, bf16[512,512]{1,0:T(8,128)(2,1)}, u32[]{:S(2)}) copy-start(bf16[512,512]{1,0:T(8,128)(2,1)} %copy-done.10) | copy-start | bytes 1572868
  155.5 13.2 %collective-permute-start.29 = (bf16[512,512]{1,0:T(8,128)(2,1)}, bf16[512,512]{1,0:T(8,128)(2,1)S(1)}, u32[]{:S(2)}, u32[]{:S(2)}) collective-permute-start(bf16[512,512]{1,0:T(8,128)(2,1)} %get-tuple-element.46), channel_id=1, source_target_pairs={{0,2},{1,3},{2,0},{3,1},{4,6},{5,7},{6,4},{7,5},{8,10},{9,11},{10,... | collective-permute-start | bytes 1572872 | tf_op jit(solution)/shard_map/ppermute | solution.py:44
  165.2 13.1 %collective-permute-start.32 = (bf16[512,512]{1,0:T(8,128)(2,1)S(1)}, bf16[512,512]{1,0:T(8,128)(2,1)S(1)}, u32[]{:S(2)}, u32[]{:S(2)}) collective-permute-start(bf16[512,512]{1,0:T(8,128)(2,1)S(1)} %copy-done.11), channel_id=1, source_target_pairs={{0,2},{1,3},{2,0},{3,1},{4,6},{5,7},{6,4},{7,5},{8,10},{9,11},{10,... | collective-permute-start | bytes 1572872 | tf_op jit(solution)/shard_map/ppermute | solution.py:44
  168.6 77.2 %collective-permute-start.19 = (bf16[512,4096]{1,0:T(8,128)(2,1)}, bf16[512,4096]{1,0:T(8,128)(2,1)}, u32[]{:S(2)}, u32[]{:S(2)}) collective-permute-start(bf16[512,4096]{1,0:T(8,128)(2,1)} %igrad.2), channel_id=1, source_target_pairs={{0,1},{1,0},{2,3},{3,2},{4,5},{5,4},{6,7},{7,6},{8,9},{9,8},{10,11... | collective-permute-start | bytes 12582920 | tf_op jit(solution)/shard_map/ppermute | solution.py:48
  178.4 5.2 %collective-permute-start.30 = (bf16[256,512]{1,0:T(8,128)(2,1)S(1)}, bf16[256,512]{1,0:T(8,128)(2,1)S(1)}, u32[]{:S(2)}, u32[]{:S(2)}) collective-permute-start(bf16[256,512]{1,0:T(8,128)(2,1)S(1)} %get-tuple-element.64), channel_id=1, source_target_pairs={{0,12},{1,13},{2,14},{3,15},{4,0},{5,1},{6,2},{7,3},{8,4},{9,5},{1... | collective-permute-start | bytes 786440 | tf_op jit(solution)/shard_map/ppermute | solution.py:40
  179.2 6.5 %collective-permute-start.33 = (bf16[256,512]{1,0:T(8,128)(2,1)S(1)}, bf16[256,512]{1,0:T(8,128)(2,1)S(1)}, u32[]{:S(2)}, u32[]{:S(2)}) collective-permute-start(bf16[256,512]{1,0:T(8,128)(2,1)S(1)} %get-tuple-element.65), channel_id=1, source_target_pairs={{0,4},{1,5},{2,6},{3,7},{4,8},{5,9},{6,10},{7,11},{8,12},{9,13},{1... | collective-permute-start | bytes 786440 | tf_op jit(solution)/shard_map/ppermute | solution.py:36
  183.6 18.8 %collective-permute-start.27 = (bf16[512,512]{1,0:T(8,128)(2,1)S(1)}, bf16[512,512]{1,0:T(8,128)(2,1)S(1)}, u32[]{:S(2)}, u32[]{:S(2)}) collective-permute-start(bf16[512,512]{1,0:T(8,128)(2,1)S(1)} %get-tuple-element.42), channel_id=1, source_target_pairs={{0,2},{1,3},{2,0},{3,1},{4,6},{5,7},{6,4},{7,5},{8,10},{9,11},{10,... | collective-permute-start | bytes 1572872 | tf_op jit(solution)/shard_map/ppermute | solution.py:44
  185.7 11.1 %collective-permute-start.25 = (bf16[512,512]{1,0:T(8,128)(2,1)S(1)}, bf16[512,512]{1,0:T(8,128)(2,1)S(1)}, u32[]{:S(2)}, u32[]{:S(2)}) collective-permute-start(bf16[512,512]{1,0:T(8,128)(2,1)S(1)} %add_convert_fusion.2), channel_id=1, source_target_pairs={{0,4},{1,5},{2,6},{3,7},{4,8},{5,9},{6,10},{7,11},{8,12},{9,13},{1... | collective-permute-start | bytes 1572872 | tf_op jit(solution)/shard_map/ppermute | solution.py:36
  185.8 11.0 %copy-start.16 = (bf16[256,512]{1,0:T(8,128)(2,1)S(1)}, bf16[256,512]{1,0:T(8,128)(2,1)}, u32[]{:S(2)}) copy-start(bf16[256,512]{1,0:T(8,128)(2,1)} %get-tuple-element.55) | copy-start | bytes 786436
  185.9 19.1 %collective-permute-start.31 = (bf16[512,512]{1,0:T(8,128)(2,1)S(1)}, bf16[512,512]{1,0:T(8,128)(2,1)S(1)}, u32[]{:S(2)}, u32[]{:S(2)}) collective-permute-start(bf16[512,512]{1,0:T(8,128)(2,1)S(1)} %pad_maximum_fusion), channel_id=1, source_target_pairs={{0,12},{1,13},{2,14},{3,15},{4,0},{5,1},{6,2},{7,3},{8,4},{9,5},{1... | collective-permute-start | bytes 1572872 | tf_op jit(solution)/shard_map/ppermute | solution.py:40
  188.9 18.4 %collective-permute-start.34 = (bf16[512,512]{1,0:T(8,128)(2,1)S(1)}, bf16[512,512]{1,0:T(8,128)(2,1)S(1)}, u32[]{:S(2)}, u32[]{:S(2)}) collective-permute-start(bf16[512,512]{1,0:T(8,128)(2,1)S(1)} %pad_maximum_fusion.1), channel_id=1, source_target_pairs={{0,4},{1,5},{2,6},{3,7},{4,8},{5,9},{6,10},{7,11},{8,12},{9,13},{1... | collective-permute-start | bytes 1572872 | tf_op jit(solution)/shard_map/ppermute | solution.py:36
  196.8 5.5 %collective-permute-start.41 = (bf16[256,512]{1,0:T(8,128)(2,1)S(1)}, bf16[256,512]{1,0:T(8,128)(2,1)S(1)}, u32[]{:S(2)}, u32[]{:S(2)}) collective-permute-start(bf16[256,512]{1,0:T(8,128)(2,1)S(1)} %copy-done.16), channel_id=1, source_target_pairs={{0,16},{16,0},{32,48},{48,32},{64,80},{80,64},{96,112},{112,96},{1... | collective-permute-start | bytes 786440 | tf_op jit(solution)/shard_map/ppermute | solution.py:56
  202.3 16.2 %collective-permute-start.22 = (bf16[512,512]{1,0:T(8,128)(2,1)S(1)}, bf16[512,512]{1,0:T(8,128)(2,1)S(1)}, u32[]{:S(2)}, u32[]{:S(2)}) collective-permute-start(bf16[512,512]{1,0:T(8,128)(2,1)S(1)} %get-tuple-element.36), channel_id=1, source_target_pairs={{0,4},{1,5},{2,6},{3,7},{4,8},{5,9},{6,10},{7,11},{8,12},{9,13},{1... | collective-permute-start | bytes 1572872 | tf_op jit(solution)/shard_map/ppermute | solution.py:36
  202.4 18.0 %collective-permute-start.21 = (bf16[512,512]{1,0:T(8,128)(2,1)S(1)}, bf16[512,512]{1,0:T(8,128)(2,1)S(1)}, u32[]{:S(2)}, u32[]{:S(2)}) collective-permute-start(bf16[512,512]{1,0:T(8,128)(2,1)S(1)} %add_convert_fusion.3), channel_id=1, source_target_pairs={{0,12},{1,13},{2,14},{3,15},{4,0},{5,1},{6,2},{7,3},{8,4},{9,5},{1... | collective-permute-start | bytes 1572872 | tf_op jit(solution)/shard_map/ppermute | solution.py:40
  205.0 18.4 %collective-permute-start.26 = (bf16[512,512]{1,0:T(8,128)(2,1)S(1)}, bf16[512,512]{1,0:T(8,128)(2,1)S(1)}, u32[]{:S(2)}, u32[]{:S(2)}) collective-permute-start(bf16[512,512]{1,0:T(8,128)(2,1)S(1)} %add_convert_fusion.1), channel_id=1, source_target_pairs={{0,2},{1,3},{2,0},{3,1},{4,6},{5,7},{6,4},{7,5},{8,10},{9,11},{10,... | collective-permute-start | bytes 1572872 | tf_op jit(solution)/shard_map/ppermute | solution.py:44
  207.3 24.6 %collective-permute-start.42 = (bf16[256,1024]{1,0:T(8,128)(2,1)S(1)}, bf16[256,1024]{1,0:T(8,128)(2,1)S(1)}, u32[]{:S(2)}, u32[]{:S(2)}) collective-permute-start(bf16[256,1024]{1,0:T(8,128)(2,1)S(1)} %get-tuple-element.54), channel_id=1, source_target_pairs={{0,32},{16,48},{32,64},{48,80},{64,96},{80,112},{96,0},{112,16},{1... | collective-permute-start | bytes 1572872 | tf_op jit(solution)/shard_map/ppermute | solution.py:52
  218.5 15.9 %collective-permute-start.43 = (bf16[256,1024]{1,0:T(8,128)(2,1)S(1)}, bf16[256,1024]{1,0:T(8,128)(2,1)S(1)}, u32[]{:S(2)}, u32[]{:S(2)}) collective-permute-start(bf16[256,1024]{1,0:T(8,128)(2,1)S(1)} %get-tuple-element.54), channel_id=1, source_target_pairs={{0,64},{16,80},{32,96},{48,112},{64,0},{80,16},{96,32},{112,48},{1... | collective-permute-start | bytes 1572872 | tf_op jit(solution)/shard_map/ppermute | solution.py:52
  220.4 23.4 %collective-permute-start.44 = (bf16[256,1024]{1,0:T(8,128)(2,1)S(1)}, bf16[256,1024]{1,0:T(8,128)(2,1)S(1)}, u32[]{:S(2)}, u32[]{:S(2)}) collective-permute-start(bf16[256,1024]{1,0:T(8,128)(2,1)S(1)} %get-tuple-element.54), channel_id=1, source_target_pairs={{0,96},{16,112},{32,0},{48,16},{64,32},{80,48},{96,64},{112,80},{1... | collective-permute-start | bytes 1572872 | tf_op jit(solution)/shard_map/ppermute | solution.py:52
  223.4 20.4 %collective-permute-start.36 = (f32[256,512]{1,0:T(8,128)S(1)}, f32[256,512]{1,0:T(8,128)S(1)}, u32[]{:S(2)}, u32[]{:S(2)}) collective-permute-start(f32[256,512]{1,0:T(8,128)S(1)} %get-tuple-element.61), channel_id=1, source_target_pairs={{0,1},{1,0},{2,3},{3,2},{4,5},{5,4},{6,7},{7,6},{8,9},{9,8},{10,11... | collective-permute-start | bytes 1572872 | tf_op jit(solution)/shard_map/ppermute | solution.py:48
  231.9 12.0 %collective-permute-start.35 = (f32[256,512]{1,0:T(8,128)S(1)}, f32[256,512]{1,0:T(8,128)S(1)}, u32[]{:S(2)}, u32[]{:S(2)}) collective-permute-start(f32[256,512]{1,0:T(8,128)S(1)} %get-tuple-element.59), channel_id=1, source_target_pairs={{0,1},{1,0},{2,3},{3,2},{4,5},{5,4},{6,7},{7,6},{8,9},{9,8},{10,11... | collective-permute-start | bytes 1572872 | tf_op jit(solution)/shard_map/ppermute | solution.py:48
  243.8 2.0 copy-start.15
  (1 other events, 0.8 us)

commit v2 on v0

v2 whole, which is shorter than its diff:
```python
import functools

import jax
import jax.numpy as jnp
from jax import lax
from jax.experimental import pallas as pl
from jax.experimental.pallas import tpu as pltpu
from jax.sharding import PartitionSpec as P

F32 = jnp.float32
BF16 = jnp.bfloat16
MIB = 1 << 20
COST = 0.3

NZ, NY, NC, NX, NL = 4, 2, 2, 4, 2
DIRS = [(dz, dy) for dz in range(NZ) for dy in range(NY)]


def shard_perm(dz, dy, dc):
    perm = []
    for i in range(NZ * NY * NC):
        z, y, c = i // (NY * NC), (i // NC) % NY, i % NC
        j = ((z + dz) % NZ) * NY * NC + ((y + dy) % NY) * NC + (c + dc) % NC
        perm.append((i, j))
    return perm


def to_zp(a):
    return lax.ppermute(a, "shard", shard_perm(1, 0, 0))


def to_zm(a):
    return lax.ppermute(a, "shard", shard_perm(-1, 0, 0))


def to_y(a):
    return lax.ppermute(a, "shard", shard_perm(0, 1, 0))


def to_core(a):
    return lax.ppermute(a, "shard", shard_perm(0, 0, 1))


def to_l(a):
    return lax.ppermute(a, "replica", [(i, i ^ 1) for i in range(NX * NL)])


def to_near(a):
    return lax.ppermute(a, "replica", [(i, i ^ NL) for i in range(NX * NL)])


def to_far(a):
    perm = [(i, (NX - 1 - i // NL) * NL + i % NL) for i in range(NX * NL)]
    return lax.ppermute(a, "replica", perm)


def add(*terms):
    total = terms[0].astype(F32)
    for term in terms[1:]:
        total = total + term.astype(F32)
    return total


def whole(shape):
    return pl.BlockSpec(shape, lambda i, *_: (0,) * len(shape))


def cost(flops, nbytes, trans=0):
    return pl.CostEstimate(
        flops=int(COST * flops), bytes_accessed=int(COST * nbytes), transcendentals=int(COST * trans)
    )


def params(mib):
    return pltpu.CompilerParams(vmem_limit_bytes=mib * MIB)


def decode_kernel(order_ref, outer_ref, inner_ref, own_ref, far_ref, near_ref):
    step = pl.program_id(0)
    width = outer_ref.shape[1]
    decoded = []
    for g in range(width // 128):
        cols = slice(g * 128, (g + 1) * 128)
        delta = outer_ref[:, cols] - inner_ref[0, :, cols]
        top = jnp.max(jnp.abs(delta), axis=1, keepdims=True) + 1e-06
        scale = top.astype(BF16).astype(F32)
        code = (delta / scale).astype(BF16).astype(F32)
        decoded.append((code * scale).astype(BF16))
    decoded = jnp.concatenate(decoded, axis=1)

    @pl.when(step == 0)
    def _():
        own_ref[...] = decoded

    @pl.when(step == 1)
    def _():
        far_ref[...] = decoded

    @pl.when(step >= 2)
    def _():
        near_ref[0] = decoded


def decode(order, outer, inner):
    rows, cols = outer.shape
    width = cols // NX
    one = jax.ShapeDtypeStruct((rows, width), BF16)
    return pl.pallas_call(
        decode_kernel,
        grid_spec=pltpu.PrefetchScalarGridSpec(
            num_scalar_prefetch=1,
            grid=(NX,),
            in_specs=[
                pl.BlockSpec((rows, width), lambda i, p: (0, p[i])),
                pl.BlockSpec((1, rows, width), lambda i, p: (0, 0, p[i])),
            ],
            out_specs=[whole((rows, width))] * 2
            + [pl.BlockSpec((1, rows, width), lambda i, p: (jnp.maximum(i - 2, 0), 0, 0))],
        ),
        out_shape=[one, one, jax.ShapeDtypeStruct((2, rows, width), BF16)],
        compiler_params=params(32),
        cost_estimate=cost(10 * rows * cols, 10 * rows * cols),
        name="decode",
    )(order, outer, inner)


def pre_kernel(factor, counts, has_sum, last, off_ref, *refs):
    n = len(counts)
    refs = list(refs)
    x_refs = [refs.pop(0) for _ in range(2)]
    pieces = [refs.pop(0) for _ in range(n)]
    sums = [refs.pop(0) for _ in range(2)] if has_sum else [None, None]
    cots = [refs.pop(0) for _ in range(2)] if last else [None, None]
    for x_ref, sum_ref, cot_ref, out_ref in zip(x_refs, sums, cots, refs):
        pre = sum_ref[...] if has_sum else None
        at = 0
        for piece, count in zip(pieces, counts):
            depth = piece.shape[0] // count
            for part in range(count):
                cols = pl.ds(pl.multiple_of(off_ref[at], 256), depth)
                rows = piece[part * depth:(part + 1) * depth]
                term = jnp.dot(x_ref[:, cols], rows, preferred_element_type=F32)
                pre = term if pre is None else pre + term
                at += 1
        if last:
            pre = pre * factor
            sig = 0.5 + 0.5 * jnp.tanh(0.5 * pre)
            pre = (cot_ref[...].astype(F32) * sig * (1.0 + pre * (1.0 - sig))).astype(BF16)
        out_ref[...] = pre


def pre_of(factor, x_pair, pieces, counts, offs, sums=None, cots=None, cot_block=None):
    toks, feats = x_pair[0].shape
    width = pieces[0].shape[1]
    depth = sum(p.shape[0] for p in pieces)
    tile = toks // 2
    n = len(offs)
    scalars = jnp.stack(list(offs) + [0 if cot_block is None else cot_block]).astype(jnp.int32)
    row = pl.BlockSpec((tile, width), lambda i, s: (i, 0))
    in_specs = [pl.BlockSpec((tile, feats), lambda i, s: (i, 0))] * 2
    in_specs += [whole(p.shape) for p in pieces]
    args = list(x_pair) + list(pieces)
    if sums is not None:
        in_specs += [row, row]
        args += list(sums)
    if cots is not None:
        in_specs += [pl.BlockSpec((tile, width), lambda i, s: (i, s[n])), row]
        args += list(cots)
    last = cots is not None
    return pl.pallas_call(
        functools.partial(pre_kernel, factor, counts, sums is not None, last),
        grid_spec=pltpu.PrefetchScalarGridSpec(
            num_scalar_prefetch=1,
            grid=(toks // tile,),
            in_specs=in_specs,
            out_specs=[row, row],
        ),
        out_shape=[jax.ShapeDtypeStruct((toks, width), BF16 if last else F32)] * 2,
        compiler_params=params(60 if last else 48),
        cost_estimate=cost(4 * toks * depth * width, 4 * toks * feats + 2 * depth * width + 8 * toks * width),
        name="slope" if last else "pre",
    )(scalars, *args)


def wgrad_kernel(halves, blk_ref, xo_ref, xp_ref, so_ref, sp_ref, *out_refs):
    step = pl.program_id(0)
    dims = (((0,), (0,)), ((), ()))
    term = lax.dot_general(xo_ref[...], so_ref[...], dims, preferred_element_type=F32)
    term = term + lax.dot_general(xp_ref[...], sp_ref[...], dims, preferred_element_type=F32)
    term = term.astype(BF16)
    out_refs = list(out_refs)
    for k, halved in enumerate(halves):
        mine = [out_refs.pop(0) for _ in range(2 if halved else 1)]

        @pl.when(step == k)
        def _(mine=mine):
            at = 0
            for ref in mine:
                ref[...] = term[at:at + ref.shape[0]]
                at += ref.shape[0]


def wgrad_of(blks, halves, x_pair, slopes):
    toks, feats = x_pair[0].shape
    width = slopes[0].shape[1]
    n = len(blks)
    rows = feats // (NZ * NY)
    shapes = []
    for halved in halves:
        shapes += [(rows // 2, width)] * 2 if halved else [(rows, width)]
    outs = pl.pallas_call(
        functools.partial(wgrad_kernel, halves),
        grid_spec=pltpu.PrefetchScalarGridSpec(
            num_scalar_prefetch=1,
            grid=(n,),
            in_specs=[pl.BlockSpec((toks, rows), lambda i, b: (0, b[i]))] * 2
            + [whole((toks, width))] * 2,
            out_specs=[whole(s) for s in shapes],
        ),
        out_shape=[jax.ShapeDtypeStruct(s, BF16) for s in shapes],
        compiler_params=params(48),
        cost_estimate=cost(4 * toks * n * rows * width, 4 * toks * n * rows + 2 * n * rows * width),
        name="wgrad",
    )(jnp.stack(blks).astype(jnp.int32), *x_pair, *slopes)
    outs = list(outs)
    return [[outs.pop(0) for _ in range(2)] if halved else outs.pop(0) for halved in halves]


def igrad_kernel(factor, counts, has_term, off_ref, s_ref, *refs):
    out_ref = refs[-1]
    n = len(counts)
    at = 0
    dims = (((1,), (1,)), ((), ()))
    for piece, count in zip(refs[:n], counts):
        depth = piece.shape[0] // count
        for part in range(count):
            cols = pl.ds(pl.multiple_of(off_ref[at], 256), depth)
            rows = piece[part * depth:(part + 1) * depth]
            total = lax.dot_general(s_ref[...], rows, dims, preferred_element_type=F32)
            if has_term:
                total = (total + refs[n][:, cols].astype(F32)) * factor
            out_ref[:, cols] = total.astype(BF16)
            at += 1


def igrad_of(factor, counts, offs, slope, pieces, term=None):
    toks, width = slope.shape
    feats = sum(p.shape[0] for p in pieces)
    tile = toks // 2
    extra = [] if term is None else [term]
    return pl.pallas_call(
        functools.partial(igrad_kernel, factor, counts, term is not None),
        grid_spec=pltpu.PrefetchScalarGridSpec(
            num_scalar_prefetch=1,
            grid=(toks // tile,),
            in_specs=[pl.BlockSpec((tile, width), lambda i, s: (i, 0))]
            + [whole(p.shape) for p in pieces]
            + [pl.BlockSpec((tile, feats), lambda i, s: (i, 0)) for _ in extra],
            out_specs=pl.BlockSpec((tile, feats), lambda i, s: (i, 0)),
        ),
        out_shape=jax.ShapeDtypeStruct((toks, feats), BF16),
        compiler_params=params(48),
        cost_estimate=cost(2 * toks * feats * width, 2 * toks * feats + 2 * feats * width),
        name="igrad",
    )(jnp.stack(offs).astype(jnp.int32), slope, *pieces, *extra)


def by_core(core, mine, other, axis):
    return jnp.where(
        core == 0,
        jnp.concatenate([mine, other], axis=axis),
        jnp.concatenate([other, mine], axis=axis),
    )


def place_kernel(order_ref, own_ref, near_ref, out_ref):
    step = pl.program_id(0)

    @pl.when(step < 2)
    def _():
        out_ref[...] = own_ref[0]

    @pl.when(step >= 2)
    def _():
        out_ref[...] = near_ref[0]


def side_by_side(order, own, near):
    half, rows, width = own.shape
    n = 2 * half
    return pl.pallas_call(
        place_kernel,
        grid_spec=pltpu.PrefetchScalarGridSpec(
            num_scalar_prefetch=1,
            grid=(n,),
            in_specs=[
                pl.BlockSpec((1, rows, width), lambda i, p: (jnp.minimum(i, 1), 0, 0)),
                pl.BlockSpec((1, rows, width), lambda i, p: (jnp.maximum(i - 2, 0), 0, 0)),
            ],
            out_specs=pl.BlockSpec((rows, width), lambda i, p: (0, p[i])),
        ),
        out_shape=jax.ShapeDtypeStruct((rows, n * width), own.dtype),
        compiler_params=params(32),
        cost_estimate=cost(0, 4 * n * rows * width),
        name="place",
    )(order, own, near)


def hold(a, *deps):
    return lax.optimization_barrier((a,) + deps)[0]


def shards(tokens, cotangent, next_weight, inner_weight, outer_weight, momentum):
    toks, feats = tokens.shape
    factor = feats ** (-0.5)
    me = lax.axis_index("shard")
    z, y, core = me // (NY * NC), (me // NC) % NY, me % NC
    pos = lax.axis_index("replica")
    low = pos % NL
    x = pos // NL
    near = x + 1 - 2 * (x % 2)
    order = jnp.stack([x, NX - 1 - x, near, NX - 1 - near]).astype(jnp.int32)

    blk = {(dz, dy): ((z + dz) % NZ) * NY + (y + dy) % NY for dz, dy in DIRS}
    rows = feats // (NZ * NY)
    half = rows // 2
    cols = next_weight.shape[2] // NC

    def offs(*dirs):
        out = []
        for d in dirs:
            at = blk[d[:2]] * rows
            out.append(at + half if d[2:] == (1,) else at)
        return out

    keep = lax.dynamic_slice_in_dim(next_weight[0], core * cols, cols, 1)
    give = lax.dynamic_slice_in_dim(next_weight[0], (1 - core) * cols, cols, 1)
    w00 = by_core(core, keep, to_core(give), 0)

    w30, w10 = to_zp(w00), to_zm(w00)
    a01, b01 = to_y(w00[:half]), to_y(w00[half:])
    x_pair = (tokens, to_core(hold(tokens, w00)))
    own_dec, far_dec, near_dec = decode(order, hold(outer_weight, w00), inner_weight)
    near_got = to_near(hold(near_dec, x_pair[1], a01))
    a01h = hold(a01, own_dec)
    a31, a11 = to_zp(a01h), to_zm(a01h)
    b20 = to_zm(w10[half:])
    b31_b11 = to_y(hold(jnp.concatenate([w30[half:], w10[half:]], axis=0), b01))
    a20 = to_zp(w30[:half])

    first, first_counts = [w00, w30, w10, a01, b01], [1] * 5
    first_offs = offs((0, 0), (3, 0), (1, 0), (0, 1), (0, 1, 1))
    sums = pre_of(factor, x_pair, first, first_counts, first_offs)
    a21 = to_zm(hold(a11, sums[0]))
    b21 = to_y(hold(b20, sums[0], b31_b11))
    far_send = add(far_dec, hold(near_got, sums[0])[1]).astype(BF16)
    far_got = to_far(far_send)
    cot_give = lax.dynamic_slice_in_dim(cotangent, (1 - core) * cols, cols, 1)
    cots = (cotangent, to_core(hold(cot_give, sums[0])))
    second, second_counts = [a20, b20, a31, b31_b11, a11], [1, 1, 1, 2, 1]
    second_offs = offs((2, 0), (2, 0, 1), (3, 1), (3, 1, 1), (1, 1, 1), (1, 1))
    sums = pre_of(
        factor, x_pair, second, second_counts, second_offs, (hold(sums[0], far_send), sums[1])
    )

    share = momentum.shape[1]

    def share_of(a, which):
        return lax.dynamic_slice_in_dim(a, which * share, share, 1)

    x_terms = (own_dec, near_got[0], hold(far_got, sums[0]))
    other = add(*[share_of(a, 1 - low) for a in x_terms]).astype(BF16)
    third, third_offs = [a21, b21], offs((2, 1), (2, 1, 1))
    slopes = pre_of(
        factor, x_pair, third, [1, 1], third_offs, (hold(sums[0], other), sums[1]), cots, core
    )
    got = hold(to_l(other), slopes[0])
    average = add(*[share_of(a, low) for a in x_terms], got) / (NX * NL)
    outer_share = lax.dynamic_slice_in_dim(outer_weight, pos * share, share, 1)
    new_momentum = 0.9 * momentum + average
    new_outer = outer_share - 0.7 * (average + 0.9 * new_momentum)
    inner_share = new_outer.astype(BF16)
    inner_other = to_l(inner_share)

    early, late = [(2, 1), (3, 1)], [(1, 1), (2, 0), (3, 0), (1, 0), (0, 1), (0, 0)]
    g21, g31 = wgrad_of(
        [blk[d] for d in early], (False,) * 2, x_pair, (hold(slopes[0], inner_share), slopes[1])
    )
    inner_pair = by_core(low, inner_share, hold(inner_other, g21), 1)
    inner_far = to_far(inner_pair)

    r31, r21 = to_zm(g31), to_zp(g21)
    late_slopes = (hold(slopes[0], inner_pair), slopes[1])
    g11, g20, g30, g10, g01, g00 = wgrad_of(
        [blk[d] for d in late], (False,) * 6, x_pair, late_slopes
    )

    s11 = add(g11, r21).astype(BF16)
    r11, r20 = to_zp(s11), to_zm(hold(g20, r31))
    inner_own = jnp.stack([inner_pair, inner_far])
    inner_near = to_near(inner_own)
    pieces, counts = first + second + third, first_counts + second_counts + [1, 1]
    piece_offs = first_offs + second_offs + third_offs
    part = igrad_of(factor, counts, piece_offs, hold(slopes[1], s11, r31, inner_own), pieces)

    s30 = add(g30, hold(r20, part)).astype(BF16)
    s01 = add(g01, r31, hold(r11, part, inner_near)).astype(BF16)
    t30, t01, t10 = to_zm(s30), to_y(s01), to_zp(hold(g10, s01))
    part_got = to_core(hold(part, s30, s01))
    input_grad = igrad_of(
        factor, counts, piece_offs, hold(slopes[0], s30, s01, inner_near), pieces, part_got
    )
    new_inner = side_by_side(order, hold(inner_own, input_grad), inner_near)
    g00 = hold(g00, input_grad, new_inner)

    def rows_of(which):
        terms = [lax.dynamic_slice_in_dim(a, which * half, half, 0) for a in (g00, t30, t10, t01)]
        return add(*terms) * factor

    weight_grad = by_core(core, rows_of(core), to_core(rows_of(1 - core)), 1)[None]
    return (input_grad, weight_grad, new_outer, new_momentum, new_inner)


def solution(mesh):
    return jax.shard_map(
        shards,
        mesh=mesh,
        in_specs=(
            P(("replica", "shard"), None),
            P(("replica", "shard"), None),
            P("replica", "shard", None),
            P("replica", "shard", None),
            P("shard", None),
            P("shard", "replica"),
        ),
        out_specs=(
            P(("replica", "shard"), None),
            P("replica", "shard", None),
            P("shard", "replica"),
            P("shard", "replica"),
            P("shard", None),
        ),
        check_vma=False,
    )
```

time: 410 us -> 198 us (0.48)
  waiting for transfers between devices: 317 us -> 40.7 us
  Pallas kernels: 0 us -> 74.2 us
  matrix products: 49.1 us -> 0 us
  starting transfers between devices: 0.35 us -> 42.8 us
  between operations: 15.7 us -> 0.91 us
  local copies, waits for them, and re-layouts: 9.87 us -> 16.4 us
  other arithmetic: 18.1 us -> 22.3 us
    psum x1 -> x0, waiting for transfers between devices: 162 us -> none  [shards(): lax.psum(decoded.astype(jnp.bfloat16), 'replica').astype(jnp.float32)]
    reduce_scatter x1 -> x0, waiting for transfers between devices: 134 us -> none  [shards(): lax.psum_scatter(lax.dot_general(tokens, slope, (((0,), (0,)), ((), ())),...]
    pallas_call x0 -> x9, Pallas kernels: none -> 74.2 us  [the longest x3 26.7 us: pre_of(): pl.pallas_call(functools.partial(pre_kernel, factor, counts, sums is not...]
    dot_general x3 -> x0, matrix products: 49.1 us -> none  [the longest x1 17.5 us: shards(): lax.dot_general(tokens, slope, (((0,), (0,)), ((), ())), preferred_elemen...]
    ppermute x0 -> x29, starting transfers between devices: none -> 42.8 us  [the longest x7 15.7 us: to_zm(): return lax.ppermute(a, 'shard', shard_perm(-1, 0, 0))]
    ppermute x0 -> x29, waiting for transfers between devices: none -> 40.7 us  [the longest x6 25.2 us: to_zp(): return lax.ppermute(a, 'shard', shard_perm(1, 0, 0))]
    all_gather x2 -> x0, waiting for transfers between devices: 19.5 us -> none  [the longest x1 19.4 us: shards(): lax.all_gather(new_outer.astype(jnp.bfloat16), 'replica', axis=1, tiled=T...]
    concatenate x0 -> x2, other arithmetic: none -> 4.9 us  [the longest x1 2.7 us: by_core(): jnp.concatenate([mine, other], axis=axis)]
  transfers between devices with their start and end apart: 4 -> 29, of which waited for: 3 -> 11; matrix products, arithmetic and copies ran while one was open for 13% -> 8% of each run, Pallas kernels for 0% -> 38%
where the time goes in v2:
time: 198 us; the launch traced here: 197 us
  Pallas kernels  74.2 us (37%)
  starting transfers between devices  42.8 us (22%)
  waiting for transfers between devices  40.7 us (21%)
  other arithmetic  22.3 us (11%)
  local copies, waits for them, and re-layouts  16.4 us (8%)
    pallas_call x3, Pallas kernels, pre_of(): pl.pallas_call(functools.partial(pre_kernel, factor, counts, sums is not...  26.7 us
    ppermute x6, waiting for transfers between devices, to_zp(): return lax.ppermute(a, 'shard', shard_perm(1, 0, 0))  25.2 us
    pallas_call x2, Pallas kernels, igrad_of(): pl.pallas_call(functools.partial(igrad_kernel, factor, counts, term is no...  20.2 us
    pallas_call x2, Pallas kernels, wgrad_of(): pl.pallas_call(functools.partial(wgrad_kernel, halves), grid_spec=pltpu.P...  18.7 us
    ppermute x7, starting transfers between devices, to_zm(): return lax.ppermute(a, 'shard', shard_perm(-1, 0, 0))  15.7 us
    ppermute x5, starting transfers between devices, to_core(): return lax.ppermute(a, 'shard', shard_perm(0, 0, 1))  10.1 us
    ppermute x5, starting transfers between devices, to_y(): return lax.ppermute(a, 'shard', shard_perm(0, 1, 0))  9.36 us
    unnamed x54, local copies, waits for them, and re-layouts  8.59 us
  transfers between devices with their start and end apart: 29, of which 11 were waited for; matrix products, arithmetic and copies ran while one was open for 8% of the time, Pallas kernels for 38%

profile of v2, /device:TPU:1, one launch (start us, length us, event | category | flops | bytes accessed | tf_op | source)
XLA Modules:
  0.0 197.3 jit_solution(12130600897661156317)
XLA Ops:
  0.7 1.3 dynamic-slice_bitcast_fusion.1
  1.9 1.5 collective-permute-start
  3.4 1.5 collective-permute-done
  5.0 0.5 maximum_select_fusion.1.refs_2_.refs_0_
  5.5 0.5 collective-permute-start.1
  5.9 1.7 collective-permute-start.4
  7.6 2.1 %collective-permute-start.5 = (bf16[512,1024]{1,0:T(8,128)(2,1)S(1)}, bf16[512,1024]{1,0:T(8,128)(2,1)S(1)}, u32[]{:S(2)}, u32[]{:S(2)}) collective-permute-start(bf16[512,1024]{1,0:T(8,128)(2,1)S(1)} %maximum_select_fusion.1.refs_2_.refs_0_), channel_id=1, source_target_pairs={{0,12},{1,13},{2,14},{3,15},{4,0},{5,1},{6,2},{7,3},{8,4},{9,5},{1... | collective-permute-start | bytes 3145736 | tf_op jit(solution)/shard_map/ppermute | solution.py:33
  9.8 1.0 fusion.8
  10.8 2.9 %collective-permute-start.2 = (bf16[256,1024]{1,0:T(8,128)(2,1)}, bf16[256,1024]{1,0:T(8,128)(2,1)}, u32[]{:S(2)}, u32[]{:S(2)}) collective-permute-start(bf16[256,1024]{1,0:T(8,128)(2,1)} %get-tuple-element.97), channel_id=1, source_target_pairs={{0,2},{1,3},{2,0},{3,1},{4,6},{5,7},{6,4},{7,5},{8,10},{9,11},{10,... | collective-permute-start | bytes 1572872 | tf_op jit(solution)/shard_map/ppermute | solution.py:37
  13.8 2.2 %copy-done.7 = f32[256,4096]{1,0:T(8,128)S(1)} copy-done((f32[256,4096]{1,0:T(8,128)S(1)}, f32[256,4096]{1,0:T(8,128)}, u32[]{:S(2)}) %copy-start.7) | copy-done | bytes 4194328
  16.0 2.2 %copy-done.15 = f32[1,256,4096]{2,1,0:T(8,128)S(1)} copy-done((f32[1,256,4096]{2,1,0:T(8,128)S(1)}, f32[1,256,4096]{2,1,0:T(8,128)}, u32[]{:S(2)}) %copy-start.15) | copy-done | bytes 4194328
  18.2 4.0 %decode.1 = (bf16[256,1024]{1,0:T(8,128)(2,1)S(1)}, bf16[256,1024]{1,0:T(8,128)(2,1)S(1)}, bf16[2,256,1024]{2,1,0:T(8,128)(2,1)}) custom-call(s32[4]{0:T(128)S(1)} %pad_add_fusion.1.order_ref, f32[256,4096]{1,0:T(8,128)S(1)} %copy-done.7, f32[1,256,4096]{2,1,0:T(8,128)S(1)} %copy-done.15), custom_call_target="tpu_custom_call" | custom-call | flops 3145728 | bytes 3145728 | tf_op jit(solution)/shard_map/decode/pallas_call | solution.py:108
  22.2 3.5 %collective-permute-done.2.refs_5_.refs_3_ = bf16[256,1024]{1,0:T(8,128)(2,1)} collective-permute-done((bf16[256,1024]{1,0:T(8,128)(2,1)}, bf16[256,1024]{1,0:T(8,128)(2,1)}, u32[]{:S(2)}, u32[]{:S(2)}) %collective-permute-start.2) | collective-permute-done | bytes 524320 | tf_op jit(solution)/shard_map/ppermute | solution.py:37
  25.7 1.2 collective-permute-start.13
  26.9 6.4 %collective-permute-done.4.refs_3_.refs_1_ = bf16[512,1024]{1,0:T(8,128)(2,1)S(1)} collective-permute-done((bf16[512,1024]{1,0:T(8,128)(2,1)S(1)}, bf16[512,1024]{1,0:T(8,128)(2,1)S(1)}, u32[]{:S(2)}, u32[]{:S(2)}) %collective-permute-start.4) | collective-permute-done | bytes 1048608 | tf_op jit(solution)/shard_map/ppermute | solution.py:29
  33.3 0.9 fusion.7
  34.2 0.9 slice.31
  35.1 2.2 %pad_maximum_fusion = bf16[512,1024]{1,0:T(8,128)(2,1)} fusion(bf16[256,1024]{1,0:T(8,128)(2,1)} %slice.31, bf16[256,1024]{1,0:T(8,128)(2,1)S(1)} %get-tuple-element.95), kind=kLoop, calls=%fused_computation.5 | loop fusion | flops 2097152 | bytes 2097152 | tf_op jit(solution)/shard_map/concatenate | solution.py:348
  37.3 2.9 %collective-permute-start.9 = (bf16[512,1024]{1,0:T(8,128)(2,1)}, bf16[512,1024]{1,0:T(8,128)(2,1)}, u32[]{:S(2)}, u32[]{:S(2)}) collective-permute-start(bf16[512,1024]{1,0:T(8,128)(2,1)} %pad_maximum_fusion), channel_id=1, source_target_pairs={{0,2},{1,3},{2,0},{3,1},{4,6},{5,7},{6,4},{7,5},{8,10},{9,11},{10,... | collective-permute-start | bytes 3145736 | tf_op jit(solution)/shard_map/ppermute | solution.py:37
  40.2 1.5 collective-permute-start.8
  41.8 2.3 %constant_dynamic-slice_fusion = bf16[512,1024]{1,0:T(8,128)(2,1)} fusion(bf16[512,2048]{1,0:T(8,128)(2,1)} %refs_6_.1, s32[]{:T(128)S(6)} %select_n.159), kind=kLoop, calls=%fused_computation.24 | loop fusion | bytes 2097156 | tf_op jit(solution)/shard_map/dynamic_slice | solution.py:358
  44.0 2.7 %collective-permute-start.3 = (bf16[256,1024]{1,0:T(8,128)(2,1)}, bf16[256,1024]{1,0:T(8,128)(2,1)}, u32[]{:S(2)}, u32[]{:S(2)}) collective-permute-start(bf16[256,1024]{1,0:T(8,128)(2,1)} %collective-permute-done.2.refs_5_.refs_3_), channel_id=1, source_target_pairs={{0,12},{1,13},{2,14},{3,15},{4,0},{5,1},{6,2},{7,3},{8,4},{9,5},{1... | collective-permute-start | bytes 1572872 | tf_op jit(solution)/shard_map/ppermute | solution.py:33
  46.7 8.7 %pre.2 = (f32[512,1024]{1,0:T(8,128)}, f32[512,1024]{1,0:T(8,128)}) custom-call(s32[6]{0:T(128)S(1)} %stack.154.off_ref, bf16[512,4096]{1,0:T(8,128)(2,1)} %xo_ref.3, bf16[512,4096]{1,0:T(8,128)(2,1)} %collective-permute-done.1.refs_1_.xp_ref, bf16[512,1024]{1,0:T(8,128)(2,1)S(1)} %maximum_select_fusion.1.refs_2_.refs_0_, ...), custom_call_target="tpu_custom_call" | custom-call | flops 1288490240 | bytes 5033164 | tf_op jit(solution)/shard_map/pre/pallas_call | solution.py:170
  55.5 2.2 %collective-permute-start.15 = (bf16[512,1024]{1,0:T(8,128)(2,1)}, bf16[512,1024]{1,0:T(8,128)(2,1)}, u32[]{:S(2)}, u32[]{:S(2)}) collective-permute-start(bf16[512,1024]{1,0:T(8,128)(2,1)} %constant_dynamic-slice_fusion), channel_id=1, source_target_pairs={{0,1},{1,0},{2,3},{3,2},{4,5},{5,4},{6,7},{7,6},{8,9},{9,8},{10,11... | collective-permute-start | bytes 3145736 | tf_op jit(solution)/shard_map/ppermute | solution.py:41
  57.7 1.2 fusion
  58.9 4.1 %collective-permute-done.9.refs_5_.refs_8_ = bf16[512,1024]{1,0:T(8,128)(2,1)} collective-permute-done((bf16[512,1024]{1,0:T(8,128)(2,1)}, bf16[512,1024]{1,0:T(8,128)(2,1)}, u32[]{:S(2)}, u32[]{:S(2)}) %collective-permute-start.9) | collective-permute-done | bytes 1048608 | tf_op jit(solution)/shard_map/ppermute | solution.py:37
  63.0 2.5 %collective-permute-start.14 = (bf16[256,1024]{1,0:T(8,128)(2,1)S(1)}, bf16[256,1024]{1,0:T(8,128)(2,1)}, u32[]{:S(2)}, u32[]{:S(2)}) collective-permute-start(bf16[256,1024]{1,0:T(8,128)(2,1)S(1)} %fusion), channel_id=1, source_target_pairs={{0,96},{16,112},{32,64},{48,80},{64,32},{80,48},{96,0},{112,16},{1... | collective-permute-start | bytes 1572872 | tf_op jit(solution)/shard_map/ppermute | solution.py:54
  65.5 2.7 %collective-permute-start.10 = (bf16[256,1024]{1,0:T(8,128)(2,1)}, bf16[256,1024]{1,0:T(8,128)(2,1)S(1)}, u32[]{:S(2)}, u32[]{:S(2)}) collective-permute-start(bf16[256,1024]{1,0:T(8,128)(2,1)} %collective-permute-done.8.refs_3_.refs_6_), channel_id=1, source_target_pairs={{0,2},{1,3},{2,0},{3,1},{4,6},{5,7},{6,4},{7,5},{8,10},{9,11},{10,... | collective-permute-start | bytes 1572872 | tf_op jit(solution)/shard_map/ppermute | solution.py:37
  68.2 0.8 copy-done.8
  69.0 1.4 collective-permute-start.7
  70.6 1.1 slice.34
  71.7 1.0 copy-done.9
  72.7 9.2 %pre.3 = (f32[512,1024]{1,0:T(8,128)S(1)}, f32[512,1024]{1,0:T(8,128)}) custom-call(s32[7]{0:T(128)S(1)} %stack.155.off_ref, bf16[512,4096]{1,0:T(8,128)(2,1)} %xo_ref.3, bf16[512,4096]{1,0:T(8,128)(2,1)} %collective-permute-done.1.refs_1_.xp_ref, bf16[256,1024]{1,0:T(8,128)(2,1)S(1)} %collective-permute-done.11.refs_2_.refs_5_, ...), custom_call_target="tpu_custom_call" | custom-call | flops 966367616 | bytes 4718592 | tf_op jit(solution)/shard_map/pre/pallas_call | solution.py:170
  81.9 1.3 copy-done.16
  83.2 1.1 fusion.5
  84.3 0.9 collective-permute-start.16
  85.3 0.6 pad_add_fusion.off_ref
  85.9 0.8 copy-done.11
  86.8 8.8 %slope.1 = (bf16[512,1024]{1,0:T(8,128)(2,1)}, bf16[512,1024]{1,0:T(8,128)(2,1)}) custom-call(s32[3]{0:T(128)} %pad_add_fusion.off_ref, bf16[512,4096]{1,0:T(8,128)(2,1)} %xo_ref.3, bf16[512,4096]{1,0:T(8,128)(2,1)} %collective-permute-done.1.refs_1_.xp_ref, bf16[256,1024]{1,0:T(8,128)(2,1)} %copy-done.13, bf16[256,1024]{1,0:T(8,128)(2,1)} %copy-done.11, ...), custom_call_target="tpu_custom_call" | custom-call | flops 322122560 | bytes 4089446 | tf_op jit(solution)/shard_map/slope/pallas_call | solution.py:170
  95.7 2.5 %fusion.6 = (bf16[256,512]{1,0:T(8,128)(2,1)S(1)}, f32[256,512]{1,0:T(8,128)}, f32[256,512]{1,0:T(8,128)}) fusion(bf16[256,512]{1,0:T(8,128)(2,1)S(1)} %collective-permute-done.16, bf16[256,1024]{1,0:T(8,128)(2,1)} %collective-permute-done.14, s32[]{:T(128)S(6)} %select_n.167, bf16[1,256,1024]{2,1,0:T(8,128)(2,1)S(1)} %slice.34, ...), kind=kLoop, calls=%fused_computation.28 | loop fusion | flops 1966080 | bytes 3407880 | tf_op jit(solution)/shard_map/convert_element_type | solution.py:382
  98.2 0.8 collective-permute-start.17
  99.0 5.9 %wgrad.2 = (bf16[512,1024]{1,0:T(8,128)(2,1)}, bf16[512,1024]{1,0:T(8,128)(2,1)}) custom-call(s32[2]{0:T(128)S(1)} %pad_add_fusion.2.blk_ref, bf16[512,4096]{1,0:T(8,128)(2,1)} %xo_ref.3, bf16[512,4096]{1,0:T(8,128)(2,1)} %collective-permute-done.1.refs_1_.xp_ref, bf16[512,1024]{1,0:T(8,128)(2,1)S(1)} %copy-done.3, bf16[512,1024]{1,0:T(8,128)(2,1)S(1)} %copy-done.5), custom_call_target="tpu_custom_call" | custom-call | flops 644245120 | bytes 1258291 | tf_op jit(solution)/shard_map/wgrad/pallas_call | solution.py:211
  105.0 2.7 %collective-permute-start.18 = (bf16[512,1024]{1,0:T(8,128)(2,1)}, bf16[512,1024]{1,0:T(8,128)(2,1)}, u32[]{:S(2)}, u32[]{:S(2)}) collective-permute-start(bf16[512,1024]{1,0:T(8,128)(2,1)} %get-tuple-element.75), channel_id=1, source_target_pairs={{0,12},{1,13},{2,14},{3,15},{4,0},{5,1},{6,2},{7,3},{8,4},{9,5},{1... | collective-permute-start | bytes 3145736 | tf_op jit(solution)/shard_map/ppermute | solution.py:33
  108.3 12.8 %wgrad.3 = (bf16[512,1024]{1,0:T(8,128)(2,1)S(1)}, bf16[512,1024]{1,0:T(8,128)(2,1)}, bf16[512,1024]{1,0:T(8,128)(2,1)S(1)}, bf16[512,1024]{1,0:T(8,128)(2,1)}, ...) custom-call(s32[6]{0:T(128)S(1)} %stack.162.blk_ref, bf16[512,4096]{1,0:T(8,128)(2,1)} %xo_ref.3, ...), custom_call_target="tpu_custom_call" | custom-call | flops 1932735232 | bytes 3774873 | tf_op jit(solution)/shard_map/wgrad/pallas_call | solution.py:211
  121.1 1.2 pad_maximum_fusion.1.own_ref
  122.4 5.5 %collective-permute-done.20 = bf16[512,1024]{1,0:T(8,128)(2,1)} collective-permute-done((bf16[512,1024]{1,0:T(8,128)(2,1)}, bf16[512,1024]{1,0:T(8,128)(2,1)}, u32[]{:S(2)}, u32[]{:S(2)}) %collective-permute-start.20) | collective-permute-done | bytes 1048608 | tf_op jit(solution)/shard_map/ppermute | solution.py:29
  127.9 2.6 %add_convert_fusion.2 = bf16[512,1024]{1,0:T(8,128)(2,1)} fusion(bf16[512,1024]{1,0:T(8,128)(2,1)} %collective-permute-done.20, bf16[512,1024]{1,0:T(8,128)(2,1)S(1)} %get-tuple-element.77), kind=kLoop, calls=%fused_computation.3 | loop fusion | flops 2097152 | bytes 3145728 | tf_op jit(solution)/shard_map/convert_element_type | solution.py:398
  130.5 2.7 %collective-permute-start.19 = (bf16[512,1024]{1,0:T(8,128)(2,1)}, bf16[512,1024]{1,0:T(8,128)(2,1)}, u32[]{:S(2)}, u32[]{:S(2)}) collective-permute-start(bf16[512,1024]{1,0:T(8,128)(2,1)} %get-tuple-element.76), channel_id=1, source_target_pairs={{0,12},{1,13},{2,14},{3,15},{4,0},{5,1},{6,2},{7,3},{8,4},{9,5},{1... | collective-permute-start | bytes 3145736 | tf_op jit(solution)/shard_map/ppermute | solution.py:33
  133.3 9.8 %igrad.2 = bf16[512,4096]{1,0:T(8,128)(2,1)} custom-call(s32[13]{0:T(128)S(1)} %stack.146.off_ref, bf16[512,1024]{1,0:T(8,128)(2,1)S(1)} %copy-done.6, bf16[512,1024]{1,0:T(8,128)(2,1)} %copy-done, bf16[512,1024]{1,0:T(8,128)(2,1)} %copy-done.1, bf16[512,1024]{1,0:T(8,128)(2,1)} %copy-done.2, bf16[256,1024]{1,0:T(8,128)(2,1)} %collective-permute-done.2.refs_5_.refs_3_, ...), custom_call_target="tpu_custom_call" | custom-call | flops 1288490240 | bytes 3774873 | tf_op jit(solution)/shard_map/igrad/pallas_call | solution.py:251
  143.2 9.2 %collective-permute-done.22 = bf16[512,1024]{1,0:T(8,128)(2,1)} collective-permute-done((bf16[512,1024]{1,0:T(8,128)(2,1)}, bf16[512,1024]{1,0:T(8,128)(2,1)}, u32[]{:S(2)}, u32[]{:S(2)}) %collective-permute-start.22) | collective-permute-done | bytes 1048608 | tf_op jit(solution)/shard_map/ppermute | solution.py:29
  152.4 2.7 %add_convert_fusion.1 = bf16[512,1024]{1,0:T(8,128)(2,1)} fusion(bf16[512,1024]{1,0:T(8,128)(2,1)} %collective-permute-done.19, bf16[512,1024]{1,0:T(8,128)(2,1)S(1)} %copy-done.18), kind=kLoop, calls=%fused_computation.2 | loop fusion | flops 2097152 | bytes 3145728 | tf_op jit(solution)/shard_map/convert_element_type | solution.py:406
  155.1 3.0 %add_convert_fusion = bf16[512,1024]{1,0:T(8,128)(2,1)} fusion(bf16[512,1024]{1,0:T(8,128)(2,1)} %collective-permute-done.22, bf16[512,1024]{1,0:T(8,128)(2,1)} %collective-permute-done.18, bf16[512,1024]{1,0:T(8,128)(2,1)S(1)} %copy-done.20), kind=kLoop, calls=%fused_computation.1 | loop fusion | flops 3145728 | bytes 4194304 | tf_op jit(solution)/shard_map/convert_element_type | solution.py:407
  158.1 5.1 %collective-permute-start.24 = (bf16[512,4096]{1,0:T(8,128)(2,1)}, bf16[512,4096]{1,0:T(8,128)(2,1)}, u32[]{:S(2)}, u32[]{:S(2)}) collective-permute-start(bf16[512,4096]{1,0:T(8,128)(2,1)} %igrad.2), channel_id=1, source_target_pairs={{0,1},{1,0},{2,3},{3,2},{4,5},{5,4},{6,7},{7,6},{8,9},{9,8},{10,11... | collective-permute-start | bytes 12582920 | tf_op jit(solution)/shard_map/ppermute | solution.py:41
  163.3 0.8 collective-permute-start.27
  164.1 2.7 %collective-permute-start.25 = (bf16[512,1024]{1,0:T(8,128)(2,1)}, bf16[512,1024]{1,0:T(8,128)(2,1)}, u32[]{:S(2)}, u32[]{:S(2)}) collective-permute-start(bf16[512,1024]{1,0:T(8,128)(2,1)} %add_convert_fusion.1), channel_id=1, source_target_pairs={{0,12},{1,13},{2,14},{3,15},{4,0},{5,1},{6,2},{7,3},{8,4},{9,5},{1... | collective-permute-start | bytes 3145736 | tf_op jit(solution)/shard_map/ppermute | solution.py:33
  166.8 3.6 %collective-permute-done.24.refs_12_ = bf16[512,4096]{1,0:T(8,128)(2,1)} collective-permute-done((bf16[512,4096]{1,0:T(8,128)(2,1)}, bf16[512,4096]{1,0:T(8,128)(2,1)}, u32[]{:S(2)}, u32[]{:S(2)}) %collective-permute-start.24) | collective-permute-done | bytes 4194336 | tf_op jit(solution)/shard_map/ppermute | solution.py:41
  170.4 10.4 %igrad.3 = bf16[512,4096]{1,0:T(8,128)(2,1)} custom-call(s32[13]{0:T(128)S(1)} %stack.146.off_ref, bf16[512,1024]{1,0:T(8,128)(2,1)S(1)} %copy-done.4, bf16[512,1024]{1,0:T(8,128)(2,1)} %copy-done, bf16[512,1024]{1,0:T(8,128)(2,1)} %copy-done.1, bf16[512,1024]{1,0:T(8,128)(2,1)} %copy-done.2, bf16[256,1024]{1,0:T(8,128)(2,1)} %collective-permute-done.2.refs_5_.refs_3_, ...), custom_call_target="tpu_custom_call" | custom-call | flops 1288490240 | bytes 3774873 | tf_op jit(solution)/shard_map/igrad/pallas_call | solution.py:251
  180.9 4.6 %place.1 = bf16[256,4096]{1,0:T(8,128)(2,1)} custom-call(s32[4]{0:T(128)S(1)} %pad_add_fusion.1.order_ref, bf16[2,256,1024]{2,1,0:T(8,128)(2,1)} %pad_maximum_fusion.1.own_ref, bf16[2,256,1024]{2,1,0:T(8,128)(2,1)} %collective-permute-done.23.near_ref), custom_call_target="tpu_custom_call" | custom-call | bytes 1258291 | tf_op jit(solution)/shard_map/place/pallas_call | solution.py:291
  185.5 4.1 %collective-permute-done.26 = bf16[512,1024]{1,0:T(8,128)(2,1)} collective-permute-done((bf16[512,1024]{1,0:T(8,128)(2,1)}, bf16[512,1024]{1,0:T(8,128)(2,1)}, u32[]{:S(2)}, u32[]{:S(2)}) %collective-permute-start.26) | collective-permute-done | bytes 1048608 | tf_op jit(solution)/shard_map/ppermute | solution.py:29
  189.6 0.3 collective-permute-done.27
  189.9 2.7 %multiply_bitcast_fusion = (f32[1,256,1024]{2,1,0:T(8,128)S(1)}, f32[256,1024]{1,0:T(8,128)S(1)}) fusion(bf16[512,1024]{1,0:T(8,128)(2,1)} %collective-permute-done.27, s32[]{:T(128)S(6)} %select_n.172, bf16[512,1024]{1,0:T(8,128)(2,1)} %collective-permute-done.26, bf16[512,1024]{1,0:T(8,128)(2,1)} %collective-permute-done.25, ...), kind=kLoop, calls=%fused_computation.10 | loop fusion | flops 4194304 | bytes 6291464 | tf_op jit(solution)/shard_map/concatenate | solution.py:271
  192.6 0.9 collective-permute-start.28
  193.5 2.3 %collective-permute-done.28 = f32[256,1024]{1,0:T(8,128)S(1)} collective-permute-done((f32[256,1024]{1,0:T(8,128)S(1)}, f32[256,1024]{1,0:T(8,128)S(1)}, u32[]{:S(2)}, u32[]{:S(2)}) %collective-permute-start.28) | collective-permute-done | bytes 1048608 | tf_op jit(solution)/shard_map/ppermute | solution.py:41
  195.8 1.6 maximum_select_fusion
  (83 shorter events, 1.7 us)
Async XLA Ops:
  1.9 3.0 %collective-permute-start = (bf16[256,1024]{1,0:T(8,128)(2,1)S(1)}, bf16[256,1024]{1,0:T(8,128)(2,1)S(1)}, u32[]{:S(2)}, u32[]{:S(2)}) collective-permute-start(bf16[256,1024]{1,0:T(8,128)(2,1)S(1)} %get-tuple-element.99), channel_id=1, source_target_pairs={{0,1},{1,0},{2,3},{3,2},{4,5},{5,4},{6,7},{7,6},{8,9},{9,8},{10,11... | collective-permute-start | bytes 1572872 | tf_op jit(solution)/shard_map/ppermute | solution.py:41
  5.5 41.3 %copy-start = (bf16[512,1024]{1,0:T(8,128)(2,1)}, bf16[512,1024]{1,0:T(8,128)(2,1)S(1)}, u32[]{:S(2)}) copy-start(bf16[512,1024]{1,0:T(8,128)(2,1)S(1)} %maximum_select_fusion.1.refs_2_.refs_0_) | copy-start | bytes 3145732
  5.5 20.2 %collective-permute-start.1 = (bf16[512,4096]{1,0:T(8,128)(2,1)}, bf16[512,4096]{1,0:T(8,128)(2,1)}, u32[]{:S(2)}, u32[]{:S(2)}) collective-permute-start(bf16[512,4096]{1,0:T(8,128)(2,1)} %xo_ref.3), channel_id=1, source_target_pairs={{0,1},{1,0},{2,3},{3,2},{4,5},{5,4},{6,7},{7,6},{8,9},{9,8},{10,11... | collective-permute-start | bytes 12582920 | tf_op jit(solution)/shard_map/ppermute | solution.py:41
  5.9 27.3 %collective-permute-start.4 = (bf16[512,1024]{1,0:T(8,128)(2,1)S(1)}, bf16[512,1024]{1,0:T(8,128)(2,1)S(1)}, u32[]{:S(2)}, u32[]{:S(2)}) collective-permute-start(bf16[512,1024]{1,0:T(8,128)(2,1)S(1)} %maximum_select_fusion.1.refs_2_.refs_0_), channel_id=1, source_target_pairs={{0,4},{1,5},{2,6},{3,7},{4,8},{5,9},{6,10},{7,11},{8,12},{9,13},{1... | collective-permute-start | bytes 3145736 | tf_op jit(solution)/shard_map/ppermute | solution.py:29
  7.6 26.6 %collective-permute-start.5 = (bf16[512,1024]{1,0:T(8,128)(2,1)S(1)}, bf16[512,1024]{1,0:T(8,128)(2,1)S(1)}, u32[]{:S(2)}, u32[]{:S(2)}) collective-permute-start(bf16[512,1024]{1,0:T(8,128)(2,1)S(1)} %maximum_select_fusion.1.refs_2_.refs_0_), channel_id=1, source_target_pairs={{0,12},{1,13},{2,14},{3,15},{4,0},{5,1},{6,2},{7,3},{8,4},{9,5},{1... | collective-permute-start | bytes 3145736 | tf_op jit(solution)/shard_map/ppermute | solution.py:33
  10.8 14.9 %collective-permute-start.2 = (bf16[256,1024]{1,0:T(8,128)(2,1)}, bf16[256,1024]{1,0:T(8,128)(2,1)}, u32[]{:S(2)}, u32[]{:S(2)}) collective-permute-start(bf16[256,1024]{1,0:T(8,128)(2,1)} %get-tuple-element.97), channel_id=1, source_target_pairs={{0,2},{1,3},{2,0},{3,1},{4,6},{5,7},{6,4},{7,5},{8,10},{9,11},{10,... | collective-permute-start | bytes 1572872 | tf_op jit(solution)/shard_map/ppermute | solution.py:37
  13.7 23.6 %collective-permute-start.6 = (bf16[256,1024]{1,0:T(8,128)(2,1)}, bf16[256,1024]{1,0:T(8,128)(2,1)}, u32[]{:S(2)}, u32[]{:S(2)}) collective-permute-start(bf16[256,1024]{1,0:T(8,128)(2,1)} %get-tuple-element.96), channel_id=1, source_target_pairs={{0,2},{1,3},{2,0},{3,1},{4,6},{5,7},{6,4},{7,5},{8,10},{9,11},{10,... | collective-permute-start | bytes 1572872 | tf_op jit(solution)/shard_map/ppermute | solution.py:37
  13.8 2.2 %copy-start.7 = (f32[256,4096]{1,0:T(8,128)S(1)}, f32[256,4096]{1,0:T(8,128)}, u32[]{:S(2)}) copy-start(f32[256,4096]{1,0:T(8,128)} %outer_ref) | copy-start | bytes 12582916
  16.0 2.2 %copy-start.15 = (f32[1,256,4096]{2,1,0:T(8,128)S(1)}, f32[1,256,4096]{2,1,0:T(8,128)}, u32[]{:S(2)}) copy-start(f32[1,256,4096]{2,1,0:T(8,128)} %inner_ref.1) | copy-start | bytes 12582916
  22.2 15.1 %copy-start.21 = (bf16[256,1024]{1,0:T(8,128)(2,1)}, bf16[256,1024]{1,0:T(8,128)(2,1)S(1)}, u32[]{:S(2)}) copy-start(bf16[256,1024]{1,0:T(8,128)(2,1)S(1)} %get-tuple-element.55) | copy-start | bytes 1572868
  22.2 15.1 %copy-start.23 = (bf16[256,1024]{1,0:T(8,128)(2,1)}, bf16[256,1024]{1,0:T(8,128)(2,1)S(1)}, u32[]{:S(2)}) copy-start(bf16[256,1024]{1,0:T(8,128)(2,1)S(1)} %get-tuple-element.49) | copy-start | bytes 1572868
  25.7 29.7 %collective-permute-start.13 = (bf16[2,256,1024]{2,1,0:T(8,128)(2,1)}, bf16[2,256,1024]{2,1,0:T(8,128)(2,1)}, u32[]{:S(2)}, u32[]{:S(2)}) collective-permute-start(bf16[2,256,1024]{2,1,0:T(8,128)(2,1)} %get-tuple-element.57), channel_id=1, source_target_pairs={{0,32},{16,48},{32,0},{48,16},{64,96},{80,112},{96,64},{112,80},{1... | collective-permute-start | bytes 3145736 | tf_op jit(solution)/shard_map/ppermute | solution.py:49
  33.3 13.4 %copy-start.1 = (bf16[512,1024]{1,0:T(8,128)(2,1)}, bf16[512,1024]{1,0:T(8,128)(2,1)S(1)}, u32[]{:S(2)}) copy-start(bf16[512,1024]{1,0:T(8,128)(2,1)S(1)} %collective-permute-done.4.refs_3_.refs_1_) | copy-start | bytes 3145732
  34.2 12.5 %copy-start.2 = (bf16[512,1024]{1,0:T(8,128)(2,1)}, bf16[512,1024]{1,0:T(8,128)(2,1)S(1)}, u32[]{:S(2)}) copy-start(bf16[512,1024]{1,0:T(8,128)(2,1)S(1)} %collective-permute-done.5.refs_4_.refs_2_) | copy-start | bytes 3145732
  37.3 25.8 %collective-permute-start.9 = (bf16[512,1024]{1,0:T(8,128)(2,1)}, bf16[512,1024]{1,0:T(8,128)(2,1)}, u32[]{:S(2)}, u32[]{:S(2)}) collective-permute-start(bf16[512,1024]{1,0:T(8,128)(2,1)} %pad_maximum_fusion), channel_id=1, source_target_pairs={{0,2},{1,3},{2,0},{3,1},{4,6},{5,7},{6,4},{7,5},{8,10},{9,11},{10,... | collective-permute-start | bytes 3145736 | tf_op jit(solution)/shard_map/ppermute | solution.py:37
  40.2 15.3 %collective-permute-start.8 = (bf16[256,1024]{1,0:T(8,128)(2,1)}, bf16[256,1024]{1,0:T(8,128)(2,1)}, u32[]{:S(2)}, u32[]{:S(2)}) collective-permute-start(bf16[256,1024]{1,0:T(8,128)(2,1)} %slice.31), channel_id=1, source_target_pairs={{0,12},{1,13},{2,14},{3,15},{4,0},{5,1},{6,2},{7,3},{8,4},{9,5},{1... | collective-permute-start | bytes 1572872 | tf_op jit(solution)/shard_map/ppermute | solution.py:33
  44.0 13.6 %copy-start.22 = (bf16[256,1024]{1,0:T(8,128)(2,1)S(1)}, bf16[256,1024]{1,0:T(8,128)(2,1)}, u32[]{:S(2)}) copy-start(bf16[256,1024]{1,0:T(8,128)(2,1)} %copy-done.21) | copy-start | bytes 1572868
  44.0 24.2 %collective-permute-start.12 = (bf16[256,1024]{1,0:T(8,128)(2,1)}, bf16[256,1024]{1,0:T(8,128)(2,1)S(1)}, u32[]{:S(2)}, u32[]{:S(2)}) collective-permute-start(bf16[256,1024]{1,0:T(8,128)(2,1)} %collective-permute-done.2.refs_5_.refs_3_), channel_id=1, source_target_pairs={{0,4},{1,5},{2,6},{3,7},{4,8},{5,9},{6,10},{7,11},{8,12},{9,13},{1... | collective-permute-start | bytes 1572872 | tf_op jit(solution)/shard_map/ppermute | solution.py:29
  44.0 21.5 %collective-permute-start.3 = (bf16[256,1024]{1,0:T(8,128)(2,1)}, bf16[256,1024]{1,0:T(8,128)(2,1)}, u32[]{:S(2)}, u32[]{:S(2)}) collective-permute-start(bf16[256,1024]{1,0:T(8,128)(2,1)} %collective-permute-done.2.refs_5_.refs_3_), channel_id=1, source_target_pairs={{0,12},{1,13},{2,14},{3,15},{4,0},{5,1},{6,2},{7,3},{8,4},{9,5},{1... | collective-permute-start | bytes 1572872 | tf_op jit(solution)/shard_map/ppermute | solution.py:33
  55.4 16.2 %collective-permute-start.11 = (bf16[256,1024]{1,0:T(8,128)(2,1)}, bf16[256,1024]{1,0:T(8,128)(2,1)S(1)}, u32[]{:S(2)}, u32[]{:S(2)}) collective-permute-start(bf16[256,1024]{1,0:T(8,128)(2,1)} %get-tuple-element.94), channel_id=1, source_target_pairs={{0,4},{1,5},{2,6},{3,7},{4,8},{5,9},{6,10},{7,11},{8,12},{9,13},{1... | collective-permute-start | bytes 1572872 | tf_op jit(solution)/shard_map/ppermute | solution.py:29
  55.5 30.4 %collective-permute-start.15 = (bf16[512,1024]{1,0:T(8,128)(2,1)}, bf16[512,1024]{1,0:T(8,128)(2,1)}, u32[]{:S(2)}, u32[]{:S(2)}) collective-permute-start(bf16[512,1024]{1,0:T(8,128)(2,1)} %constant_dynamic-slice_fusion), channel_id=1, source_target_pairs={{0,1},{1,0},{2,3},{3,2},{4,5},{5,4},{6,7},{7,6},{8,9},{9,8},{10,11... | collective-permute-start | bytes 3145736 | tf_op jit(solution)/shard_map/ppermute | solution.py:41
  63.0 20.2 %collective-permute-start.14 = (bf16[256,1024]{1,0:T(8,128)(2,1)S(1)}, bf16[256,1024]{1,0:T(8,128)(2,1)}, u32[]{:S(2)}, u32[]{:S(2)}) collective-permute-start(bf16[256,1024]{1,0:T(8,128)(2,1)S(1)} %fusion), channel_id=1, source_target_pairs={{0,96},{16,112},{32,64},{48,80},{64,32},{80,48},{96,0},{112,16},{1... | collective-permute-start | bytes 1572872 | tf_op jit(solution)/shard_map/ppermute | solution.py:54
  65.5 20.3 %collective-permute-start.10 = (bf16[256,1024]{1,0:T(8,128)(2,1)}, bf16[256,1024]{1,0:T(8,128)(2,1)S(1)}, u32[]{:S(2)}, u32[]{:S(2)}) collective-permute-start(bf16[256,1024]{1,0:T(8,128)(2,1)} %collective-permute-done.8.refs_3_.refs_6_), channel_id=1, source_target_pairs={{0,2},{1,3},{2,0},{3,1},{4,6},{5,7},{6,4},{7,5},{8,10},{9,11},{10,... | collective-permute-start | bytes 1572872 | tf_op jit(solution)/shard_map/ppermute | solution.py:37
  68.2 0.8 copy-start.8
  69.0 16.8 %collective-permute-start.7 = (bf16[256,1024]{1,0:T(8,128)(2,1)}, bf16[256,1024]{1,0:T(8,128)(2,1)S(1)}, u32[]{:S(2)}, u32[]{:S(2)}) collective-permute-start(bf16[256,1024]{1,0:T(8,128)(2,1)} %collective-permute-done.3.refs_6_.refs_9_), channel_id=1, source_target_pairs={{0,12},{1,13},{2,14},{3,15},{4,0},{5,1},{6,2},{7,3},{8,4},{9,5},{1... | collective-permute-start | bytes 1572872 | tf_op jit(solution)/shard_map/ppermute | solution.py:33
  71.7 1.0 copy-start.9
  72.7 10.5 %copy-start.24 = (bf16[256,1024]{1,0:T(8,128)(2,1)S(1)}, bf16[256,1024]{1,0:T(8,128)(2,1)}, u32[]{:S(2)}) copy-start(bf16[256,1024]{1,0:T(8,128)(2,1)} %copy-done.23) | copy-start | bytes 1572868
  81.9 1.3 copy-start.16
  84.3 11.4 %collective-permute-start.16 = (bf16[256,512]{1,0:T(8,128)(2,1)S(1)}, bf16[256,512]{1,0:T(8,128)(2,1)S(1)}, u32[]{:S(2)}, u32[]{:S(2)}) collective-permute-start(bf16[256,512]{1,0:T(8,128)(2,1)S(1)} %fusion.5), channel_id=1, source_target_pairs={{0,16},{16,0},{32,48},{48,32},{64,80},{80,64},{96,112},{112,96},{1... | collective-permute-start | bytes 786440 | tf_op jit(solution)/shard_map/ppermute | solution.py:45
  85.8 0.8 copy-start.11
  85.9 1.0 copy-start.13
  86.8 8.8 %copy-start.26 = (f32[256,512]{1,0:T(8,128)S(1)}, f32[256,512]{1,0:T(8,128)}, u32[]{:S(2)}) copy-start(f32[256,512]{1,0:T(8,128)} %param.11) | copy-start | bytes 1572868
  95.6 3.4 %copy-start.3 = (bf16[512,1024]{1,0:T(8,128)(2,1)S(1)}, bf16[512,1024]{1,0:T(8,128)(2,1)}, u32[]{:S(2)}) copy-start(bf16[512,1024]{1,0:T(8,128)(2,1)} %get-tuple-element.82.so_ref.s_ref) | copy-start | bytes 3145732
  95.6 3.4 %copy-start.5 = (bf16[512,1024]{1,0:T(8,128)(2,1)S(1)}, bf16[512,1024]{1,0:T(8,128)(2,1)}, u32[]{:S(2)}) copy-start(bf16[512,1024]{1,0:T(8,128)(2,1)} %get-tuple-element.78.sp_ref.s_ref) | copy-start | bytes 3145732
  98.2 9.4 %collective-permute-start.17 = (bf16[256,512]{1,0:T(8,128)(2,1)S(1)}, bf16[256,512]{1,0:T(8,128)(2,1)S(1)}, u32[]{:S(2)}, u32[]{:S(2)}) collective-permute-start(bf16[256,512]{1,0:T(8,128)(2,1)S(1)} %get-tuple-element.89), channel_id=1, source_target_pairs={{0,16},{16,0},{32,48},{48,32},{64,80},{80,64},{96,112},{112,96},{1... | collective-permute-start | bytes 786440 | tf_op jit(solution)/shard_map/ppermute | solution.py:45
  105.0 22.9 %collective-permute-start.20 = (bf16[512,1024]{1,0:T(8,128)(2,1)}, bf16[512,1024]{1,0:T(8,128)(2,1)}, u32[]{:S(2)}, u32[]{:S(2)}) collective-permute-start(bf16[512,1024]{1,0:T(8,128)(2,1)} %get-tuple-element.70), channel_id=1, source_target_pairs={{0,4},{1,5},{2,6},{3,7},{4,8},{5,9},{6,10},{7,11},{8,12},{9,13},{1... | collective-permute-start | bytes 3145736 | tf_op jit(solution)/shard_map/ppermute | solution.py:29
  105.0 25.5 %collective-permute-start.18 = (bf16[512,1024]{1,0:T(8,128)(2,1)}, bf16[512,1024]{1,0:T(8,128)(2,1)}, u32[]{:S(2)}, u32[]{:S(2)}) collective-permute-start(bf16[512,1024]{1,0:T(8,128)(2,1)} %get-tuple-element.75), channel_id=1, source_target_pairs={{0,12},{1,13},{2,14},{3,15},{4,0},{5,1},{6,2},{7,3},{8,4},{9,5},{1... | collective-permute-start | bytes 3145736 | tf_op jit(solution)/shard_map/ppermute | solution.py:33
  107.8 13.3 %collective-permute-start.21 = (bf16[256,1024]{1,0:T(8,128)(2,1)S(1)}, bf16[256,1024]{1,0:T(8,128)(2,1)S(1)}, u32[]{:S(2)}, u32[]{:S(2)}) collective-permute-start(bf16[256,1024]{1,0:T(8,128)(2,1)S(1)} %maximum_select_fusion.2), channel_id=1, source_target_pairs={{0,96},{16,112},{32,64},{48,80},{64,32},{80,48},{96,0},{112,16},{1... | collective-permute-start | bytes 1572872 | tf_op jit(solution)/shard_map/ppermute | solution.py:54
  121.1 9.4 %copy-start.17 = (bf16[512,1024]{1,0:T(8,128)(2,1)}, bf16[512,1024]{1,0:T(8,128)(2,1)S(1)}, u32[]{:S(2)}) copy-start(bf16[512,1024]{1,0:T(8,128)(2,1)S(1)} %get-tuple-element.73) | copy-start | bytes 3145732
  121.1 9.4 %copy-start.19 = (bf16[512,1024]{1,0:T(8,128)(2,1)}, bf16[512,1024]{1,0:T(8,128)(2,1)S(1)}, u32[]{:S(2)}) copy-start(bf16[512,1024]{1,0:T(8,128)(2,1)S(1)} %get-tuple-element.80) | copy-start | bytes 3145732
  122.3 11.0 %copy-start.6 = (bf16[512,1024]{1,0:T(8,128)(2,1)S(1)}, bf16[512,1024]{1,0:T(8,128)(2,1)}, u32[]{:S(2)}) copy-start(bf16[512,1024]{1,0:T(8,128)(2,1)} %get-tuple-element.78.sp_ref.s_ref) | copy-start | bytes 3145732
  122.3 11.0 %copy-start.10 = (bf16[256,1024]{1,0:T(8,128)(2,1)S(1)}, bf16[256,1024]{1,0:T(8,128)(2,1)}, u32[]{:S(2)}) copy-start(bf16[256,1024]{1,0:T(8,128)(2,1)} %copy-done.8) | copy-start | bytes 1572868
  122.3 11.0 %copy-start.12 = (bf16[256,1024]{1,0:T(8,128)(2,1)S(1)}, bf16[256,1024]{1,0:T(8,128)(2,1)}, u32[]{:S(2)}) copy-start(bf16[256,1024]{1,0:T(8,128)(2,1)} %copy-done.11) | copy-start | bytes 1572868
  122.3 11.0 %copy-start.14 = (bf16[256,1024]{1,0:T(8,128)(2,1)S(1)}, bf16[256,1024]{1,0:T(8,128)(2,1)}, u32[]{:S(2)}) copy-start(bf16[256,1024]{1,0:T(8,128)(2,1)} %copy-done.13) | copy-start | bytes 1572868
  122.3 20.9 %collective-permute-start.23 = (bf16[2,256,1024]{2,1,0:T(8,128)(2,1)}, bf16[2,256,1024]{2,1,0:T(8,128)(2,1)}, u32[]{:S(2)}, u32[]{:S(2)}) collective-permute-start(bf16[2,256,1024]{2,1,0:T(8,128)(2,1)} %pad_maximum_fusion.1.own_ref), channel_id=1, source_target_pairs={{0,32},{16,48},{32,0},{48,16},{64,96},{80,112},{96,64},{112,80},{1... | collective-permute-start | bytes 3145736 | tf_op jit(solution)/shard_map/ppermute | solution.py:49
  130.5 22.0 %collective-permute-start.22 = (bf16[512,1024]{1,0:T(8,128)(2,1)}, bf16[512,1024]{1,0:T(8,128)(2,1)}, u32[]{:S(2)}, u32[]{:S(2)}) collective-permute-start(bf16[512,1024]{1,0:T(8,128)(2,1)} %add_convert_fusion.2), channel_id=1, source_target_pairs={{0,4},{1,5},{2,6},{3,7},{4,8},{5,9},{6,10},{7,11},{8,12},{9,13},{1... | collective-permute-start | bytes 3145736 | tf_op jit(solution)/shard_map/ppermute | solution.py:29
  130.5 22.0 %collective-permute-start.19 = (bf16[512,1024]{1,0:T(8,128)(2,1)}, bf16[512,1024]{1,0:T(8,128)(2,1)}, u32[]{:S(2)}, u32[]{:S(2)}) collective-permute-start(bf16[512,1024]{1,0:T(8,128)(2,1)} %get-tuple-element.76), channel_id=1, source_target_pairs={{0,12},{1,13},{2,14},{3,15},{4,0},{5,1},{6,2},{7,3},{8,4},{9,5},{1... | collective-permute-start | bytes 3145736 | tf_op jit(solution)/shard_map/ppermute | solution.py:33
  133.3 19.2 %copy-start.18 = (bf16[512,1024]{1,0:T(8,128)(2,1)S(1)}, bf16[512,1024]{1,0:T(8,128)(2,1)}, u32[]{:S(2)}) copy-start(bf16[512,1024]{1,0:T(8,128)(2,1)} %copy-done.17) | copy-start | bytes 3145732
  143.0 12.1 %copy-start.20 = (bf16[512,1024]{1,0:T(8,128)(2,1)S(1)}, bf16[512,1024]{1,0:T(8,128)(2,1)}, u32[]{:S(2)}) copy-start(bf16[512,1024]{1,0:T(8,128)(2,1)} %copy-done.19) | copy-start | bytes 3145732
  155.1 15.3 %copy-start.4 = (bf16[512,1024]{1,0:T(8,128)(2,1)S(1)}, bf16[512,1024]{1,0:T(8,128)(2,1)}, u32[]{:S(2)}) copy-start(bf16[512,1024]{1,0:T(8,128)(2,1)} %get-tuple-element.82.so_ref.s_ref) | copy-start | bytes 3145732
  158.1 12.3 %collective-permute-start.24 = (bf16[512,4096]{1,0:T(8,128)(2,1)}, bf16[512,4096]{1,0:T(8,128)(2,1)}, u32[]{:S(2)}, u32[]{:S(2)}) collective-permute-start(bf16[512,4096]{1,0:T(8,128)(2,1)} %igrad.2), channel_id=1, source_target_pairs={{0,1},{1,0},{2,3},{3,2},{4,5},{5,4},{6,7},{7,6},{8,9},{9,8},{10,11... | collective-permute-start | bytes 12582920 | tf_op jit(solution)/shard_map/ppermute | solution.py:41
  163.3 26.3 %collective-permute-start.26 = (bf16[512,1024]{1,0:T(8,128)(2,1)}, bf16[512,1024]{1,0:T(8,128)(2,1)}, u32[]{:S(2)}, u32[]{:S(2)}) collective-permute-start(bf16[512,1024]{1,0:T(8,128)(2,1)} %get-tuple-element.88), channel_id=1, source_target_pairs={{0,4},{1,5},{2,6},{3,7},{4,8},{5,9},{6,10},{7,11},{8,12},{9,13},{1... | collective-permute-start | bytes 3145736 | tf_op jit(solution)/shard_map/ppermute | solution.py:29
  163.3 26.6 %collective-permute-start.27 = (bf16[512,1024]{1,0:T(8,128)(2,1)}, bf16[512,1024]{1,0:T(8,128)(2,1)}, u32[]{:S(2)}, u32[]{:S(2)}) collective-permute-start(bf16[512,1024]{1,0:T(8,128)(2,1)} %add_convert_fusion), channel_id=1, source_target_pairs={{0,2},{1,3},{2,0},{3,1},{4,6},{5,7},{6,4},{7,5},{8,10},{9,11},{10,... | collective-permute-start | bytes 3145736 | tf_op jit(solution)/shard_map/ppermute | solution.py:37
  164.1 25.8 %collective-permute-start.25 = (bf16[512,1024]{1,0:T(8,128)(2,1)}, bf16[512,1024]{1,0:T(8,128)(2,1)}, u32[]{:S(2)}, u32[]{:S(2)}) collective-permute-start(bf16[512,1024]{1,0:T(8,128)(2,1)} %add_convert_fusion.1), channel_id=1, source_target_pairs={{0,12},{1,13},{2,14},{3,15},{4,0},{5,1},{6,2},{7,3},{8,4},{9,5},{1... | collective-permute-start | bytes 3145736 | tf_op jit(solution)/shard_map/ppermute | solution.py:33
  180.9 9.0 %copy-start.25 = (bf16[512,1024]{1,0:T(8,128)(2,1)S(1)}, bf16[512,1024]{1,0:T(8,128)(2,1)}, u32[]{:S(2)}) copy-start(bf16[512,1024]{1,0:T(8,128)(2,1)} %get-tuple-element.86) | copy-start | bytes 3145732
  192.6 3.2 %collective-permute-start.28 = (f32[256,1024]{1,0:T(8,128)S(1)}, f32[256,1024]{1,0:T(8,128)S(1)}, u32[]{:S(2)}, u32[]{:S(2)}) collective-permute-start(f32[256,1024]{1,0:T(8,128)S(1)} %get-tuple-element.93), channel_id=1, source_target_pairs={{0,1},{1,0},{2,3},{3,2},{4,5},{5,4},{6,7},{7,6},{8,9},{9,8},{10,11... | collective-permute-start | bytes 3145736 | tf_op jit(solution)/shard_map/ppermute | solution.py:41

commit v3 on v2

v3 whole, which is shorter than its diff:
```python
import functools

import jax
import jax.numpy as jnp
from jax import lax
from jax.experimental import pallas as pl
from jax.experimental.pallas import tpu as pltpu
from jax.sharding import PartitionSpec as P

F32 = jnp.float32
BF16 = jnp.bfloat16
MIB = 1 << 20
COST = 0.3

NZ, NY, NC, NX, NL = 4, 2, 2, 4, 2
DIRS = [(dz, dy) for dz in range(NZ) for dy in range(NY)]


def shard_perm(dz, dy, dc):
    perm = []
    for i in range(NZ * NY * NC):
        z, y, c = i // (NY * NC), (i // NC) % NY, i % NC
        j = ((z + dz) % NZ) * NY * NC + ((y + dy) % NY) * NC + (c + dc) % NC
        perm.append((i, j))
    return perm


def to_zp(a):
    return lax.ppermute(a, "shard", shard_perm(1, 0, 0))


def to_zm(a):
    return lax.ppermute(a, "shard", shard_perm(-1, 0, 0))


def to_y(a):
    return lax.ppermute(a, "shard", shard_perm(0, 1, 0))


def to_core(a):
    return lax.ppermute(a, "shard", shard_perm(0, 0, 1))


def to_l(a):
    return lax.ppermute(a, "replica", [(i, i ^ 1) for i in range(NX * NL)])


def to_x(a, dx):
    perm = [(i, (i // NL + dx) % NX * NL + i % NL) for i in range(NX * NL)]
    return lax.ppermute(a, "replica", perm)


def to_l(a):
    return lax.ppermute(a, "replica", [(i, i ^ 1) for i in range(NX * NL)])


def to_near(a):
    return lax.ppermute(a, "replica", [(i, i ^ NL) for i in range(NX * NL)])


def to_far(a):
    perm = [(i, (NX - 1 - i // NL) * NL + i % NL) for i in range(NX * NL)]
    return lax.ppermute(a, "replica", perm)


def add(*terms):
    total = terms[0].astype(F32)
    for term in terms[1:]:
        total = total + term.astype(F32)
    return total


EARLY = [(3, 1), (1, 1), (2, 1)]
LATE = [(2, 0), (0, 1)]
LAST = [(3, 0), (1, 0), (0, 0)]
AT_EARLY = len(DIRS)
AT_LATE = AT_EARLY + len(EARLY)
AT_LAST = AT_LATE + len(LATE)
AT_CORE = AT_LAST + len(LAST)
AT_OTHER = AT_CORE + 1
AT_X = AT_CORE + 2


def place_of(where, s, depth, rows):
    base = s[where[0]]
    return base if depth == rows else base * (rows // depth) + where[1]


def whole(shape):
    return pl.BlockSpec(shape, lambda i, *_: (0,) * len(shape))


def cost(flops, nbytes, trans=0):
    return pl.CostEstimate(
        flops=int(COST * flops), bytes_accessed=int(COST * nbytes), transcendentals=int(COST * trans)
    )


def params(mib):
    return pltpu.CompilerParams(vmem_limit_bytes=mib * MIB)


def decode_kernel(pos_ref, outer_ref, inner_ref, *out_refs):
    step = pl.program_id(0)
    width = outer_ref.shape[1]
    decoded = []
    for g in range(width // 128):
        cols = slice(g * 128, (g + 1) * 128)
        delta = outer_ref[:, cols] - inner_ref[0, :, cols]
        top = jnp.max(jnp.abs(delta), axis=1, keepdims=True) + 1e-06
        scale = top.astype(BF16).astype(F32)
        code = (delta / scale).astype(BF16).astype(F32)
        decoded.append((code * scale).astype(BF16))
    decoded = jnp.concatenate(decoded, axis=1)
    for k, out_ref in enumerate(out_refs):
        @pl.when(step == k)
        def _(out_ref=out_ref):
            out_ref[...] = decoded


def decode(pos, outer, inner):
    rows, cols = outer.shape
    width = cols // NX
    return pl.pallas_call(
        decode_kernel,
        grid_spec=pltpu.PrefetchScalarGridSpec(
            num_scalar_prefetch=1,
            grid=(NX,),
            in_specs=[
                pl.BlockSpec((rows, width), lambda i, p: (0, lax.rem(p[AT_X] + i, NX))),
                pl.BlockSpec((1, rows, width), lambda i, p: (0, 0, lax.rem(p[AT_X] + i, NX))),
            ],
            out_specs=[whole((rows, width))] * NX,
        ),
        out_shape=[jax.ShapeDtypeStruct((rows, width), BF16)] * NX,
        compiler_params=params(60),
        cost_estimate=cost(10 * rows * cols, 10 * rows * cols),
        name="decode",
    )(pos, outer, inner)


def sum_kernel(n, factor, blk_ref, *refs):
    total = refs[0][...].astype(F32)
    for ref in refs[1:n]:
        total = total + ref[...].astype(F32)
    if factor is not None:
        total = total * factor
    refs[n][...] = total.astype(refs[n].dtype)


def sum_of(pos, terms, rows, dtype, at=None, factor=None):
    width = terms[0].shape[1]
    n = len(terms)
    tile = rows // 2
    first = (lambda s: 0) if at is None else (lambda s: 2 * s[at])
    return pl.pallas_call(
        functools.partial(sum_kernel, n, factor),
        grid_spec=pltpu.PrefetchScalarGridSpec(
            num_scalar_prefetch=1,
            grid=(2,),
            in_specs=[pl.BlockSpec((tile, width), lambda i, s: (first(s) + i, 0))] * n,
            out_specs=pl.BlockSpec((tile, width), lambda i, s: (i, 0)),
        ),
        out_shape=jax.ShapeDtypeStruct((rows, width), dtype),
        compiler_params=params(60),
        cost_estimate=cost(n * rows * width, 2 * (n + 1) * rows * width),
        name="sum",
    )(pos, *terms)


def fold_kernel(up_ref, a_ref, low_ref, b_ref, up_out, low_out):
    up_out[...] = (up_ref[...].astype(F32) + a_ref[...].astype(F32)).astype(BF16)
    low_out[...] = (low_ref[...].astype(F32) + b_ref[...].astype(F32)).astype(BF16)


def fold(up, a, low, b):
    rows, width = a.shape
    block = (rows, width // 2)
    upper, lower = pl.BlockSpec(block, lambda i: (0, i)), pl.BlockSpec(block, lambda i: (1, i))
    return pl.pallas_call(
        fold_kernel,
        grid=(2,),
        in_specs=[upper, upper, lower, upper],
        out_specs=[upper, lower],
        out_shape=[jax.ShapeDtypeStruct(up.shape, BF16)] * 2,
        input_output_aliases={0: 0, 2: 1},
        compiler_params=params(60),
        cost_estimate=cost(2 * rows * width, 12 * rows * width),
        name="fold",
    )(up, a, low, b)


def halves_kernel(a_ref, b_ref, up_ref, low_ref):
    total = (a_ref[...].astype(F32) + b_ref[...].astype(F32)).astype(BF16)
    step = pl.program_id(0)

    @pl.when(step == 0)
    def _():
        up_ref[...] = total

    @pl.when(step == 1)
    def _():
        low_ref[...] = total


def halves_of(a, b):
    rows, width = a.shape[0] // 2, a.shape[1]
    return pl.pallas_call(
        halves_kernel,
        grid=(2,),
        in_specs=[pl.BlockSpec((rows, width), lambda i: (i, 0))] * 2,
        out_specs=[whole((rows, width))] * 2,
        out_shape=[jax.ShapeDtypeStruct((rows, width), BF16)] * 2,
        compiler_params=params(60),
        cost_estimate=cost(2 * rows * width, 12 * rows * width),
        name="halves",
    )(a, b)


def pre_kernel(factor, n, has_sum, last, off_ref, *refs):
    refs = list(refs)
    pieces = [refs.pop(0) for _ in range(n)]
    x_refs = [[refs.pop(0) for _ in range(n)] for _ in range(2)]
    sums = [refs.pop(0) for _ in range(2)] if has_sum else [None, None]
    cots = [refs.pop(0) for _ in range(2)] if last else [None, None]
    for xs, sum_ref, cot_ref, out_ref in zip(x_refs, sums, cots, refs):
        pre = sum_ref[...] if has_sum else None
        for x_ref, piece in zip(xs, pieces):
            term = jnp.dot(x_ref[...], piece[...], preferred_element_type=F32)
            pre = term if pre is None else pre + term
        if last:
            pre = pre * factor
            sig = 0.5 + 0.5 * jnp.tanh(0.5 * pre)
            pre = (cot_ref[...].astype(F32) * sig * (1.0 + pre * (1.0 - sig))).astype(BF16)
        out_ref[...] = pre


def pre_of(factor, pos, x_pair, pieces, offs, sums=None, cots=None):
    toks, feats = x_pair[0].shape
    width = pieces[0].shape[1]
    depth = sum(p.shape[0] for p in pieces)
    tile = toks // 2
    n = len(pieces)
    rows = feats // (NZ * NY)
    row = pl.BlockSpec((tile, width), lambda i, s: (i, 0))
    x_specs = [
        pl.BlockSpec(
            (tile, p.shape[0]), lambda i, s, p=p, w=w: (i, place_of(w, s, p.shape[0], rows))
        )
        for p, w in zip(pieces, offs)
    ]
    in_specs = [whole(p.shape) for p in pieces] + x_specs + x_specs
    args = list(pieces) + [x_pair[0]] * n + [x_pair[1]] * n
    if sums is not None:
        in_specs += [row, row]
        args += list(sums)
    if cots is not None:
        in_specs += [pl.BlockSpec((tile, width), lambda i, s: (i, s[AT_CORE]))] * 2
        args += list(cots)
    last = cots is not None
    return pl.pallas_call(
        functools.partial(pre_kernel, factor, n, sums is not None, last),
        grid_spec=pltpu.PrefetchScalarGridSpec(
            num_scalar_prefetch=1,
            grid=(toks // tile,),
            in_specs=in_specs,
            out_specs=[row, row],
        ),
        out_shape=[jax.ShapeDtypeStruct((toks, width), BF16 if last else F32)] * 2,
        compiler_params=params(60),
        cost_estimate=cost(4 * toks * depth * width, 4 * toks * depth + 2 * depth * width + 8 * toks * width),
        name="slope" if last else "pre",
    )(pos, *args)


def wgrad_kernel(halves, blk_ref, xo_ref, xp_ref, so_ref, sp_ref, *out_refs):
    step = pl.program_id(0)
    dims = (((0,), (0,)), ((), ()))
    term = lax.dot_general(xo_ref[...], so_ref[...], dims, preferred_element_type=F32)
    term = term + lax.dot_general(xp_ref[...], sp_ref[...], dims, preferred_element_type=F32)
    term = term.astype(BF16)
    out_refs = list(out_refs)
    for k, halved in enumerate(halves):
        mine = [out_refs.pop(0) for _ in range(2 if halved else 1)]

        @pl.when(step == k)
        def _(mine=mine):
            at = 0
            for ref in mine:
                ref[...] = term[at:at + ref.shape[0]]
                at += ref.shape[0]


def wgrad_of(pos, at, halves, x_pair, slopes):
    toks, feats = x_pair[0].shape
    width = slopes[0].shape[1]
    n = len(halves)
    rows = feats // (NZ * NY)
    shapes = []
    for halved in halves:
        shapes += [(rows // 2, width)] * 2 if halved else [(rows, width)]
    outs = pl.pallas_call(
        functools.partial(wgrad_kernel, halves),
        grid_spec=pltpu.PrefetchScalarGridSpec(
            num_scalar_prefetch=1,
            grid=(n,),
            in_specs=[pl.BlockSpec((toks, rows), lambda i, s: (0, s[at + i]))] * 2
            + [whole((toks, width))] * 2,
            out_specs=[whole(s) for s in shapes],
        ),
        out_shape=[jax.ShapeDtypeStruct(s, BF16) for s in shapes],
        compiler_params=params(60),
        cost_estimate=cost(4 * toks * n * rows * width, 4 * toks * n * rows + 2 * n * rows * width),
        name="wgrad",
    )(pos, *x_pair, *slopes)
    outs = list(outs)
    return [[outs.pop(0) for _ in range(2)] if halved else outs.pop(0) for halved in halves]


def late_kernel(n, offs, rows, s_ref, xo_ref, xp_ref, so_ref, sp_ref, *refs):
    step = pl.program_id(0)
    m = len(offs)
    pieces, outs, part_ref = refs[:m], refs[m:m + n], refs[m + n]
    tile = part_ref.shape[0]

    @pl.when(step < n)
    def _():
        dims = (((0,), (0,)), ((), ()))
        term = lax.dot_general(xo_ref[...], so_ref[...], dims, preferred_element_type=F32)
        term = term + lax.dot_general(xp_ref[...], sp_ref[...], dims, preferred_element_type=F32)
        term = term.astype(BF16)
        for k, out_ref in enumerate(outs):
            @pl.when(step == k)
            def _(out_ref=out_ref):
                out_ref[...] = term

    @pl.when(step >= n)
    def _():
        dims = (((1,), (1,)), ((), ()))
        slope = sp_ref[pl.ds(pl.multiple_of((step - n) * tile, tile), tile), :]
        for where, piece in zip(offs, pieces):
            depth = piece.shape[0]
            cols = pl.ds(pl.multiple_of(place_of(where, s_ref, depth, rows) * depth, 256), depth)
            part_ref[:, cols] = lax.dot_general(
                slope, piece[...], dims, preferred_element_type=F32
            ).astype(BF16)


def late_of(pos, x_pair, slopes, offs, pieces):
    toks, feats = x_pair[0].shape
    width = slopes[0].shape[1]
    n = len(LATE)
    rows = feats // (NZ * NY)
    tile = toks // 2
    outs = pl.pallas_call(
        functools.partial(late_kernel, n, offs, rows),
        grid_spec=pltpu.PrefetchScalarGridSpec(
            num_scalar_prefetch=1,
            grid=(n + toks // tile,),
            in_specs=[pl.BlockSpec((toks, rows), lambda i, s: (0, s[AT_LATE + jnp.minimum(i, n - 1)]))] * 2
            + [whole((toks, width))] * 2
            + [whole(p.shape) for p in pieces],
            out_specs=[whole((rows, width))] * n
            + [pl.BlockSpec((tile, feats), lambda i, s: (jnp.maximum(i - n, 0), 0))],
        ),
        out_shape=[jax.ShapeDtypeStruct((rows, width), BF16)] * n
        + [jax.ShapeDtypeStruct((toks, feats), BF16)],
        compiler_params=params(60),
        cost_estimate=cost(
            2 * toks * (2 * n * rows + feats) * width, 4 * toks * feats + 4 * feats * width
        ),
        name="late",
    )(pos, *x_pair, *slopes, *pieces)
    return outs


def igrad_kernel(factor, offs, rows, has_term, pos_ref, s_ref, *refs):
    n = len(offs)
    out_ref = refs[-1]
    dims = (((1,), (1,)), ((), ()))
    for where, piece in zip(offs, refs):
        depth = piece.shape[0]
        cols = pl.ds(pl.multiple_of(place_of(where, pos_ref, depth, rows) * depth, 256), depth)
        total = lax.dot_general(s_ref[...], piece[...], dims, preferred_element_type=F32)
        if has_term:
            total = (total + refs[n][:, cols].astype(F32)) * factor
        out_ref[:, cols] = total.astype(BF16)


def igrad_of(factor, pos, offs, slope, pieces, term=None):
    toks, width = slope.shape
    feats = sum(p.shape[0] for p in pieces)
    tile = toks // 2
    extra = [] if term is None else [term]
    return pl.pallas_call(
        functools.partial(
            igrad_kernel, factor, offs, feats // (NZ * NY), term is not None
        ),
        grid_spec=pltpu.PrefetchScalarGridSpec(
            num_scalar_prefetch=1,
            grid=(toks // tile,),
            in_specs=[pl.BlockSpec((tile, width), lambda i, s: (i, 0))]
            + [whole(p.shape) for p in pieces]
            + [pl.BlockSpec((tile, feats), lambda i, s: (i, 0)) for _ in extra],
            out_specs=pl.BlockSpec((tile, feats), lambda i, s: (i, 0)),
        ),
        out_shape=jax.ShapeDtypeStruct((toks, feats), BF16),
        compiler_params=params(60),
        cost_estimate=cost(2 * toks * feats * width, 2 * toks * feats + 2 * feats * width),
        name="igrad",
    )(pos, slope, *pieces, *extra)


def by_core(core, mine, other, axis):
    return jnp.where(
        core == 0,
        jnp.concatenate([mine, other], axis=axis),
        jnp.concatenate([other, mine], axis=axis),
    )


def place_kernel(pos_ref, *refs):
    for k, part_ref in enumerate(refs[:-1]):
        @pl.when(pl.program_id(0) == k)
        def _(part_ref=part_ref):
            refs[-1][...] = part_ref[...]


def side_by_side(pos, parts):
    rows, width = parts[0].shape
    n = len(parts)
    return pl.pallas_call(
        place_kernel,
        grid_spec=pltpu.PrefetchScalarGridSpec(
            num_scalar_prefetch=1,
            grid=(n,),
            in_specs=[whole((rows, width))] * n,
            out_specs=pl.BlockSpec((rows, width), lambda i, p: (0, lax.rem(p[AT_X] + n - i, n))),
        ),
        out_shape=jax.ShapeDtypeStruct((rows, n * width), parts[0].dtype),
        compiler_params=params(60),
        cost_estimate=cost(0, 4 * n * rows * width),
        name="place",
    )(pos, *parts)


def hold(a, *deps):
    return lax.optimization_barrier((a,) + deps)[0]


def shards(tokens, cotangent, next_weight, inner_weight, outer_weight, momentum):
    toks, feats = tokens.shape
    factor = feats ** (-0.5)
    me = lax.axis_index("shard")
    z, y, core = me // (NY * NC), (me // NC) % NY, me % NC
    replica = lax.axis_index("replica")
    low = replica % NL

    blk = {(dz, dy): ((z + dz) % NZ) * NY + (y + dy) % NY for dz, dy in DIRS}
    rows = feats // (NZ * NY)
    half = rows // 2
    cols = next_weight.shape[2] // NC

    def offs(*dirs):
        return [(DIRS.index(d[:2]), d[2] if len(d) == 3 else 0) for d in dirs]

    pos = jnp.stack(
        [blk[d] for d in DIRS + EARLY + LATE + LAST] + [core, 1 - core, replica // NL]
    ).astype(jnp.int32)

    keep = lax.dynamic_slice_in_dim(next_weight[0], core * cols, cols, 1)
    give = lax.dynamic_slice_in_dim(next_weight[0], (1 - core) * cols, cols, 1)
    w00 = by_core(core, keep, to_core(give), 0)

    w30, w10, w01 = to_zp(w00), to_zm(w00), to_y(w00)
    x_pair = (tokens, to_core(hold(tokens, w00)))
    cots = (cotangent, to_core(hold(cotangent, w00)))
    dec = decode(pos, hold(outer_weight, w00), inner_weight)
    x1, x2, x3 = [to_x(hold(dec[dx], x_pair[1], cots[1]), dx) for dx in (1, 2, 3)]

    a20 = to_zp(hold(w30, w01, dec[0], x1)[:half])
    b20 = to_zm(hold(w10, w01, dec[0], x1)[half:])
    first, first_offs = [w00, w30, w10, w01], offs((0, 0), (3, 0), (1, 0), (0, 1))
    sums = pre_of(factor, pos, x_pair, first, first_offs)

    a21, b21 = to_y(hold(a20, sums[0])), to_y(hold(b20, sums[0]))
    w31, w11 = to_zp(hold(w01, sums[0], a20)), to_zm(hold(w01, sums[0], b20))
    share = momentum.shape[1]

    def share_of(a, which):
        return lax.dynamic_slice_in_dim(a, which * share, share, 1)

    second, second_offs = [a20, b20], offs((2, 0), (2, 0, 1))
    sums = pre_of(factor, pos, x_pair, second, second_offs, sums)
    x_terms = [hold(dec[0], sums[0]), x1, x2, x3]
    other = add(*[share_of(a, 1 - low) for a in x_terms]).astype(BF16)
    low_got = to_l(hold(other, a21, b21, w31, w11))
    third, third_offs = [w31, w11, a21, b21], offs((3, 1), (1, 1), (2, 1), (2, 1, 1))
    slopes = pre_of(factor, pos, x_pair, third, third_offs, sums, cots)
    mine = [share_of(a, low) for a in x_terms]
    average = add(*mine, hold(low_got, slopes[0])) / (NX * NL)
    outer_share = lax.dynamic_slice_in_dim(outer_weight, replica * share, share, 1)
    new_momentum = 0.9 * momentum + average
    new_outer = outer_share - 0.7 * (average + 0.9 * new_momentum)
    inner_share = new_outer.astype(BF16)
    inner_other = to_l(inner_share)

    early_slopes = (hold(slopes[0], inner_share), slopes[1])
    g31, g11, g21 = wgrad_of(pos, AT_EARLY, (False,) * 3, x_pair, early_slopes)
    inner_other = hold(inner_other, g21)
    inner_pair = by_core(low, inner_share, inner_other, 1)
    g31, g11, g21 = [hold(g, inner_other) for g in (g31, g11, g21)]
    e2 = to_x(inner_pair, 2)

    r31, r11, r21 = to_zm(g31), to_zp(g11), to_y(g21)
    late_slopes = (hold(slopes[0], inner_pair), slopes[1])
    pieces, piece_offs = first + second + third, first_offs + second_offs + third_offs
    g20, g01, part = late_of(pos, x_pair, late_slopes, piece_offs, pieces)

    ha20, hb20 = halves_of(g20, hold(r21, r31, r11, e2))
    ra20, rb20 = to_zm(ha20), to_zp(hb20)
    part_got = to_core(hold(part, ha20))
    last_slopes = (hold(slopes[0], ha20, hb20), slopes[1])
    g30, g10, g00 = wgrad_of(pos, AT_LAST, (False,) * 3, x_pair, last_slopes)
    s01 = sum_of(pos, [g01, hold(r31, g30), r11], rows, BF16)
    t01 = to_y(s01)

    s30, s10 = fold(g30, ra20, g10, hold(rb20, s01))
    t30, t10 = to_zm(s30), to_zp(s10)
    e1, e3 = [to_x(hold(inner_pair, s30), dx) for dx in (1, 3)]
    input_grad = igrad_of(
        factor, pos, piece_offs, hold(slopes[0], s30, s10), pieces, part_got
    )
    new_inner = side_by_side(pos, [hold(inner_pair, input_grad), e1, e2, e3])
    terms = [hold(g00, new_inner), t30, t10, t01]

    def rows_of(which, own):
        halves = [lax.dynamic_slice_in_dim(a, which * half, half, 0) for a in [own] + terms[1:]]
        return add(*halves) * factor

    give_rows = rows_of(1 - core, terms[0])
    keep_rows = rows_of(core, hold(terms[0], give_rows))
    weight_grad = by_core(core, keep_rows, to_core(give_rows), 1)[None]
    return (input_grad, weight_grad, new_outer, new_momentum, new_inner)


def solution(mesh):
    return jax.shard_map(
        shards,
        mesh=mesh,
        in_specs=(
            P(("replica", "shard"), None),
            P(("replica", "shard"), None),
            P("replica", "shard", None),
            P("replica", "shard", None),
            P("shard", None),
            P("shard", "replica"),
        ),
        out_specs=(
            P(("replica", "shard"), None),
            P("replica", "shard", None),
            P("shard", "replica"),
            P("shard", "replica"),
            P("shard", None),
        ),
        check_vma=False,
    )
```

time: 198 us -> 186 us (0.939)
  Pallas kernels: 74.2 us -> 88.2 us
  other arithmetic: 22.3 us -> 9.56 us
  local copies, waits for them, and re-layouts: 16.4 us -> 4.55 us
  waiting for transfers between devices: 40.7 us -> 36.1 us
  starting transfers between devices: 42.8 us -> 46.7 us
    ppermute x6, waiting for transfers between devices: 25.2 us -> 3.43 us  [to_zp(): return lax.ppermute(a, 'shard', shard_perm(1, 0, 0))]
    pallas_call x5 -> x8, Pallas kernels: 46.9 us -> 60.4 us  [the longest x3 25.3 us: pre_of(): pl.pallas_call(functools.partial(pre_kernel, factor, n, sums is not None,...]
    ppermute x7 -> x6, waiting for transfers between devices: 0.02 us -> 10.8 us  [to_zm(): return lax.ppermute(a, 'shard', shard_perm(-1, 0, 0))]
    ppermute x5, waiting for transfers between devices: 7.9 us -> 18.7 us  [to_y(): return lax.ppermute(a, 'shard', shard_perm(0, 1, 0))]
    convert_element_type x4 -> x0, other arithmetic: 9.53 us -> none  [the longest x1 3.04 us: shards(): s01 = add(g01, r31, hold(r11, part, inner_near)).astype(BF16)]
    unnamed x54 -> x36, local copies, waits for them, and re-layouts: 8.59 us -> 2.51 us
    ppermute x5, waiting for transfers between devices: 7.46 us -> 2.13 us  [to_core(): return lax.ppermute(a, 'shard', shard_perm(0, 0, 1))]
    ppermute x4 -> x6, starting transfers between devices: 4.05 us -> 8.87 us  [to_x(): return lax.ppermute(a, 'replica', perm)]
  transfers between devices with their start and end apart: 29 -> 30, of which waited for: 11 -> 12; matrix products, arithmetic and copies ran while one was open for 8% -> 2% of each run, Pallas kernels for 38% -> 46%
where the time goes in v3:
time: 186 us
  Pallas kernels  88.2 us (47%)
  starting transfers between devices  46.7 us (25%)
  waiting for transfers between devices  36.1 us (19%)
  other arithmetic  9.56 us (5%)
  local copies, waits for them, and re-layouts  4.55 us (2%)
    pallas_call x3, Pallas kernels, pre_of(): pl.pallas_call(functools.partial(pre_kernel, factor, n, sums is not None,...  25.3 us
    ppermute x5, waiting for transfers between devices, to_y(): return lax.ppermute(a, 'shard', shard_perm(0, 1, 0))  18.7 us
    pallas_call x2, Pallas kernels, wgrad_of(): pl.pallas_call(functools.partial(wgrad_kernel, halves), grid_spec=pltpu.P...  16.9 us
    ppermute x6, starting transfers between devices, to_zm(): return lax.ppermute(a, 'shard', shard_perm(-1, 0, 0))  16.3 us
    pallas_call x1, Pallas kernels, late_of(): pl.pallas_call(functools.partial(late_kernel, n, offs, rows), grid_spec=p...  14.8 us
    pallas_call x1, Pallas kernels, igrad_of(): pl.pallas_call(functools.partial(igrad_kernel, factor, offs, feats // (NZ...  11.1 us
    ppermute x5, starting transfers between devices, to_core(): return lax.ppermute(a, 'shard', shard_perm(0, 0, 1))  11 us
    ppermute x6, waiting for transfers between devices, to_zm(): return lax.ppermute(a, 'shard', shard_perm(-1, 0, 0))  10.8 us
  transfers between devices with their start and end apart: 30, of which 12 were waited for; matrix products, arithmetic and copies ran while one was open for 2% of the time, Pallas kernels for 46%

profile of v3, /device:TPU:1, one launch (start us, length us, event | category | flops | bytes accessed | tf_op | source)
XLA Modules:
  0.0 185.9 jit_solution(2124231812522451561)
XLA Ops:
  0.7 1.3 dynamic-slice_bitcast_fusion.1
  1.9 1.5 collective-permute-start
  3.4 1.5 collective-permute-done
  5.0 0.5 maximum_select_fusion.1.refs_0_
  5.5 0.5 collective-permute-start.4
  5.9 0.1 collective-permute-start.5
  6.1 3.8 %collective-permute-start.3 = (bf16[512,1024]{1,0:T(8,128)(2,1)S(1)}, bf16[512,1024]{1,0:T(8,128)(2,1)S(1)}, u32[]{:S(2)}, u32[]{:S(2)}) collective-permute-start(bf16[512,1024]{1,0:T(8,128)(2,1)S(1)} %maximum_select_fusion.1.refs_0_), channel_id=1, source_target_pairs={{0,12},{1,13},{2,14},{3,15},{4,0},{5,1},{6,2},{7,3},{8,4},{9,5},{1... | collective-permute-start | bytes 3145736 | tf_op jit(solution)/shard_map/ppermute | solution.py:33
  9.9 2.9 %collective-permute-start.1 = (bf16[512,1024]{1,0:T(8,128)(2,1)S(1)}, bf16[512,1024]{1,0:T(8,128)(2,1)}, u32[]{:S(2)}, u32[]{:S(2)}) collective-permute-start(bf16[512,1024]{1,0:T(8,128)(2,1)S(1)} %maximum_select_fusion.1.refs_0_), channel_id=1, source_target_pairs={{0,2},{1,3},{2,0},{3,1},{4,6},{5,7},{6,4},{7,5},{8,10},{9,11},{10,... | collective-permute-start | bytes 3145736 | tf_op jit(solution)/shard_map/ppermute | solution.py:37
  12.8 0.7 stack.55.off_ref.pos_ref.blk_ref.s_ref
  13.5 6.8 %decode.1 = (bf16[256,1024]{1,0:T(8,128)(2,1)}, bf16[256,1024]{1,0:T(8,128)(2,1)}, bf16[256,1024]{1,0:T(8,128)(2,1)}, bf16[256,1024]{1,0:T(8,128)(2,1)}) custom-call(s32[19]{0:T(128)} %stack.55.off_ref.pos_ref.blk_ref.s_ref, f32[256,4096]{1,0:T(8,128)} %outer_ref, f32[1,256,4096]{2,1,0:T(8,128)} %inner_ref.1), custom_call_target="tpu_custom_call" | custom-call | flops 3145728 | bytes 3145728 | tf_op jit(solution)/shard_map/decode/pallas_call | solution.py:124
  20.4 1.3 collective-permute-start.6
  21.7 10.4 %collective-permute-done.3.refs_2_ = bf16[512,1024]{1,0:T(8,128)(2,1)S(1)} collective-permute-done((bf16[512,1024]{1,0:T(8,128)(2,1)S(1)}, bf16[512,1024]{1,0:T(8,128)(2,1)S(1)}, u32[]{:S(2)}, u32[]{:S(2)}) %collective-permute-start.3) | collective-permute-done | bytes 1048608 | tf_op jit(solution)/shard_map/ppermute | solution.py:33
  32.1 3.5 %collective-permute-done.1.refs_3_ = bf16[512,1024]{1,0:T(8,128)(2,1)} collective-permute-done((bf16[512,1024]{1,0:T(8,128)(2,1)S(1)}, bf16[512,1024]{1,0:T(8,128)(2,1)}, u32[]{:S(2)}, u32[]{:S(2)}) %collective-permute-start.1) | collective-permute-done | bytes 1048608 | tf_op jit(solution)/shard_map/ppermute | solution.py:37
  35.6 0.8 copy-done.16
  36.4 1.3 collective-permute-start.9
  37.8 0.3 collective-permute-start.7
  38.0 2.7 %collective-permute-start.13 = (bf16[256,1024]{1,0:T(8,128)(2,1)}, bf16[256,1024]{1,0:T(8,128)(2,1)}, u32[]{:S(2)}, u32[]{:S(2)}) collective-permute-start(bf16[256,1024]{1,0:T(8,128)(2,1)} %get-tuple-element.78), channel_id=1, source_target_pairs={{0,64},{16,80},{32,96},{48,112},{64,0},{80,16},{96,32},{112,48},{1... | collective-permute-start | bytes 1572872 | tf_op jit(solution)/shard_map/ppermute | solution.py:50
  40.8 9.6 %pre.2 = (f32[512,1024]{1,0:T(8,128)}, f32[512,1024]{1,0:T(8,128)}) custom-call(s32[19]{0:T(128)} %stack.55.off_ref.pos_ref.blk_ref.s_ref, bf16[512,1024]{1,0:T(8,128)(2,1)} %copy-done, bf16[512,1024]{1,0:T(8,128)(2,1)} %copy-done.2, bf16[512,1024]{1,0:T(8,128)(2,1)} %copy-done.1, bf16[512,1024]{1,0:T(8,128)(2,1)} %collective-permute-done.1.refs_3_, ...), custom_call_target="tpu_custom_call" | custom-call | flops 1288490240 | bytes 3774873 | tf_op jit(solution)/shard_map/pre/pallas_call | solution.py:261
  50.4 0.2 collective-permute-start.8
  50.5 2.6 %collective-permute-start.10 = (bf16[512,1024]{1,0:T(8,128)(2,1)}, bf16[512,1024]{1,0:T(8,128)(2,1)S(1)}, u32[]{:S(2)}, u32[]{:S(2)}) collective-permute-start(bf16[512,1024]{1,0:T(8,128)(2,1)} %collective-permute-done.1.refs_3_), channel_id=1, source_target_pairs={{0,12},{1,13},{2,14},{3,15},{4,0},{5,1},{6,2},{7,3},{8,4},{9,5},{1... | collective-permute-start | bytes 3145736 | tf_op jit(solution)/shard_map/ppermute | solution.py:33
  53.1 2.8 %collective-permute-start.14 = (bf16[256,1024]{1,0:T(8,128)(2,1)}, bf16[256,1024]{1,0:T(8,128)(2,1)}, u32[]{:S(2)}, u32[]{:S(2)}) collective-permute-start(bf16[256,1024]{1,0:T(8,128)(2,1)} %get-tuple-element.80), channel_id=1, source_target_pairs={{0,96},{16,112},{32,0},{48,16},{64,32},{80,48},{96,64},{112,80},{1... | collective-permute-start | bytes 1572872 | tf_op jit(solution)/shard_map/ppermute | solution.py:50
  55.9 2.0 %collective-permute-start.11 = (bf16[256,1024]{1,0:T(8,128)(2,1)}, bf16[256,1024]{1,0:T(8,128)(2,1)S(1)}, u32[]{:S(2)}, u32[]{:S(2)}) collective-permute-start(bf16[256,1024]{1,0:T(8,128)(2,1)} %collective-permute-done.7.refs_0_.refs_4_), channel_id=1, source_target_pairs={{0,2},{1,3},{2,0},{3,1},{4,6},{5,7},{6,4},{7,5},{8,10},{9,11},{10,... | collective-permute-start | bytes 1572872 | tf_op jit(solution)/shard_map/ppermute | solution.py:37
  57.9 0.9 collective-permute-start.12
  58.9 5.6 %pre.3 = (f32[512,1024]{1,0:T(8,128)}, f32[512,1024]{1,0:T(8,128)}) custom-call(s32[19]{0:T(128)} %stack.55.off_ref.pos_ref.blk_ref.s_ref, bf16[256,1024]{1,0:T(8,128)(2,1)} %collective-permute-done.7.refs_0_.refs_4_, bf16[256,1024]{1,0:T(8,128)(2,1)} %collective-permute-done.9.refs_1_.refs_5_, bf16[512,4096]{1,0:T(8,128)(2,1)} %xo_ref.5, ...), custom_call_target="tpu_custom_call" | custom-call | flops 322122560 | bytes 1887436 | tf_op jit(solution)/shard_map/pre/pallas_call | solution.py:261
  64.5 1.3 add_convert_fusion
  65.8 1.6 collective-permute-done.11.refs_2_.refs_8_
  67.4 11.2 %collective-permute-done.12.refs_3_.refs_9_ = bf16[256,1024]{1,0:T(8,128)(2,1)S(1)} collective-permute-done((bf16[256,1024]{1,0:T(8,128)(2,1)}, bf16[256,1024]{1,0:T(8,128)(2,1)S(1)}, u32[]{:S(2)}, u32[]{:S(2)}) %collective-permute-start.12) | collective-permute-done | bytes 524320 | tf_op jit(solution)/shard_map/ppermute | solution.py:37
  78.7 0.7 collective-permute-start.15
  79.3 0.1 copy-done.6
  79.5 0.3 copy-done.3
  79.8 0.3 copy-done.4
  80.1 10.1 %slope.1 = (bf16[512,1024]{1,0:T(8,128)(2,1)}, bf16[512,1024]{1,0:T(8,128)(2,1)}) custom-call(s32[19]{0:T(128)} %stack.55.off_ref.pos_ref.blk_ref.s_ref, bf16[512,1024]{1,0:T(8,128)(2,1)} %copy-done.3, bf16[512,1024]{1,0:T(8,128)(2,1)} %copy-done.4, bf16[256,1024]{1,0:T(8,128)(2,1)} %copy-done.5, bf16[256,1024]{1,0:T(8,128)(2,1)} %copy-done.6, ...), custom_call_target="tpu_custom_call" | custom-call | flops 966367616 | bytes 3145728 | tf_op jit(solution)/shard_map/slope/pallas_call | solution.py:261
  90.3 2.7 %fusion = (bf16[256,512]{1,0:T(8,128)(2,1)S(1)}, f32[256,512]{1,0:T(8,128)}, f32[256,512]{1,0:T(8,128)}) fusion(bf16[256,512]{1,0:T(8,128)(2,1)} %collective-permute-done.15, bf16[256,1024]{1,0:T(8,128)(2,1)} %collective-permute-done.14, s32[]{:T(128)S(6)} %select_n.151, bf16[256,1024]{1,0:T(8,128)(2,1)} %collective-permute-done.13, ...), kind=kLoop, calls=%fused_computation.11 | loop fusion | flops 2228224 | bytes 3670024 | tf_op jit(solution)/shard_map/convert_element_type | solution.py:505
  93.0 0.4 collective-permute-start.16
  93.4 8.4 %wgrad.2 = (bf16[512,1024]{1,0:T(8,128)(2,1)}, bf16[512,1024]{1,0:T(8,128)(2,1)}, bf16[512,1024]{1,0:T(8,128)(2,1)}) custom-call(s32[19]{0:T(128)} %stack.55.off_ref.pos_ref.blk_ref.s_ref, bf16[512,4096]{1,0:T(8,128)(2,1)} %xo_ref.5, bf16[512,4096]{1,0:T(8,128)(2,1)} %collective-permute-done.4.refs_8_.refs_9_.refs_10_.refs_11_.refs_4_.refs_5_.xp_ref, ...), custom_call_target="tpu_custom_call" | custom-call | flops 966367616 | bytes 1887436 | tf_op jit(solution)/shard_map/wgrad/pallas_call | solution.py:302
  101.9 2.7 %collective-permute-start.17 = (bf16[512,1024]{1,0:T(8,128)(2,1)}, bf16[512,1024]{1,0:T(8,128)(2,1)}, u32[]{:S(2)}, u32[]{:S(2)}) collective-permute-start(bf16[512,1024]{1,0:T(8,128)(2,1)} %get-tuple-element.89), channel_id=1, source_target_pairs={{0,2},{1,3},{2,0},{3,1},{4,6},{5,7},{6,4},{7,5},{8,10},{9,11},{10,... | collective-permute-start | bytes 3145736 | tf_op jit(solution)/shard_map/ppermute | solution.py:37
  104.6 2.6 %collective-permute-start.18 = (bf16[512,1024]{1,0:T(8,128)(2,1)}, bf16[512,1024]{1,0:T(8,128)(2,1)S(1)}, u32[]{:S(2)}, u32[]{:S(2)}) collective-permute-start(bf16[512,1024]{1,0:T(8,128)(2,1)} %get-tuple-element.91), channel_id=1, source_target_pairs={{0,12},{1,13},{2,14},{3,15},{4,0},{5,1},{6,2},{7,3},{8,4},{9,5},{1... | collective-permute-start | bytes 3145736 | tf_op jit(solution)/shard_map/ppermute | solution.py:33
  107.2 0.1 maximum_select_fusion.2.refs_0_
  107.3 0.6 collective-permute-start.20
  107.9 14.8 %late.1 = (bf16[512,1024]{1,0:T(8,128)(2,1)}, bf16[512,1024]{1,0:T(8,128)(2,1)}, bf16[512,4096]{1,0:T(8,128)(2,1)}) custom-call(s32[19]{0:T(128)} %stack.55.off_ref.pos_ref.blk_ref.s_ref, bf16[512,4096]{1,0:T(8,128)(2,1)} %xo_ref.5, bf16[512,4096]{1,0:T(8,128)(2,1)} %collective-permute-done.4.refs_8_.refs_9_.refs_10_.refs_11_.refs_4_.refs_5_.xp_ref, ...), custom_call_target="tpu_custom_call" | custom-call | flops 1932735232 | bytes 7549747 | tf_op jit(solution)/shard_map/late/pallas_call | solution.py:355
  122.8 0.2 collective-permute-done.19.refs_2_
  123.0 0.4 collective-permute-done.17.b_ref
  123.4 0.4 collective-permute-done.18.refs_1_
  123.8 3.2 %halves.1 = (bf16[256,1024]{1,0:T(8,128)(2,1)}, bf16[256,1024]{1,0:T(8,128)(2,1)}) custom-call(bf16[512,1024]{1,0:T(8,128)(2,1)} %get-tuple-element.88.a_ref, bf16[512,1024]{1,0:T(8,128)(2,1)} %collective-permute-done.17.b_ref), custom_call_target="tpu_custom_call" | custom-call | flops 157286 | bytes 943718 | tf_op jit(solution)/shard_map/halves/pallas_call | solution.py:208
  127.0 7.1 %collective-permute-start.23 = (bf16[512,4096]{1,0:T(8,128)(2,1)}, bf16[512,4096]{1,0:T(8,128)(2,1)}, u32[]{:S(2)}, u32[]{:S(2)}) collective-permute-start(bf16[512,4096]{1,0:T(8,128)(2,1)} %get-tuple-element.107), channel_id=1, source_target_pairs={{0,1},{1,0},{2,3},{3,2},{4,5},{5,4},{6,7},{7,6},{8,9},{9,8},{10,11... | collective-permute-start | bytes 12582920 | tf_op jit(solution)/shard_map/ppermute | solution.py:41
  134.1 3.3 %collective-permute-start.21 = (bf16[256,1024]{1,0:T(8,128)(2,1)}, bf16[256,1024]{1,0:T(8,128)(2,1)}, u32[]{:S(2)}, u32[]{:S(2)}) collective-permute-start(bf16[256,1024]{1,0:T(8,128)(2,1)} %get-tuple-element.95), channel_id=1, source_target_pairs={{0,12},{1,13},{2,14},{3,15},{4,0},{5,1},{6,2},{7,3},{8,4},{9,5},{1... | collective-permute-start | bytes 1572872 | tf_op jit(solution)/shard_map/ppermute | solution.py:33
  137.4 8.4 %wgrad.3 = (bf16[512,1024]{1,0:T(8,128)(2,1)}, bf16[512,1024]{1,0:T(8,128)(2,1)}, bf16[512,1024]{1,0:T(8,128)(2,1)}) custom-call(s32[19]{0:T(128)} %stack.55.off_ref.pos_ref.blk_ref.s_ref, bf16[512,4096]{1,0:T(8,128)(2,1)} %xo_ref.5, bf16[512,4096]{1,0:T(8,128)(2,1)} %collective-permute-done.4.refs_8_.refs_9_.refs_10_.refs_11_.refs_4_.refs_5_.xp_ref, ...), custom_call_target="tpu_custom_call" | custom-call | flops 966367616 | bytes 1887436 | tf_op jit(solution)/shard_map/wgrad/pallas_call | solution.py:302
  145.8 3.5 %sum.1 = bf16[512,1024]{1,0:T(8,128)(2,1)} custom-call(s32[19]{0:T(128)} %stack.55.off_ref.pos_ref.blk_ref.s_ref, bf16[512,1024]{1,0:T(8,128)(2,1)} %get-tuple-element.100.refs_0_, bf16[512,1024]{1,0:T(8,128)(2,1)} %copy-done.9, bf16[512,1024]{1,0:T(8,128)(2,1)} %copy-done.8), custom_call_target="tpu_custom_call" | custom-call | flops 471859 | bytes 1258291 | tf_op jit(solution)/shard_map/sum/pallas_call | solution.py:156
  149.4 0.5 collective-permute-start.28
  149.9 0.8 copy-done.17
  150.8 2.4 %fold.1 = (bf16[512,1024]{1,0:T(8,128)(2,1)}, bf16[512,1024]{1,0:T(8,128)(2,1)}) custom-call(bf16[512,1024]{1,0:T(8,128)(2,1)} %get-tuple-element.98.up_ref, bf16[256,1024]{1,0:T(8,128)(2,1)} %collective-permute-done.21.a_ref, bf16[512,1024]{1,0:T(8,128)(2,1)} %get-tuple-element.99.low_ref, ...), custom_call_target="tpu_custom_call", output_to_operand_aliasing={{0}: (0, {}), {1}: (2, {})} | custom-call | flops 157286 | bytes 943718 | tf_op jit(solution)/shard_map/fold/pallas_call | solution.py:180
  153.2 2.7 %collective-permute-start.26 = (bf16[512,1024]{1,0:T(8,128)(2,1)}, bf16[512,1024]{1,0:T(8,128)(2,1)}, u32[]{:S(2)}, u32[]{:S(2)}) collective-permute-start(bf16[512,1024]{1,0:T(8,128)(2,1)} %get-tuple-element.103), channel_id=1, source_target_pairs={{0,12},{1,13},{2,14},{3,15},{4,0},{5,1},{6,2},{7,3},{8,4},{9,5},{1... | collective-permute-start | bytes 3145736 | tf_op jit(solution)/shard_map/ppermute | solution.py:33
  155.8 0.5 collective-permute-start.25
  156.4 1.0 collective-permute-start.24
  157.3 11.1 %igrad.1 = bf16[512,4096]{1,0:T(8,128)(2,1)} custom-call(s32[19]{0:T(128)} %stack.55.off_ref.pos_ref.blk_ref.s_ref, bf16[512,1024]{1,0:T(8,128)(2,1)} %get-tuple-element.105.so_ref.s_ref, bf16[512,1024]{1,0:T(8,128)(2,1)} %copy-done, bf16[512,1024]{1,0:T(8,128)(2,1)} %copy-done.2, bf16[512,1024]{1,0:T(8,128)(2,1)} %copy-done.1, ...), custom_call_target="tpu_custom_call" | custom-call | flops 1288490240 | bytes 3774873 | tf_op jit(solution)/shard_map/igrad/pallas_call | solution.py:395
  168.4 1.0 collective-permute-done.24.refs_1_
  169.4 4.1 %place.1 = bf16[256,4096]{1,0:T(8,128)(2,1)} custom-call(s32[19]{0:T(128)} %stack.55.off_ref.pos_ref.blk_ref.s_ref, bf16[256,1024]{1,0:T(8,128)(2,1)} %copy-done.7, bf16[256,1024]{1,0:T(8,128)(2,1)} %collective-permute-done.24.refs_1_, bf16[256,1024]{1,0:T(8,128)(2,1)} %copy-done.12, bf16[256,1024]{1,0:T(8,128)(2,1)} %copy-done.13), custom_call_target="tpu_custom_call" | custom-call | bytes 1258291 | tf_op jit(solution)/shard_map/place/pallas_call | solution.py:432
  173.5 2.0 %collective-permute-done.28 = bf16[512,1024]{1,0:T(8,128)(2,1)S(1)} collective-permute-done((bf16[512,1024]{1,0:T(8,128)(2,1)}, bf16[512,1024]{1,0:T(8,128)(2,1)S(1)}, u32[]{:S(2)}, u32[]{:S(2)}) %collective-permute-start.28) | collective-permute-done | bytes 1048608 | tf_op jit(solution)/shard_map/ppermute | solution.py:37
  175.5 3.1 %collective-permute-done.27 = bf16[512,1024]{1,0:T(8,128)(2,1)} collective-permute-done((bf16[512,1024]{1,0:T(8,128)(2,1)}, bf16[512,1024]{1,0:T(8,128)(2,1)}, u32[]{:S(2)}, u32[]{:S(2)}) %collective-permute-start.27) | collective-permute-done | bytes 1048608 | tf_op jit(solution)/shard_map/ppermute | solution.py:29
  178.6 1.7 add_multiply_fusion
  180.3 1.8 collective-permute-start.29
  182.1 1.7 multiply_bitcast_fusion
  183.8 0.6 collective-permute-done.29
  184.4 1.6 maximum_select_fusion
  (55 shorter events, 0.3 us)
Async XLA Ops:
  1.9 3.0 %collective-permute-start = (bf16[256,1024]{1,0:T(8,128)(2,1)S(1)}, bf16[256,1024]{1,0:T(8,128)(2,1)S(1)}, u32[]{:S(2)}, u32[]{:S(2)}) collective-permute-start(bf16[256,1024]{1,0:T(8,128)(2,1)S(1)} %get-tuple-element.117), channel_id=1, source_target_pairs={{0,1},{1,0},{2,3},{3,2},{4,5},{5,4},{6,7},{7,6},{8,9},{9,8},{10,11... | collective-permute-start | bytes 1572872 | tf_op jit(solution)/shard_map/ppermute | solution.py:41
  5.5 14.9 %copy-start = (bf16[512,1024]{1,0:T(8,128)(2,1)}, bf16[512,1024]{1,0:T(8,128)(2,1)S(1)}, u32[]{:S(2)}) copy-start(bf16[512,1024]{1,0:T(8,128)(2,1)S(1)} %maximum_select_fusion.1.refs_0_) | copy-start | bytes 3145732
  5.5 14.9 %collective-permute-start.4 = (bf16[512,4096]{1,0:T(8,128)(2,1)}, bf16[512,4096]{1,0:T(8,128)(2,1)}, u32[]{:S(2)}, u32[]{:S(2)}) collective-permute-start(bf16[512,4096]{1,0:T(8,128)(2,1)} %xo_ref.5), channel_id=1, source_target_pairs={{0,1},{1,0},{2,3},{3,2},{4,5},{5,4},{6,7},{7,6},{8,9},{9,8},{10,11... | collective-permute-start | bytes 12582920 | tf_op jit(solution)/shard_map/ppermute | solution.py:41
  5.9 14.4 %collective-permute-start.5 = (bf16[512,2048]{1,0:T(8,128)(2,1)}, bf16[512,2048]{1,0:T(8,128)(2,1)}, u32[]{:S(2)}, u32[]{:S(2)}) collective-permute-start(bf16[512,2048]{1,0:T(8,128)(2,1)} %refs_14_.1), channel_id=1, source_target_pairs={{0,1},{1,0},{2,3},{3,2},{4,5},{5,4},{6,7},{7,6},{8,9},{9,8},{10,11... | collective-permute-start | bytes 6291464 | tf_op jit(solution)/shard_map/ppermute | solution.py:41
  6.1 26.0 %collective-permute-start.3 = (bf16[512,1024]{1,0:T(8,128)(2,1)S(1)}, bf16[512,1024]{1,0:T(8,128)(2,1)S(1)}, u32[]{:S(2)}, u32[]{:S(2)}) collective-permute-start(bf16[512,1024]{1,0:T(8,128)(2,1)S(1)} %maximum_select_fusion.1.refs_0_), channel_id=1, source_target_pairs={{0,12},{1,13},{2,14},{3,15},{4,0},{5,1},{6,2},{7,3},{8,4},{9,5},{1... | collective-permute-start | bytes 3145736 | tf_op jit(solution)/shard_map/ppermute | solution.py:33
  9.9 25.7 %collective-permute-start.1 = (bf16[512,1024]{1,0:T(8,128)(2,1)S(1)}, bf16[512,1024]{1,0:T(8,128)(2,1)}, u32[]{:S(2)}, u32[]{:S(2)}) collective-permute-start(bf16[512,1024]{1,0:T(8,128)(2,1)S(1)} %maximum_select_fusion.1.refs_0_), channel_id=1, source_target_pairs={{0,2},{1,3},{2,0},{3,1},{4,6},{5,7},{6,4},{7,5},{8,10},{9,11},{10,... | collective-permute-start | bytes 3145736 | tf_op jit(solution)/shard_map/ppermute | solution.py:37
  12.8 24.9 %collective-permute-start.2 = (bf16[512,1024]{1,0:T(8,128)(2,1)S(1)}, bf16[512,1024]{1,0:T(8,128)(2,1)S(1)}, u32[]{:S(2)}, u32[]{:S(2)}) collective-permute-start(bf16[512,1024]{1,0:T(8,128)(2,1)S(1)} %maximum_select_fusion.1.refs_0_), channel_id=1, source_target_pairs={{0,4},{1,5},{2,6},{3,7},{4,8},{5,9},{6,10},{7,11},{8,12},{9,13},{1... | collective-permute-start | bytes 3145736 | tf_op jit(solution)/shard_map/ppermute | solution.py:29
  20.4 15.2 %collective-permute-start.6 = (bf16[256,1024]{1,0:T(8,128)(2,1)}, bf16[256,1024]{1,0:T(8,128)(2,1)S(1)}, u32[]{:S(2)}, u32[]{:S(2)}) collective-permute-start(bf16[256,1024]{1,0:T(8,128)(2,1)} %get-tuple-element.65), channel_id=1, source_target_pairs={{0,32},{16,48},{32,64},{48,80},{64,96},{80,112},{96,0},{112,16},{1... | collective-permute-start | bytes 1572872 | tf_op jit(solution)/shard_map/ppermute | solution.py:50
  32.1 8.7 %copy-start.1 = (bf16[512,1024]{1,0:T(8,128)(2,1)}, bf16[512,1024]{1,0:T(8,128)(2,1)S(1)}, u32[]{:S(2)}) copy-start(bf16[512,1024]{1,0:T(8,128)(2,1)S(1)} %collective-permute-done.3.refs_2_) | copy-start | bytes 3145732
  35.6 0.8 copy-start.16
  36.4 14.0 %collective-permute-start.9 = (bf16[256,1024]{1,0:T(8,128)(2,1)S(1)}, bf16[256,1024]{1,0:T(8,128)(2,1)}, u32[]{:S(2)}, u32[]{:S(2)}) collective-permute-start(bf16[256,1024]{1,0:T(8,128)(2,1)S(1)} %slice.7), channel_id=1, source_target_pairs={{0,12},{1,13},{2,14},{3,15},{4,0},{5,1},{6,2},{7,3},{8,4},{9,5},{1... | collective-permute-start | bytes 1572872 | tf_op jit(solution)/shard_map/ppermute | solution.py:33
  37.7 3.0 %copy-start.2 = (bf16[512,1024]{1,0:T(8,128)(2,1)}, bf16[512,1024]{1,0:T(8,128)(2,1)S(1)}, u32[]{:S(2)}) copy-start(bf16[512,1024]{1,0:T(8,128)(2,1)S(1)} %collective-permute-done.2.refs_1_) | copy-start | bytes 3145732
  37.8 12.6 %collective-permute-start.7 = (bf16[256,1024]{1,0:T(8,128)(2,1)S(1)}, bf16[256,1024]{1,0:T(8,128)(2,1)}, u32[]{:S(2)}, u32[]{:S(2)}) collective-permute-start(bf16[256,1024]{1,0:T(8,128)(2,1)S(1)} %slice.6), channel_id=1, source_target_pairs={{0,4},{1,5},{2,6},{3,7},{4,8},{5,9},{6,10},{7,11},{8,12},{9,13},{1... | collective-permute-start | bytes 1572872 | tf_op jit(solution)/shard_map/ppermute | solution.py:29
  38.0 19.9 %collective-permute-start.13 = (bf16[256,1024]{1,0:T(8,128)(2,1)}, bf16[256,1024]{1,0:T(8,128)(2,1)}, u32[]{:S(2)}, u32[]{:S(2)}) collective-permute-start(bf16[256,1024]{1,0:T(8,128)(2,1)} %get-tuple-element.78), channel_id=1, source_target_pairs={{0,64},{16,80},{32,96},{48,112},{64,0},{80,16},{96,32},{112,48},{1... | collective-permute-start | bytes 1572872 | tf_op jit(solution)/shard_map/ppermute | solution.py:50
  50.4 28.3 %collective-permute-start.8 = (bf16[512,1024]{1,0:T(8,128)(2,1)}, bf16[512,1024]{1,0:T(8,128)(2,1)S(1)}, u32[]{:S(2)}, u32[]{:S(2)}) collective-permute-start(bf16[512,1024]{1,0:T(8,128)(2,1)} %collective-permute-done.1.refs_3_), channel_id=1, source_target_pairs={{0,4},{1,5},{2,6},{3,7},{4,8},{5,9},{6,10},{7,11},{8,12},{9,13},{1... | collective-permute-start | bytes 3145736 | tf_op jit(solution)/shard_map/ppermute | solution.py:29
  50.5 28.1 %collective-permute-start.10 = (bf16[512,1024]{1,0:T(8,128)(2,1)}, bf16[512,1024]{1,0:T(8,128)(2,1)S(1)}, u32[]{:S(2)}, u32[]{:S(2)}) collective-permute-start(bf16[512,1024]{1,0:T(8,128)(2,1)} %collective-permute-done.1.refs_3_), channel_id=1, source_target_pairs={{0,12},{1,13},{2,14},{3,15},{4,0},{5,1},{6,2},{7,3},{8,4},{9,5},{1... | collective-permute-start | bytes 3145736 | tf_op jit(solution)/shard_map/ppermute | solution.py:33
  53.1 11.4 %collective-permute-start.14 = (bf16[256,1024]{1,0:T(8,128)(2,1)}, bf16[256,1024]{1,0:T(8,128)(2,1)}, u32[]{:S(2)}, u32[]{:S(2)}) collective-permute-start(bf16[256,1024]{1,0:T(8,128)(2,1)} %get-tuple-element.80), channel_id=1, source_target_pairs={{0,96},{16,112},{32,0},{48,16},{64,32},{80,48},{96,64},{112,80},{1... | collective-permute-start | bytes 1572872 | tf_op jit(solution)/shard_map/ppermute | solution.py:50
  55.9 11.5 %collective-permute-start.11 = (bf16[256,1024]{1,0:T(8,128)(2,1)}, bf16[256,1024]{1,0:T(8,128)(2,1)S(1)}, u32[]{:S(2)}, u32[]{:S(2)}) collective-permute-start(bf16[256,1024]{1,0:T(8,128)(2,1)} %collective-permute-done.7.refs_0_.refs_4_), channel_id=1, source_target_pairs={{0,2},{1,3},{2,0},{3,1},{4,6},{5,7},{6,4},{7,5},{8,10},{9,11},{10,... | collective-permute-start | bytes 1572872 | tf_op jit(solution)/shard_map/ppermute | solution.py:37
  57.9 20.7 %collective-permute-start.12 = (bf16[256,1024]{1,0:T(8,128)(2,1)}, bf16[256,1024]{1,0:T(8,128)(2,1)S(1)}, u32[]{:S(2)}, u32[]{:S(2)}) collective-permute-start(bf16[256,1024]{1,0:T(8,128)(2,1)} %collective-permute-done.9.refs_1_.refs_5_), channel_id=1, source_target_pairs={{0,2},{1,3},{2,0},{3,1},{4,6},{5,7},{6,4},{7,5},{8,10},{9,11},{10,... | collective-permute-start | bytes 1572872 | tf_op jit(solution)/shard_map/ppermute | solution.py:37
  58.9 5.7 %copy-start.15 = (bf16[256,1024]{1,0:T(8,128)(2,1)S(1)}, bf16[256,1024]{1,0:T(8,128)(2,1)}, u32[]{:S(2)}) copy-start(bf16[256,1024]{1,0:T(8,128)(2,1)} %get-tuple-element.76) | copy-start | bytes 1572868
  67.4 11.9 %copy-start.5 = (bf16[256,1024]{1,0:T(8,128)(2,1)}, bf16[256,1024]{1,0:T(8,128)(2,1)S(1)}, u32[]{:S(2)}) copy-start(bf16[256,1024]{1,0:T(8,128)(2,1)S(1)} %collective-permute-done.11.refs_2_.refs_8_) | copy-start | bytes 1572868
  78.7 0.8 copy-start.6
  78.7 1.1 copy-start.3
  78.7 1.5 copy-start.4
  78.7 11.6 %collective-permute-start.15 = (bf16[256,512]{1,0:T(8,128)(2,1)S(1)}, bf16[256,512]{1,0:T(8,128)(2,1)}, u32[]{:S(2)}, u32[]{:S(2)}) collective-permute-start(bf16[256,512]{1,0:T(8,128)(2,1)S(1)} %add_convert_fusion), channel_id=1, source_target_pairs={{0,16},{16,0},{32,48},{48,32},{64,80},{80,64},{96,112},{112,96},{1... | collective-permute-start | bytes 786440 | tf_op jit(solution)/shard_map/ppermute | solution.py:54
  80.1 10.2 %copy-start.14 = (f32[256,512]{1,0:T(8,128)S(1)}, f32[256,512]{1,0:T(8,128)}, u32[]{:S(2)}) copy-start(f32[256,512]{1,0:T(8,128)} %param.11) | copy-start | bytes 1572868
  93.0 8.8 %collective-permute-start.16 = (bf16[256,512]{1,0:T(8,128)(2,1)S(1)}, bf16[256,512]{1,0:T(8,128)(2,1)S(1)}, u32[]{:S(2)}, u32[]{:S(2)}) collective-permute-start(bf16[256,512]{1,0:T(8,128)(2,1)S(1)} %get-tuple-element.113), channel_id=1, source_target_pairs={{0,16},{16,0},{32,48},{48,32},{64,80},{80,64},{96,112},{112,96},{1... | collective-permute-start | bytes 786440 | tf_op jit(solution)/shard_map/ppermute | solution.py:54
  101.9 21.2 %collective-permute-start.19 = (bf16[512,1024]{1,0:T(8,128)(2,1)}, bf16[512,1024]{1,0:T(8,128)(2,1)S(1)}, u32[]{:S(2)}, u32[]{:S(2)}) collective-permute-start(bf16[512,1024]{1,0:T(8,128)(2,1)} %get-tuple-element.93), channel_id=1, source_target_pairs={{0,4},{1,5},{2,6},{3,7},{4,8},{5,9},{6,10},{7,11},{8,12},{9,13},{1... | collective-permute-start | bytes 3145736 | tf_op jit(solution)/shard_map/ppermute | solution.py:29
  101.9 21.5 %collective-permute-start.17 = (bf16[512,1024]{1,0:T(8,128)(2,1)}, bf16[512,1024]{1,0:T(8,128)(2,1)}, u32[]{:S(2)}, u32[]{:S(2)}) collective-permute-start(bf16[512,1024]{1,0:T(8,128)(2,1)} %get-tuple-element.89), channel_id=1, source_target_pairs={{0,2},{1,3},{2,0},{3,1},{4,6},{5,7},{6,4},{7,5},{8,10},{9,11},{10,... | collective-permute-start | bytes 3145736 | tf_op jit(solution)/shard_map/ppermute | solution.py:37
  104.6 19.2 %collective-permute-start.18 = (bf16[512,1024]{1,0:T(8,128)(2,1)}, bf16[512,1024]{1,0:T(8,128)(2,1)S(1)}, u32[]{:S(2)}, u32[]{:S(2)}) collective-permute-start(bf16[512,1024]{1,0:T(8,128)(2,1)} %get-tuple-element.91), channel_id=1, source_target_pairs={{0,12},{1,13},{2,14},{3,15},{4,0},{5,1},{6,2},{7,3},{8,4},{9,5},{1... | collective-permute-start | bytes 3145736 | tf_op jit(solution)/shard_map/ppermute | solution.py:33
  107.3 49.0 %copy-start.7 = (bf16[256,1024]{1,0:T(8,128)(2,1)}, bf16[256,1024]{1,0:T(8,128)(2,1)S(1)}, u32[]{:S(2)}) copy-start(bf16[256,1024]{1,0:T(8,128)(2,1)S(1)} %maximum_select_fusion.2.refs_0_) | copy-start | bytes 1572868
  107.3 15.4 %collective-permute-start.20 = (bf16[256,1024]{1,0:T(8,128)(2,1)S(1)}, bf16[256,1024]{1,0:T(8,128)(2,1)S(1)}, u32[]{:S(2)}, u32[]{:S(2)}) collective-permute-start(bf16[256,1024]{1,0:T(8,128)(2,1)S(1)} %maximum_select_fusion.2.refs_0_), channel_id=1, source_target_pairs={{0,64},{16,80},{32,96},{48,112},{64,0},{80,16},{96,32},{112,48},{1... | collective-permute-start | bytes 1572872 | tf_op jit(solution)/shard_map/ppermute | solution.py:50
  122.8 23.0 %copy-start.12 = (bf16[256,1024]{1,0:T(8,128)(2,1)}, bf16[256,1024]{1,0:T(8,128)(2,1)S(1)}, u32[]{:S(2)}) copy-start(bf16[256,1024]{1,0:T(8,128)(2,1)S(1)} %collective-permute-done.20.refs_2_) | copy-start | bytes 1572868
  123.0 22.8 %copy-start.8 = (bf16[512,1024]{1,0:T(8,128)(2,1)}, bf16[512,1024]{1,0:T(8,128)(2,1)S(1)}, u32[]{:S(2)}) copy-start(bf16[512,1024]{1,0:T(8,128)(2,1)S(1)} %collective-permute-done.19.refs_2_) | copy-start | bytes 3145732
  123.8 22.0 %copy-start.9 = (bf16[512,1024]{1,0:T(8,128)(2,1)}, bf16[512,1024]{1,0:T(8,128)(2,1)S(1)}, u32[]{:S(2)}) copy-start(bf16[512,1024]{1,0:T(8,128)(2,1)S(1)} %collective-permute-done.18.refs_1_) | copy-start | bytes 3145732
  127.0 29.4 %collective-permute-start.23 = (bf16[512,4096]{1,0:T(8,128)(2,1)}, bf16[512,4096]{1,0:T(8,128)(2,1)}, u32[]{:S(2)}, u32[]{:S(2)}) collective-permute-start(bf16[512,4096]{1,0:T(8,128)(2,1)} %get-tuple-element.107), channel_id=1, source_target_pairs={{0,1},{1,0},{2,3},{3,2},{4,5},{5,4},{6,7},{7,6},{8,9},{9,8},{10,11... | collective-permute-start | bytes 12582920 | tf_op jit(solution)/shard_map/ppermute | solution.py:41
  134.1 15.8 %collective-permute-start.22 = (bf16[256,1024]{1,0:T(8,128)(2,1)}, bf16[256,1024]{1,0:T(8,128)(2,1)S(1)}, u32[]{:S(2)}, u32[]{:S(2)}) collective-permute-start(bf16[256,1024]{1,0:T(8,128)(2,1)} %get-tuple-element.96), channel_id=1, source_target_pairs={{0,4},{1,5},{2,6},{3,7},{4,8},{5,9},{6,10},{7,11},{8,12},{9,13},{1... | collective-permute-start | bytes 1572872 | tf_op jit(solution)/shard_map/ppermute | solution.py:29
  134.1 15.8 %collective-permute-start.21 = (bf16[256,1024]{1,0:T(8,128)(2,1)}, bf16[256,1024]{1,0:T(8,128)(2,1)}, u32[]{:S(2)}, u32[]{:S(2)}) collective-permute-start(bf16[256,1024]{1,0:T(8,128)(2,1)} %get-tuple-element.95), channel_id=1, source_target_pairs={{0,12},{1,13},{2,14},{3,15},{4,0},{5,1},{6,2},{7,3},{8,4},{9,5},{1... | collective-permute-start | bytes 1572872 | tf_op jit(solution)/shard_map/ppermute | solution.py:33
  149.4 26.1 %collective-permute-start.28 = (bf16[512,1024]{1,0:T(8,128)(2,1)}, bf16[512,1024]{1,0:T(8,128)(2,1)S(1)}, u32[]{:S(2)}, u32[]{:S(2)}) collective-permute-start(bf16[512,1024]{1,0:T(8,128)(2,1)} %sum.1), channel_id=1, source_target_pairs={{0,2},{1,3},{2,0},{3,1},{4,6},{5,7},{6,4},{7,5},{8,10},{9,11},{10,... | collective-permute-start | bytes 3145736 | tf_op jit(solution)/shard_map/ppermute | solution.py:37
  149.9 0.9 copy-start.17
  153.2 25.4 %collective-permute-start.27 = (bf16[512,1024]{1,0:T(8,128)(2,1)}, bf16[512,1024]{1,0:T(8,128)(2,1)}, u32[]{:S(2)}, u32[]{:S(2)}) collective-permute-start(bf16[512,1024]{1,0:T(8,128)(2,1)} %get-tuple-element.104), channel_id=1, source_target_pairs={{0,4},{1,5},{2,6},{3,7},{4,8},{5,9},{6,10},{7,11},{8,12},{9,13},{1... | collective-permute-start | bytes 3145736 | tf_op jit(solution)/shard_map/ppermute | solution.py:29
  153.2 25.4 %collective-permute-start.26 = (bf16[512,1024]{1,0:T(8,128)(2,1)}, bf16[512,1024]{1,0:T(8,128)(2,1)}, u32[]{:S(2)}, u32[]{:S(2)}) collective-permute-start(bf16[512,1024]{1,0:T(8,128)(2,1)} %get-tuple-element.103), channel_id=1, source_target_pairs={{0,12},{1,13},{2,14},{3,15},{4,0},{5,1},{6,2},{7,3},{8,4},{9,5},{1... | collective-permute-start | bytes 3145736 | tf_op jit(solution)/shard_map/ppermute | solution.py:33
  155.8 12.6 %collective-permute-start.25 = (bf16[256,1024]{1,0:T(8,128)(2,1)S(1)}, bf16[256,1024]{1,0:T(8,128)(2,1)S(1)}, u32[]{:S(2)}, u32[]{:S(2)}) collective-permute-start(bf16[256,1024]{1,0:T(8,128)(2,1)S(1)} %maximum_select_fusion.2.refs_0_), channel_id=1, source_target_pairs={{0,96},{16,112},{32,0},{48,16},{64,32},{80,48},{96,64},{112,80},{1... | collective-permute-start | bytes 1572872 | tf_op jit(solution)/shard_map/ppermute | solution.py:50
  156.4 13.1 %collective-permute-start.24 = (bf16[256,1024]{1,0:T(8,128)(2,1)S(1)}, bf16[256,1024]{1,0:T(8,128)(2,1)}, u32[]{:S(2)}, u32[]{:S(2)}) collective-permute-start(bf16[256,1024]{1,0:T(8,128)(2,1)S(1)} %maximum_select_fusion.2.refs_0_), channel_id=1, source_target_pairs={{0,32},{16,48},{32,64},{48,80},{64,96},{80,112},{96,0},{112,16},{1... | collective-permute-start | bytes 1572872 | tf_op jit(solution)/shard_map/ppermute | solution.py:50
  168.4 10.2 %copy-start.10 = (bf16[512,1024]{1,0:T(8,128)(2,1)S(1)}, bf16[512,1024]{1,0:T(8,128)(2,1)}, u32[]{:S(2)}) copy-start(bf16[512,1024]{1,0:T(8,128)(2,1)} %get-tuple-element.112) | copy-start | bytes 3145732
  168.4 1.0 copy-start.13
  175.5 3.1 %copy-start.11 = (bf16[512,1024]{1,0:T(8,128)(2,1)}, bf16[512,1024]{1,0:T(8,128)(2,1)S(1)}, u32[]{:S(2)}) copy-start(bf16[512,1024]{1,0:T(8,128)(2,1)S(1)} %collective-permute-done.28) | copy-start | bytes 3145732
  180.3 4.1 %collective-permute-start.29 = (f32[256,1024]{1,0:T(8,128)S(1)}, f32[256,1024]{1,0:T(8,128)S(1)}, u32[]{:S(2)}, u32[]{:S(2)}) collective-permute-start(f32[256,1024]{1,0:T(8,128)S(1)} %add_multiply_fusion), channel_id=1, source_target_pairs={{0,1},{1,0},{2,3},{3,2},{4,5},{5,4},{6,7},{7,6},{8,9},{9,8},{10,11... | collective-permute-start | bytes 3145736 | tf_op jit(solution)/shard_map/ppermute | solution.py:41

commit v4 on v3

--- a/solution.py
+++ b/solution.py
@@ -71,8 +71,8 @@
 
 
 EARLY = [(3, 1), (1, 1), (2, 1)]
-LATE = [(2, 0), (0, 1)]
-LAST = [(3, 0), (1, 0), (0, 0)]
+LATE = [(2, 0), (0, 1), (0, 0)]
+LAST = [(3, 0), (1, 0)]
 AT_EARLY = len(DIRS)
 AT_LATE = AT_EARLY + len(EARLY)
 AT_LAST = AT_LATE + len(LATE)
@@ -494,12 +494,13 @@
     sums = pre_of(factor, pos, x_pair, second, second_offs, sums)
     x_terms = [hold(dec[0], sums[0]), x1, x2, x3]
     other = add(*[share_of(a, 1 - low) for a in x_terms]).astype(BF16)
-    low_got = to_l(hold(other, a21, b21, w31, w11))
+    mine = add(*[share_of(a, low) for a in x_terms])
+    outer_share = lax.dynamic_slice_in_dim(outer_weight, replica * share, share, 1)
+    outer_share = hold(outer_share, sums[0])
+    low_got = to_l(hold(other, mine, outer_share, a21, b21, w31, w11))
     third, third_offs = [w31, w11, a21, b21], offs((3, 1), (1, 1), (2, 1), (2, 1, 1))
     slopes = pre_of(factor, pos, x_pair, third, third_offs, sums, cots)
-    mine = [share_of(a, low) for a in x_terms]
-    average = add(*mine, hold(low_got, slopes[0])) / (NX * NL)
-    outer_share = lax.dynamic_slice_in_dim(outer_weight, replica * share, share, 1)
+    average = (mine + hold(low_got, slopes[0]).astype(F32)) / (NX * NL)
     new_momentum = 0.9 * momentum + average
     new_outer = outer_share - 0.7 * (average + 0.9 * new_momentum)
     inner_share = new_outer.astype(BF16)
@@ -515,17 +516,17 @@
     r31, r11, r21 = to_zm(g31), to_zp(g11), to_y(g21)
     late_slopes = (hold(slopes[0], inner_pair), slopes[1])
     pieces, piece_offs = first + second + third, first_offs + second_offs + third_offs
-    g20, g01, part = late_of(pos, x_pair, late_slopes, piece_offs, pieces)
+    g20, g01, g00, part = late_of(pos, x_pair, late_slopes, piece_offs, pieces)
 
     ha20, hb20 = halves_of(g20, hold(r21, r31, r11, e2))
     ra20, rb20 = to_zm(ha20), to_zp(hb20)
     part_got = to_core(hold(part, ha20))
-    last_slopes = (hold(slopes[0], ha20, hb20), slopes[1])
-    g30, g10, g00 = wgrad_of(pos, AT_LAST, (False,) * 3, x_pair, last_slopes)
-    s01 = sum_of(pos, [g01, hold(r31, g30), r11], rows, BF16)
+    s01 = sum_of(pos, [g01, hold(r31, ha20, hb20), r11], rows, BF16)
     t01 = to_y(s01)
-
-    s30, s10 = fold(g30, ra20, g10, hold(rb20, s01))
+    last_slopes = (hold(slopes[0], ha20, hb20, s01), slopes[1])
+    g30, g10 = wgrad_of(pos, AT_LAST, (False,) * 2, x_pair, last_slopes)
+
+    s30, s10 = fold(g30, ra20, g10, rb20)
     t30, t10 = to_zm(s30), to_zp(s10)
     e1, e3 = [to_x(hold(inner_pair, s30), dx) for dx in (1, 3)]
     input_grad = igrad_of(

time: 186 us -> 186 us (level)
  waiting for transfers between devices: 36.1 us -> 33.3 us
    ppermute x5, waiting for transfers between devices: 18.7 us -> 14 us  [to_y(): return lax.ppermute(a, 'shard', shard_perm(0, 1, 0))]
  transfers between devices with their start and end apart: 30 -> 30, of which waited for: 12 -> 9; matrix products, arithmetic and copies ran while one was open for 2% -> 3% of each run, Pallas kernels for 46% -> 46%
where the time goes in v4:
time: 186 us; the launch traced here: 185 us
  Pallas kernels  88.4 us (48%)
  starting transfers between devices  45.7 us (25%)
  waiting for transfers between devices  33.3 us (18%)
  other arithmetic  10.8 us (6%)
  local copies, waits for them, and re-layouts  6.29 us (3%)
    pallas_call x3, Pallas kernels, pre_of(): pl.pallas_call(functools.partial(pre_kernel, factor, n, sums is not None,...  25.1 us
    pallas_call x1, Pallas kernels, late_of(): pl.pallas_call(functools.partial(late_kernel, n, offs, rows), grid_spec=p...  16.6 us
    ppermute x6, starting transfers between devices, to_zm(): return lax.ppermute(a, 'shard', shard_perm(-1, 0, 0))  15.6 us
    pallas_call x2, Pallas kernels, wgrad_of(): pl.pallas_call(functools.partial(wgrad_kernel, halves), grid_spec=pltpu.P...  15.1 us
    ppermute x5, waiting for transfers between devices, to_y(): return lax.ppermute(a, 'shard', shard_perm(0, 1, 0))  14 us
    pallas_call x1, Pallas kernels, igrad_of(): pl.pallas_call(functools.partial(igrad_kernel, factor, offs, feats // (NZ...  11.1 us
    ppermute x6, waiting for transfers between devices, to_zm(): return lax.ppermute(a, 'shard', shard_perm(-1, 0, 0))  10.5 us
    ppermute x5, starting transfers between devices, to_core(): return lax.ppermute(a, 'shard', shard_perm(0, 0, 1))  10.4 us
  transfers between devices with their start and end apart: 30, of which 9 were waited for; matrix products, arithmetic and copies ran while one was open for 3% of the time, Pallas kernels for 46%

profile of v4, /device:TPU:1, one launch (start us, length us, event | category | flops | bytes accessed | tf_op | source)
XLA Modules:
  0.0 185.4 jit_solution(791922905131683859)
XLA Ops:
  0.7 1.3 dynamic-slice_bitcast_fusion.1
  1.9 1.5 collective-permute-start
  3.4 1.5 collective-permute-done
  5.0 0.5 maximum_select_fusion.1.refs_0_
  5.5 0.5 collective-permute-start.4
  5.9 0.1 collective-permute-start.5
  6.1 3.8 %collective-permute-start.3 = (bf16[512,1024]{1,0:T(8,128)(2,1)S(1)}, bf16[512,1024]{1,0:T(8,128)(2,1)S(1)}, u32[]{:S(2)}, u32[]{:S(2)}) collective-permute-start(bf16[512,1024]{1,0:T(8,128)(2,1)S(1)} %maximum_select_fusion.1.refs_0_), channel_id=1, source_target_pairs={{0,12},{1,13},{2,14},{3,15},{4,0},{5,1},{6,2},{7,3},{8,4},{9,5},{1... | collective-permute-start | bytes 3145736 | tf_op jit(solution)/shard_map/ppermute | solution.py:33
  9.9 2.9 %collective-permute-start.1 = (bf16[512,1024]{1,0:T(8,128)(2,1)S(1)}, bf16[512,1024]{1,0:T(8,128)(2,1)}, u32[]{:S(2)}, u32[]{:S(2)}) collective-permute-start(bf16[512,1024]{1,0:T(8,128)(2,1)S(1)} %maximum_select_fusion.1.refs_0_), channel_id=1, source_target_pairs={{0,2},{1,3},{2,0},{3,1},{4,6},{5,7},{6,4},{7,5},{8,10},{9,11},{10,... | collective-permute-start | bytes 3145736 | tf_op jit(solution)/shard_map/ppermute | solution.py:37
  12.8 0.6 stack.55.off_ref.pos_ref.blk_ref.s_ref
  13.5 6.8 %decode.1 = (bf16[256,1024]{1,0:T(8,128)(2,1)}, bf16[256,1024]{1,0:T(8,128)(2,1)}, bf16[256,1024]{1,0:T(8,128)(2,1)}, bf16[256,1024]{1,0:T(8,128)(2,1)}) custom-call(s32[19]{0:T(128)} %stack.55.off_ref.pos_ref.blk_ref.s_ref, f32[256,4096]{1,0:T(8,128)} %outer_ref, f32[1,256,4096]{2,1,0:T(8,128)} %inner_ref.1), custom_call_target="tpu_custom_call" | custom-call | flops 3145728 | bytes 3145728 | tf_op jit(solution)/shard_map/decode/pallas_call | solution.py:124
  20.3 1.3 collective-permute-start.6
  21.6 10.5 %collective-permute-done.3.refs_2_ = bf16[512,1024]{1,0:T(8,128)(2,1)S(1)} collective-permute-done((bf16[512,1024]{1,0:T(8,128)(2,1)S(1)}, bf16[512,1024]{1,0:T(8,128)(2,1)S(1)}, u32[]{:S(2)}, u32[]{:S(2)}) %collective-permute-start.3) | collective-permute-done | bytes 1048608 | tf_op jit(solution)/shard_map/ppermute | solution.py:33
  32.1 3.5 %collective-permute-done.1.refs_3_ = bf16[512,1024]{1,0:T(8,128)(2,1)} collective-permute-done((bf16[512,1024]{1,0:T(8,128)(2,1)S(1)}, bf16[512,1024]{1,0:T(8,128)(2,1)}, u32[]{:S(2)}, u32[]{:S(2)}) %collective-permute-start.1) | collective-permute-done | bytes 1048608 | tf_op jit(solution)/shard_map/ppermute | solution.py:37
  35.6 0.8 copy-done.15
  36.4 1.3 collective-permute-start.9
  37.7 0.1 collective-permute-done.2.refs_1_
  37.8 0.3 collective-permute-start.7
  38.0 2.7 %collective-permute-start.13 = (bf16[256,1024]{1,0:T(8,128)(2,1)}, bf16[256,1024]{1,0:T(8,128)(2,1)}, u32[]{:S(2)}, u32[]{:S(2)}) collective-permute-start(bf16[256,1024]{1,0:T(8,128)(2,1)} %get-tuple-element.79), channel_id=1, source_target_pairs={{0,64},{16,80},{32,96},{48,112},{64,0},{80,16},{96,32},{112,48},{1... | collective-permute-start | bytes 1572872 | tf_op jit(solution)/shard_map/ppermute | solution.py:50
  40.8 9.6 %pre.2 = (f32[512,1024]{1,0:T(8,128)}, f32[512,1024]{1,0:T(8,128)}) custom-call(s32[19]{0:T(128)} %stack.55.off_ref.pos_ref.blk_ref.s_ref, bf16[512,1024]{1,0:T(8,128)(2,1)} %copy-done, bf16[512,1024]{1,0:T(8,128)(2,1)} %copy-done.2, bf16[512,1024]{1,0:T(8,128)(2,1)} %copy-done.1, bf16[512,1024]{1,0:T(8,128)(2,1)} %collective-permute-done.1.refs_3_, ...), custom_call_target="tpu_custom_call" | custom-call | flops 1288490240 | bytes 3774873 | tf_op jit(solution)/shard_map/pre/pallas_call | solution.py:261
  50.4 0.2 collective-permute-start.8
  50.5 2.6 %collective-permute-start.10 = (bf16[512,1024]{1,0:T(8,128)(2,1)}, bf16[512,1024]{1,0:T(8,128)(2,1)S(1)}, u32[]{:S(2)}, u32[]{:S(2)}) collective-permute-start(bf16[512,1024]{1,0:T(8,128)(2,1)} %collective-permute-done.1.refs_3_), channel_id=1, source_target_pairs={{0,12},{1,13},{2,14},{3,15},{4,0},{5,1},{6,2},{7,3},{8,4},{9,5},{1... | collective-permute-start | bytes 3145736 | tf_op jit(solution)/shard_map/ppermute | solution.py:33
  53.1 2.8 %collective-permute-start.14 = (bf16[256,1024]{1,0:T(8,128)(2,1)}, bf16[256,1024]{1,0:T(8,128)(2,1)}, u32[]{:S(2)}, u32[]{:S(2)}) collective-permute-start(bf16[256,1024]{1,0:T(8,128)(2,1)} %get-tuple-element.81), channel_id=1, source_target_pairs={{0,96},{16,112},{32,0},{48,16},{64,32},{80,48},{96,64},{112,80},{1... | collective-permute-start | bytes 1572872 | tf_op jit(solution)/shard_map/ppermute | solution.py:50
  55.9 2.1 %collective-permute-start.11 = (bf16[256,1024]{1,0:T(8,128)(2,1)}, bf16[256,1024]{1,0:T(8,128)(2,1)S(1)}, u32[]{:S(2)}, u32[]{:S(2)}) collective-permute-start(bf16[256,1024]{1,0:T(8,128)(2,1)} %collective-permute-done.7.refs_0_.refs_4_), channel_id=1, source_target_pairs={{0,2},{1,3},{2,0},{3,1},{4,6},{5,7},{6,4},{7,5},{8,10},{9,11},{10,... | collective-permute-start | bytes 1572872 | tf_op jit(solution)/shard_map/ppermute | solution.py:37
  58.0 0.9 collective-permute-start.12
  58.9 1.1 constant_dynamic-slice_fusion
  60.0 5.5 %pre.3 = (f32[512,1024]{1,0:T(8,128)}, f32[512,1024]{1,0:T(8,128)}) custom-call(s32[19]{0:T(128)} %stack.55.off_ref.pos_ref.blk_ref.s_ref, bf16[256,1024]{1,0:T(8,128)(2,1)} %collective-permute-done.7.refs_0_.refs_4_, bf16[256,1024]{1,0:T(8,128)(2,1)} %collective-permute-done.9.refs_1_.refs_5_, bf16[512,4096]{1,0:T(8,128)(2,1)} %xo_ref.5, ...), custom_call_target="tpu_custom_call" | custom-call | flops 322122560 | bytes 1887436 | tf_op jit(solution)/shard_map/pre/pallas_call | solution.py:261
  65.5 2.7 %add_convert_fusion = (bf16[256,512]{1,0:T(8,128)(2,1)}, f32[256,512]{1,0:T(8,128)}) fusion(bf16[256,1024]{1,0:T(8,128)(2,1)} %collective-permute-done.14, s32[]{:T(128)S(6)} %select_n.152, bf16[256,1024]{1,0:T(8,128)(2,1)} %collective-permute-done.13, bf16[256,1024]{1,0:T(8,128)(2,1)} %copy-done.15, bf16[256,1024]{1,0:T(8,128)(2,1)} %get-tuple-element.77, ...), kind=kLoop, calls=%fused_computation.8 | loop fusion | flops 1966080 | bytes 2883592 | tf_op jit(solution)/shard_map/convert_element_type | solution.py:496
  68.2 10.5 %collective-permute-done.12.refs_3_.refs_9_ = bf16[256,1024]{1,0:T(8,128)(2,1)S(1)} collective-permute-done((bf16[256,1024]{1,0:T(8,128)(2,1)}, bf16[256,1024]{1,0:T(8,128)(2,1)S(1)}, u32[]{:S(2)}, u32[]{:S(2)}) %collective-permute-start.12) | collective-permute-done | bytes 524320 | tf_op jit(solution)/shard_map/ppermute | solution.py:37
  78.7 0.0 copy-start.4
  78.7 0.7 collective-permute-start.15
  79.3 0.1 copy-done.6
  79.5 0.3 copy-done.3
  79.8 0.3 copy-done.4
  80.1 10.0 %slope.1 = (bf16[512,1024]{1,0:T(8,128)(2,1)}, bf16[512,1024]{1,0:T(8,128)(2,1)}) custom-call(s32[19]{0:T(128)} %stack.55.off_ref.pos_ref.blk_ref.s_ref, bf16[512,1024]{1,0:T(8,128)(2,1)} %copy-done.3, bf16[512,1024]{1,0:T(8,128)(2,1)} %copy-done.4, bf16[256,1024]{1,0:T(8,128)(2,1)} %copy-done.5, bf16[256,1024]{1,0:T(8,128)(2,1)} %copy-done.6, ...), custom_call_target="tpu_custom_call" | custom-call | flops 966367616 | bytes 3145728 | tf_op jit(solution)/shard_map/slope/pallas_call | solution.py:261
  90.2 2.4 %fusion = (bf16[256,512]{1,0:T(8,128)(2,1)S(1)}, f32[256,512]{1,0:T(8,128)}, f32[256,512]{1,0:T(8,128)}) fusion(f32[256,512]{1,0:T(8,128)S(1)} %constant_dynamic-slice_fusion, f32[256,512]{1,0:T(8,128)} %get-tuple-element.117, bf16[256,512]{1,0:T(8,128)(2,1)S(1)} %collective-permute-done.15, f32[256,512]{1,0:T(8,128)} %param.11), kind=kLoop, calls=%fused_computation.13 | loop fusion | flops 1310720 | bytes 3145728 | tf_op jit(solution)/shard_map/convert_element_type | solution.py:506
  92.5 0.4 collective-permute-start.16
  92.9 8.4 %wgrad.2 = (bf16[512,1024]{1,0:T(8,128)(2,1)}, bf16[512,1024]{1,0:T(8,128)(2,1)}, bf16[512,1024]{1,0:T(8,128)(2,1)}) custom-call(s32[19]{0:T(128)} %stack.55.off_ref.pos_ref.blk_ref.s_ref, bf16[512,4096]{1,0:T(8,128)(2,1)} %xo_ref.5, bf16[512,4096]{1,0:T(8,128)(2,1)} %collective-permute-done.4.refs_8_.refs_9_.refs_10_.refs_11_.refs_4_.refs_5_.xp_ref, ...), custom_call_target="tpu_custom_call" | custom-call | flops 966367616 | bytes 1887436 | tf_op jit(solution)/shard_map/wgrad/pallas_call | solution.py:302
  101.4 2.8 %collective-permute-start.17 = (bf16[512,1024]{1,0:T(8,128)(2,1)}, bf16[512,1024]{1,0:T(8,128)(2,1)}, u32[]{:S(2)}, u32[]{:S(2)}) collective-permute-start(bf16[512,1024]{1,0:T(8,128)(2,1)} %get-tuple-element.90), channel_id=1, source_target_pairs={{0,2},{1,3},{2,0},{3,1},{4,6},{5,7},{6,4},{7,5},{8,10},{9,11},{10,... | collective-permute-start | bytes 3145736 | tf_op jit(solution)/shard_map/ppermute | solution.py:37
  104.2 2.6 %collective-permute-start.18 = (bf16[512,1024]{1,0:T(8,128)(2,1)}, bf16[512,1024]{1,0:T(8,128)(2,1)S(1)}, u32[]{:S(2)}, u32[]{:S(2)}) collective-permute-start(bf16[512,1024]{1,0:T(8,128)(2,1)} %get-tuple-element.92), channel_id=1, source_target_pairs={{0,12},{1,13},{2,14},{3,15},{4,0},{5,1},{6,2},{7,3},{8,4},{9,5},{1... | collective-permute-start | bytes 3145736 | tf_op jit(solution)/shard_map/ppermute | solution.py:33
  106.8 0.1 maximum_select_fusion.2.refs_0_
  106.9 0.6 collective-permute-start.20
  107.5 16.6 %late.1 = (bf16[512,1024]{1,0:T(8,128)(2,1)}, bf16[512,1024]{1,0:T(8,128)(2,1)}, bf16[512,1024]{1,0:T(8,128)(2,1)}, bf16[512,4096]{1,0:T(8,128)(2,1)}) custom-call(s32[19]{0:T(128)} %stack.55.off_ref.pos_ref.blk_ref.s_ref, bf16[512,4096]{1,0:T(8,128)(2,1)} %xo_ref.5, ...), custom_call_target="tpu_custom_call" | custom-call | flops 2254857728 | bytes 7549747 | tf_op jit(solution)/shard_map/late/pallas_call | solution.py:355
  124.2 3.7 %halves.1 = (bf16[256,1024]{1,0:T(8,128)(2,1)}, bf16[256,1024]{1,0:T(8,128)(2,1)}) custom-call(bf16[512,1024]{1,0:T(8,128)(2,1)} %get-tuple-element.89.a_ref, bf16[512,1024]{1,0:T(8,128)(2,1)} %collective-permute-done.17.b_ref), custom_call_target="tpu_custom_call" | custom-call | flops 157286 | bytes 943718 | tf_op jit(solution)/shard_map/halves/pallas_call | solution.py:208
  127.9 6.5 %collective-permute-start.23 = (bf16[512,4096]{1,0:T(8,128)(2,1)}, bf16[512,4096]{1,0:T(8,128)(2,1)}, u32[]{:S(2)}, u32[]{:S(2)}) collective-permute-start(bf16[512,4096]{1,0:T(8,128)(2,1)} %get-tuple-element.107), channel_id=1, source_target_pairs={{0,1},{1,0},{2,3},{3,2},{4,5},{5,4},{6,7},{7,6},{8,9},{9,8},{10,11... | collective-permute-start | bytes 12582920 | tf_op jit(solution)/shard_map/ppermute | solution.py:41
  134.4 2.7 %collective-permute-start.21 = (bf16[256,1024]{1,0:T(8,128)(2,1)}, bf16[256,1024]{1,0:T(8,128)(2,1)}, u32[]{:S(2)}, u32[]{:S(2)}) collective-permute-start(bf16[256,1024]{1,0:T(8,128)(2,1)} %get-tuple-element.96), channel_id=1, source_target_pairs={{0,12},{1,13},{2,14},{3,15},{4,0},{5,1},{6,2},{7,3},{8,4},{9,5},{1... | collective-permute-start | bytes 1572872 | tf_op jit(solution)/shard_map/ppermute | solution.py:33
  137.1 3.5 %sum.1 = bf16[512,1024]{1,0:T(8,128)(2,1)} custom-call(s32[19]{0:T(128)} %stack.55.off_ref.pos_ref.blk_ref.s_ref, bf16[512,1024]{1,0:T(8,128)(2,1)} %get-tuple-element.98.refs_0_, bf16[512,1024]{1,0:T(8,128)(2,1)} %copy-done.9, bf16[512,1024]{1,0:T(8,128)(2,1)} %copy-done.8), custom_call_target="tpu_custom_call" | custom-call | flops 471859 | bytes 1258291 | tf_op jit(solution)/shard_map/sum/pallas_call | solution.py:156
  140.6 0.3 collective-permute-start.28
  140.9 6.7 %wgrad.3 = (bf16[512,1024]{1,0:T(8,128)(2,1)}, bf16[512,1024]{1,0:T(8,128)(2,1)}) custom-call(s32[19]{0:T(128)} %stack.55.off_ref.pos_ref.blk_ref.s_ref, bf16[512,4096]{1,0:T(8,128)(2,1)} %xo_ref.5, bf16[512,4096]{1,0:T(8,128)(2,1)} %collective-permute-done.4.refs_8_.refs_9_.refs_10_.refs_11_.refs_4_.refs_5_.xp_ref, ...), custom_call_target="tpu_custom_call" | custom-call | flops 644245120 | bytes 1258291 | tf_op jit(solution)/shard_map/wgrad/pallas_call | solution.py:302
  147.6 1.8 collective-permute-done.22.b_ref
  149.4 0.8 copy-done.16
  150.2 2.4 %fold.1 = (bf16[512,1024]{1,0:T(8,128)(2,1)}, bf16[512,1024]{1,0:T(8,128)(2,1)}) custom-call(bf16[512,1024]{1,0:T(8,128)(2,1)} %get-tuple-element.101.up_ref, bf16[256,1024]{1,0:T(8,128)(2,1)} %collective-permute-done.21.a_ref, bf16[512,1024]{1,0:T(8,128)(2,1)} %get-tuple-element.102.low_ref, ...), custom_call_target="tpu_custom_call", output_to_operand_aliasing={{0}: (0, {}), {1}: (2, {})} | custom-call | flops 157286 | bytes 943718 | tf_op jit(solution)/shard_map/fold/pallas_call | solution.py:180
  152.6 0.0 collective-permute-start.27
  152.6 2.7 %collective-permute-start.26 = (bf16[512,1024]{1,0:T(8,128)(2,1)}, bf16[512,1024]{1,0:T(8,128)(2,1)}, u32[]{:S(2)}, u32[]{:S(2)}) collective-permute-start(bf16[512,1024]{1,0:T(8,128)(2,1)} %get-tuple-element.103), channel_id=1, source_target_pairs={{0,12},{1,13},{2,14},{3,15},{4,0},{5,1},{6,2},{7,3},{8,4},{9,5},{1... | collective-permute-start | bytes 3145736 | tf_op jit(solution)/shard_map/ppermute | solution.py:33
  155.3 1.7 collective-permute-start.25
  157.1 11.1 %igrad.1 = bf16[512,4096]{1,0:T(8,128)(2,1)} custom-call(s32[19]{0:T(128)} %stack.55.off_ref.pos_ref.blk_ref.s_ref, bf16[512,1024]{1,0:T(8,128)(2,1)} %get-tuple-element.105.so_ref.s_ref, bf16[512,1024]{1,0:T(8,128)(2,1)} %copy-done, bf16[512,1024]{1,0:T(8,128)(2,1)} %copy-done.2, bf16[512,1024]{1,0:T(8,128)(2,1)} %copy-done.1, ...), custom_call_target="tpu_custom_call" | custom-call | flops 1288490240 | bytes 3774873 | tf_op jit(solution)/shard_map/igrad/pallas_call | solution.py:395
  168.2 2.0 %collective-permute-done.24.refs_1_ = bf16[256,1024]{1,0:T(8,128)(2,1)S(1)} collective-permute-done((bf16[256,1024]{1,0:T(8,128)(2,1)S(1)}, bf16[256,1024]{1,0:T(8,128)(2,1)S(1)}, u32[]{:S(2)}, u32[]{:S(2)}) %collective-permute-start.24) | collective-permute-done | bytes 524320 | tf_op jit(solution)/shard_map/ppermute | solution.py:50
  170.2 0.8 copy-done.14
  170.9 4.1 %place.1 = bf16[256,4096]{1,0:T(8,128)(2,1)} custom-call(s32[19]{0:T(128)} %stack.55.off_ref.pos_ref.blk_ref.s_ref, bf16[256,1024]{1,0:T(8,128)(2,1)} %copy-done.7, bf16[256,1024]{1,0:T(8,128)(2,1)} %copy-done.14, bf16[256,1024]{1,0:T(8,128)(2,1)} %copy-done.12, bf16[256,1024]{1,0:T(8,128)(2,1)} %copy-done.13), custom_call_target="tpu_custom_call" | custom-call | bytes 1258291 | tf_op jit(solution)/shard_map/place/pallas_call | solution.py:432
  175.0 3.0 %collective-permute-done.27 = bf16[512,1024]{1,0:T(8,128)(2,1)} collective-permute-done((bf16[512,1024]{1,0:T(8,128)(2,1)}, bf16[512,1024]{1,0:T(8,128)(2,1)}, u32[]{:S(2)}, u32[]{:S(2)}) %collective-permute-start.27) | collective-permute-done | bytes 1048608 | tf_op jit(solution)/shard_map/ppermute | solution.py:29
  178.1 1.7 add_multiply_fusion
  179.8 1.8 collective-permute-start.29
  181.5 1.9 %multiply_bitcast_fusion = f32[1,256,1024]{2,1,0:T(8,128)S(1)} fusion(bf16[512,1024]{1,0:T(8,128)(2,1)} %copy-done.11, s32[]{:T(128)S(6)} %select_n.156, bf16[512,1024]{1,0:T(8,128)(2,1)} %collective-permute-done.27, bf16[512,1024]{1,0:T(8,128)(2,1)} %collective-permute-done.26, bf16[512,1024]{1,0:T(8,128)(2,1)} %get-tuple-element.112), kind=kLoop, calls=%fused_computation.2 | loop fusion | flops 2097152 | bytes 3145732 | tf_op jit(solution)/shard_map/concatenate | solution.py:417
  183.4 0.4 collective-permute-done.29
  183.8 1.6 maximum_select_fusion
  (54 shorter events, 0.2 us)
Async XLA Ops:
  1.9 3.0 %collective-permute-start = (bf16[256,1024]{1,0:T(8,128)(2,1)S(1)}, bf16[256,1024]{1,0:T(8,128)(2,1)S(1)}, u32[]{:S(2)}, u32[]{:S(2)}) collective-permute-start(bf16[256,1024]{1,0:T(8,128)(2,1)S(1)} %get-tuple-element.119), channel_id=1, source_target_pairs={{0,1},{1,0},{2,3},{3,2},{4,5},{5,4},{6,7},{7,6},{8,9},{9,8},{10,11... | collective-permute-start | bytes 1572872 | tf_op jit(solution)/shard_map/ppermute | solution.py:41
  5.5 14.8 %copy-start = (bf16[512,1024]{1,0:T(8,128)(2,1)}, bf16[512,1024]{1,0:T(8,128)(2,1)S(1)}, u32[]{:S(2)}) copy-start(bf16[512,1024]{1,0:T(8,128)(2,1)S(1)} %maximum_select_fusion.1.refs_0_) | copy-start | bytes 3145732
  5.5 14.8 %collective-permute-start.4 = (bf16[512,4096]{1,0:T(8,128)(2,1)}, bf16[512,4096]{1,0:T(8,128)(2,1)}, u32[]{:S(2)}, u32[]{:S(2)}) collective-permute-start(bf16[512,4096]{1,0:T(8,128)(2,1)} %xo_ref.5), channel_id=1, source_target_pairs={{0,1},{1,0},{2,3},{3,2},{4,5},{5,4},{6,7},{7,6},{8,9},{9,8},{10,11... | collective-permute-start | bytes 12582920 | tf_op jit(solution)/shard_map/ppermute | solution.py:41
  5.9 14.4 %collective-permute-start.5 = (bf16[512,2048]{1,0:T(8,128)(2,1)}, bf16[512,2048]{1,0:T(8,128)(2,1)}, u32[]{:S(2)}, u32[]{:S(2)}) collective-permute-start(bf16[512,2048]{1,0:T(8,128)(2,1)} %refs_14_.1), channel_id=1, source_target_pairs={{0,1},{1,0},{2,3},{3,2},{4,5},{5,4},{6,7},{7,6},{8,9},{9,8},{10,11... | collective-permute-start | bytes 6291464 | tf_op jit(solution)/shard_map/ppermute | solution.py:41
  6.1 26.0 %collective-permute-start.3 = (bf16[512,1024]{1,0:T(8,128)(2,1)S(1)}, bf16[512,1024]{1,0:T(8,128)(2,1)S(1)}, u32[]{:S(2)}, u32[]{:S(2)}) collective-permute-start(bf16[512,1024]{1,0:T(8,128)(2,1)S(1)} %maximum_select_fusion.1.refs_0_), channel_id=1, source_target_pairs={{0,12},{1,13},{2,14},{3,15},{4,0},{5,1},{6,2},{7,3},{8,4},{9,5},{1... | collective-permute-start | bytes 3145736 | tf_op jit(solution)/shard_map/ppermute | solution.py:33
  9.9 25.7 %collective-permute-start.1 = (bf16[512,1024]{1,0:T(8,128)(2,1)S(1)}, bf16[512,1024]{1,0:T(8,128)(2,1)}, u32[]{:S(2)}, u32[]{:S(2)}) collective-permute-start(bf16[512,1024]{1,0:T(8,128)(2,1)S(1)} %maximum_select_fusion.1.refs_0_), channel_id=1, source_target_pairs={{0,2},{1,3},{2,0},{3,1},{4,6},{5,7},{6,4},{7,5},{8,10},{9,11},{10,... | collective-permute-start | bytes 3145736 | tf_op jit(solution)/shard_map/ppermute | solution.py:37
  12.8 24.9 %collective-permute-start.2 = (bf16[512,1024]{1,0:T(8,128)(2,1)S(1)}, bf16[512,1024]{1,0:T(8,128)(2,1)S(1)}, u32[]{:S(2)}, u32[]{:S(2)}) collective-permute-start(bf16[512,1024]{1,0:T(8,128)(2,1)S(1)} %maximum_select_fusion.1.refs_0_), channel_id=1, source_target_pairs={{0,4},{1,5},{2,6},{3,7},{4,8},{5,9},{6,10},{7,11},{8,12},{9,13},{1... | collective-permute-start | bytes 3145736 | tf_op jit(solution)/shard_map/ppermute | solution.py:29
  20.3 15.2 %collective-permute-start.6 = (bf16[256,1024]{1,0:T(8,128)(2,1)}, bf16[256,1024]{1,0:T(8,128)(2,1)S(1)}, u32[]{:S(2)}, u32[]{:S(2)}) collective-permute-start(bf16[256,1024]{1,0:T(8,128)(2,1)} %get-tuple-element.65), channel_id=1, source_target_pairs={{0,32},{16,48},{32,64},{48,80},{64,96},{80,112},{96,0},{112,16},{1... | collective-permute-start | bytes 1572872 | tf_op jit(solution)/shard_map/ppermute | solution.py:50
  32.1 8.7 %copy-start.1 = (bf16[512,1024]{1,0:T(8,128)(2,1)}, bf16[512,1024]{1,0:T(8,128)(2,1)S(1)}, u32[]{:S(2)}) copy-start(bf16[512,1024]{1,0:T(8,128)(2,1)S(1)} %collective-permute-done.3.refs_2_) | copy-start | bytes 3145732
  35.6 0.8 copy-start.15
  36.4 14.0 %collective-permute-start.9 = (bf16[256,1024]{1,0:T(8,128)(2,1)S(1)}, bf16[256,1024]{1,0:T(8,128)(2,1)}, u32[]{:S(2)}, u32[]{:S(2)}) collective-permute-start(bf16[256,1024]{1,0:T(8,128)(2,1)S(1)} %slice.7), channel_id=1, source_target_pairs={{0,12},{1,13},{2,14},{3,15},{4,0},{5,1},{6,2},{7,3},{8,4},{9,5},{1... | collective-permute-start | bytes 1572872 | tf_op jit(solution)/shard_map/ppermute | solution.py:33
  37.7 3.0 %copy-start.2 = (bf16[512,1024]{1,0:T(8,128)(2,1)}, bf16[512,1024]{1,0:T(8,128)(2,1)S(1)}, u32[]{:S(2)}) copy-start(bf16[512,1024]{1,0:T(8,128)(2,1)S(1)} %collective-permute-done.2.refs_1_) | copy-start | bytes 3145732
  37.8 12.6 %collective-permute-start.7 = (bf16[256,1024]{1,0:T(8,128)(2,1)S(1)}, bf16[256,1024]{1,0:T(8,128)(2,1)}, u32[]{:S(2)}, u32[]{:S(2)}) collective-permute-start(bf16[256,1024]{1,0:T(8,128)(2,1)S(1)} %slice.6), channel_id=1, source_target_pairs={{0,4},{1,5},{2,6},{3,7},{4,8},{5,9},{6,10},{7,11},{8,12},{9,13},{1... | collective-permute-start | bytes 1572872 | tf_op jit(solution)/shard_map/ppermute | solution.py:29
  38.0 19.9 %collective-permute-start.13 = (bf16[256,1024]{1,0:T(8,128)(2,1)}, bf16[256,1024]{1,0:T(8,128)(2,1)}, u32[]{:S(2)}, u32[]{:S(2)}) collective-permute-start(bf16[256,1024]{1,0:T(8,128)(2,1)} %get-tuple-element.79), channel_id=1, source_target_pairs={{0,64},{16,80},{32,96},{48,112},{64,0},{80,16},{96,32},{112,48},{1... | collective-permute-start | bytes 1572872 | tf_op jit(solution)/shard_map/ppermute | solution.py:50
  50.4 28.3 %collective-permute-start.8 = (bf16[512,1024]{1,0:T(8,128)(2,1)}, bf16[512,1024]{1,0:T(8,128)(2,1)S(1)}, u32[]{:S(2)}, u32[]{:S(2)}) collective-permute-start(bf16[512,1024]{1,0:T(8,128)(2,1)} %collective-permute-done.1.refs_3_), channel_id=1, source_target_pairs={{0,4},{1,5},{2,6},{3,7},{4,8},{5,9},{6,10},{7,11},{8,12},{9,13},{1... | collective-permute-start | bytes 3145736 | tf_op jit(solution)/shard_map/ppermute | solution.py:29
  50.5 28.1 %collective-permute-start.10 = (bf16[512,1024]{1,0:T(8,128)(2,1)}, bf16[512,1024]{1,0:T(8,128)(2,1)S(1)}, u32[]{:S(2)}, u32[]{:S(2)}) collective-permute-start(bf16[512,1024]{1,0:T(8,128)(2,1)} %collective-permute-done.1.refs_3_), channel_id=1, source_target_pairs={{0,12},{1,13},{2,14},{3,15},{4,0},{5,1},{6,2},{7,3},{8,4},{9,5},{1... | collective-permute-start | bytes 3145736 | tf_op jit(solution)/shard_map/ppermute | solution.py:33
  53.1 12.4 %collective-permute-start.14 = (bf16[256,1024]{1,0:T(8,128)(2,1)}, bf16[256,1024]{1,0:T(8,128)(2,1)}, u32[]{:S(2)}, u32[]{:S(2)}) collective-permute-start(bf16[256,1024]{1,0:T(8,128)(2,1)} %get-tuple-element.81), channel_id=1, source_target_pairs={{0,96},{16,112},{32,0},{48,16},{64,32},{80,48},{96,64},{112,80},{1... | collective-permute-start | bytes 1572872 | tf_op jit(solution)/shard_map/ppermute | solution.py:50
  55.9 12.3 %collective-permute-start.11 = (bf16[256,1024]{1,0:T(8,128)(2,1)}, bf16[256,1024]{1,0:T(8,128)(2,1)S(1)}, u32[]{:S(2)}, u32[]{:S(2)}) collective-permute-start(bf16[256,1024]{1,0:T(8,128)(2,1)} %collective-permute-done.7.refs_0_.refs_4_), channel_id=1, source_target_pairs={{0,2},{1,3},{2,0},{3,1},{4,6},{5,7},{6,4},{7,5},{8,10},{9,11},{10,... | collective-permute-start | bytes 1572872 | tf_op jit(solution)/shard_map/ppermute | solution.py:37
  58.0 20.7 %collective-permute-start.12 = (bf16[256,1024]{1,0:T(8,128)(2,1)}, bf16[256,1024]{1,0:T(8,128)(2,1)S(1)}, u32[]{:S(2)}, u32[]{:S(2)}) collective-permute-start(bf16[256,1024]{1,0:T(8,128)(2,1)} %collective-permute-done.9.refs_1_.refs_5_), channel_id=1, source_target_pairs={{0,2},{1,3},{2,0},{3,1},{4,6},{5,7},{6,4},{7,5},{8,10},{9,11},{10,... | collective-permute-start | bytes 1572872 | tf_op jit(solution)/shard_map/ppermute | solution.py:37
  68.2 11.2 %copy-start.5 = (bf16[256,1024]{1,0:T(8,128)(2,1)}, bf16[256,1024]{1,0:T(8,128)(2,1)S(1)}, u32[]{:S(2)}) copy-start(bf16[256,1024]{1,0:T(8,128)(2,1)S(1)} %collective-permute-done.11.refs_2_.refs_8_) | copy-start | bytes 1572868
  78.7 0.8 copy-start.6
  78.7 1.1 copy-start.3
  78.7 1.5 copy-start.4
  78.7 11.5 %collective-permute-start.15 = (bf16[256,512]{1,0:T(8,128)(2,1)}, bf16[256,512]{1,0:T(8,128)(2,1)S(1)}, u32[]{:S(2)}, u32[]{:S(2)}) collective-permute-start(bf16[256,512]{1,0:T(8,128)(2,1)} %get-tuple-element.82), channel_id=1, source_target_pairs={{0,16},{16,0},{32,48},{48,32},{64,80},{80,64},{96,112},{112,96},{1... | collective-permute-start | bytes 786440 | tf_op jit(solution)/shard_map/ppermute | solution.py:54
  92.5 8.8 %collective-permute-start.16 = (bf16[256,512]{1,0:T(8,128)(2,1)S(1)}, bf16[256,512]{1,0:T(8,128)(2,1)S(1)}, u32[]{:S(2)}, u32[]{:S(2)}) collective-permute-start(bf16[256,512]{1,0:T(8,128)(2,1)S(1)} %get-tuple-element.113), channel_id=1, source_target_pairs={{0,16},{16,0},{32,48},{48,32},{64,80},{80,64},{96,112},{112,96},{1... | collective-permute-start | bytes 786440 | tf_op jit(solution)/shard_map/ppermute | solution.py:54
  101.4 22.8 %collective-permute-start.19 = (bf16[512,1024]{1,0:T(8,128)(2,1)}, bf16[512,1024]{1,0:T(8,128)(2,1)S(1)}, u32[]{:S(2)}, u32[]{:S(2)}) collective-permute-start(bf16[512,1024]{1,0:T(8,128)(2,1)} %get-tuple-element.94), channel_id=1, source_target_pairs={{0,4},{1,5},{2,6},{3,7},{4,8},{5,9},{6,10},{7,11},{8,12},{9,13},{1... | collective-permute-start | bytes 3145736 | tf_op jit(solution)/shard_map/ppermute | solution.py:29
  101.4 22.8 %collective-permute-start.17 = (bf16[512,1024]{1,0:T(8,128)(2,1)}, bf16[512,1024]{1,0:T(8,128)(2,1)}, u32[]{:S(2)}, u32[]{:S(2)}) collective-permute-start(bf16[512,1024]{1,0:T(8,128)(2,1)} %get-tuple-element.90), channel_id=1, source_target_pairs={{0,2},{1,3},{2,0},{3,1},{4,6},{5,7},{6,4},{7,5},{8,10},{9,11},{10,... | collective-permute-start | bytes 3145736 | tf_op jit(solution)/shard_map/ppermute | solution.py:37
  104.2 20.0 %collective-permute-start.18 = (bf16[512,1024]{1,0:T(8,128)(2,1)}, bf16[512,1024]{1,0:T(8,128)(2,1)S(1)}, u32[]{:S(2)}, u32[]{:S(2)}) collective-permute-start(bf16[512,1024]{1,0:T(8,128)(2,1)} %get-tuple-element.92), channel_id=1, source_target_pairs={{0,12},{1,13},{2,14},{3,15},{4,0},{5,1},{6,2},{7,3},{8,4},{9,5},{1... | collective-permute-start | bytes 3145736 | tf_op jit(solution)/shard_map/ppermute | solution.py:33
  106.9 50.1 %copy-start.7 = (bf16[256,1024]{1,0:T(8,128)(2,1)}, bf16[256,1024]{1,0:T(8,128)(2,1)S(1)}, u32[]{:S(2)}) copy-start(bf16[256,1024]{1,0:T(8,128)(2,1)S(1)} %maximum_select_fusion.2.refs_0_) | copy-start | bytes 1572868
  106.9 17.2 %collective-permute-start.20 = (bf16[256,1024]{1,0:T(8,128)(2,1)S(1)}, bf16[256,1024]{1,0:T(8,128)(2,1)S(1)}, u32[]{:S(2)}, u32[]{:S(2)}) collective-permute-start(bf16[256,1024]{1,0:T(8,128)(2,1)S(1)} %maximum_select_fusion.2.refs_0_), channel_id=1, source_target_pairs={{0,64},{16,80},{32,96},{48,112},{64,0},{80,16},{96,32},{112,48},{1... | collective-permute-start | bytes 1572872 | tf_op jit(solution)/shard_map/ppermute | solution.py:50
  124.2 23.5 %copy-start.12 = (bf16[256,1024]{1,0:T(8,128)(2,1)}, bf16[256,1024]{1,0:T(8,128)(2,1)S(1)}, u32[]{:S(2)}) copy-start(bf16[256,1024]{1,0:T(8,128)(2,1)S(1)} %collective-permute-done.20.refs_2_) | copy-start | bytes 1572868
  124.2 12.9 %copy-start.8 = (bf16[512,1024]{1,0:T(8,128)(2,1)}, bf16[512,1024]{1,0:T(8,128)(2,1)S(1)}, u32[]{:S(2)}) copy-start(bf16[512,1024]{1,0:T(8,128)(2,1)S(1)} %collective-permute-done.19.refs_2_) | copy-start | bytes 3145732
  124.2 12.9 %copy-start.9 = (bf16[512,1024]{1,0:T(8,128)(2,1)}, bf16[512,1024]{1,0:T(8,128)(2,1)S(1)}, u32[]{:S(2)}) copy-start(bf16[512,1024]{1,0:T(8,128)(2,1)S(1)} %collective-permute-done.18.refs_1_) | copy-start | bytes 3145732
  127.9 29.1 %collective-permute-start.23 = (bf16[512,4096]{1,0:T(8,128)(2,1)}, bf16[512,4096]{1,0:T(8,128)(2,1)}, u32[]{:S(2)}, u32[]{:S(2)}) collective-permute-start(bf16[512,4096]{1,0:T(8,128)(2,1)} %get-tuple-element.107), channel_id=1, source_target_pairs={{0,1},{1,0},{2,3},{3,2},{4,5},{5,4},{6,7},{7,6},{8,9},{9,8},{10,11... | collective-permute-start | bytes 12582920 | tf_op jit(solution)/shard_map/ppermute | solution.py:41
  134.4 15.0 %collective-permute-start.22 = (bf16[256,1024]{1,0:T(8,128)(2,1)}, bf16[256,1024]{1,0:T(8,128)(2,1)S(1)}, u32[]{:S(2)}, u32[]{:S(2)}) collective-permute-start(bf16[256,1024]{1,0:T(8,128)(2,1)} %get-tuple-element.97), channel_id=1, source_target_pairs={{0,4},{1,5},{2,6},{3,7},{4,8},{5,9},{6,10},{7,11},{8,12},{9,13},{1... | collective-permute-start | bytes 1572872 | tf_op jit(solution)/shard_map/ppermute | solution.py:29
  134.4 15.0 %collective-permute-start.21 = (bf16[256,1024]{1,0:T(8,128)(2,1)}, bf16[256,1024]{1,0:T(8,128)(2,1)}, u32[]{:S(2)}, u32[]{:S(2)}) collective-permute-start(bf16[256,1024]{1,0:T(8,128)(2,1)} %get-tuple-element.96), channel_id=1, source_target_pairs={{0,12},{1,13},{2,14},{3,15},{4,0},{5,1},{6,2},{7,3},{8,4},{9,5},{1... | collective-permute-start | bytes 1572872 | tf_op jit(solution)/shard_map/ppermute | solution.py:33
  140.6 34.4 %collective-permute-start.28 = (bf16[512,1024]{1,0:T(8,128)(2,1)}, bf16[512,1024]{1,0:T(8,128)(2,1)S(1)}, u32[]{:S(2)}, u32[]{:S(2)}) collective-permute-start(bf16[512,1024]{1,0:T(8,128)(2,1)} %sum.1), channel_id=1, source_target_pairs={{0,2},{1,3},{2,0},{3,1},{4,6},{5,7},{6,4},{7,5},{8,10},{9,11},{10,... | collective-permute-start | bytes 3145736 | tf_op jit(solution)/shard_map/ppermute | solution.py:37
  149.4 0.8 copy-start.16
  152.6 25.4 %collective-permute-start.27 = (bf16[512,1024]{1,0:T(8,128)(2,1)}, bf16[512,1024]{1,0:T(8,128)(2,1)}, u32[]{:S(2)}, u32[]{:S(2)}) collective-permute-start(bf16[512,1024]{1,0:T(8,128)(2,1)} %get-tuple-element.104), channel_id=1, source_target_pairs={{0,4},{1,5},{2,6},{3,7},{4,8},{5,9},{6,10},{7,11},{8,12},{9,13},{1... | collective-permute-start | bytes 3145736 | tf_op jit(solution)/shard_map/ppermute | solution.py:29
  152.6 25.4 %collective-permute-start.26 = (bf16[512,1024]{1,0:T(8,128)(2,1)}, bf16[512,1024]{1,0:T(8,128)(2,1)}, u32[]{:S(2)}, u32[]{:S(2)}) collective-permute-start(bf16[512,1024]{1,0:T(8,128)(2,1)} %get-tuple-element.103), channel_id=1, source_target_pairs={{0,12},{1,13},{2,14},{3,15},{4,0},{5,1},{6,2},{7,3},{8,4},{9,5},{1... | collective-permute-start | bytes 3145736 | tf_op jit(solution)/shard_map/ppermute | solution.py:33
  155.3 12.9 %collective-permute-start.25 = (bf16[256,1024]{1,0:T(8,128)(2,1)S(1)}, bf16[256,1024]{1,0:T(8,128)(2,1)S(1)}, u32[]{:S(2)}, u32[]{:S(2)}) collective-permute-start(bf16[256,1024]{1,0:T(8,128)(2,1)S(1)} %maximum_select_fusion.2.refs_0_), channel_id=1, source_target_pairs={{0,96},{16,112},{32,0},{48,16},{64,32},{80,48},{96,64},{112,80},{1... | collective-permute-start | bytes 1572872 | tf_op jit(solution)/shard_map/ppermute | solution.py:50
  157.0 13.1 %collective-permute-start.24 = (bf16[256,1024]{1,0:T(8,128)(2,1)S(1)}, bf16[256,1024]{1,0:T(8,128)(2,1)S(1)}, u32[]{:S(2)}, u32[]{:S(2)}) collective-permute-start(bf16[256,1024]{1,0:T(8,128)(2,1)S(1)} %maximum_select_fusion.2.refs_0_), channel_id=1, source_target_pairs={{0,32},{16,48},{32,64},{48,80},{64,96},{80,112},{96,0},{112,16},{1... | collective-permute-start | bytes 1572872 | tf_op jit(solution)/shard_map/ppermute | solution.py:50
  168.2 9.9 %copy-start.10 = (bf16[512,1024]{1,0:T(8,128)(2,1)S(1)}, bf16[512,1024]{1,0:T(8,128)(2,1)}, u32[]{:S(2)}) copy-start(bf16[512,1024]{1,0:T(8,128)(2,1)} %get-tuple-element.112) | copy-start | bytes 3145732
  168.2 2.0 %copy-start.13 = (bf16[256,1024]{1,0:T(8,128)(2,1)}, bf16[256,1024]{1,0:T(8,128)(2,1)S(1)}, u32[]{:S(2)}) copy-start(bf16[256,1024]{1,0:T(8,128)(2,1)S(1)} %collective-permute-done.25.refs_3_) | copy-start | bytes 1572868
  170.2 0.8 copy-start.14
  175.0 3.0 %copy-start.11 = (bf16[512,1024]{1,0:T(8,128)(2,1)}, bf16[512,1024]{1,0:T(8,128)(2,1)S(1)}, u32[]{:S(2)}) copy-start(bf16[512,1024]{1,0:T(8,128)(2,1)S(1)} %collective-permute-done.28) | copy-start | bytes 3145732
  179.8 4.0 %collective-permute-start.29 = (f32[256,1024]{1,0:T(8,128)S(1)}, f32[256,1024]{1,0:T(8,128)S(1)}, u32[]{:S(2)}, u32[]{:S(2)}) collective-permute-start(f32[256,1024]{1,0:T(8,128)S(1)} %add_multiply_fusion), channel_id=1, source_target_pairs={{0,1},{1,0},{2,3},{3,2},{4,5},{5,4},{6,7},{7,6},{8,9},{9,8},{10,11... | collective-permute-start | bytes 3145736 | tf_op jit(solution)/shard_map/ppermute | solution.py:41

commit v5 on v4

--- a/solution.py
+++ b/solution.py
@@ -541,7 +541,7 @@
 
     give_rows = rows_of(1 - core, terms[0])
     keep_rows = rows_of(core, hold(terms[0], give_rows))
-    weight_grad = by_core(core, keep_rows, to_core(give_rows), 1)[None]
+    weight_grad = by_core(core, keep_rows, to_core(give_rows.astype(BF16)).astype(F32), 1)[None]
     return (input_grad, weight_grad, new_outer, new_momentum, new_inner)
 
 

time: 186 us -> 187 us (level)
  transfers between devices with their start and end apart: 30 -> 30, of which waited for: 9 -> 8; matrix products, arithmetic and copies ran while one was open for 3% -> 3% of each run, Pallas kernels for 46% -> 45%
where the time goes in v5:
time: 187 us
  Pallas kernels  88.4 us (47%)
  starting transfers between devices  45.7 us (24%)
  waiting for transfers between devices  33.9 us (18%)
  other arithmetic  12.3 us (7%)
  local copies, waits for them, and re-layouts  5.55 us (3%)
    pallas_call x3, Pallas kernels, pre_of(): pl.pallas_call(functools.partial(pre_kernel, factor, n, sums is not None,...  25.1 us
    pallas_call x1, Pallas kernels, late_of(): pl.pallas_call(functools.partial(late_kernel, n, offs, rows), grid_spec=p...  16.6 us
    ppermute x6, starting transfers between devices, to_zm(): return lax.ppermute(a, 'shard', shard_perm(-1, 0, 0))  15.7 us
    pallas_call x2, Pallas kernels, wgrad_of(): pl.pallas_call(functools.partial(wgrad_kernel, halves), grid_spec=pltpu.P...  15.1 us
    ppermute x5, waiting for transfers between devices, to_y(): return lax.ppermute(a, 'shard', shard_perm(0, 1, 0))  14 us
    pallas_call x1, Pallas kernels, igrad_of(): pl.pallas_call(functools.partial(igrad_kernel, factor, offs, feats // (NZ...  11.1 us
    ppermute x6, waiting for transfers between devices, to_zm(): return lax.ppermute(a, 'shard', shard_perm(-1, 0, 0))  10.4 us
    ppermute x5, starting transfers between devices, to_core(): return lax.ppermute(a, 'shard', shard_perm(0, 0, 1))  10.3 us
  transfers between devices with their start and end apart: 30, of which 8 were waited for; matrix products, arithmetic and copies ran while one was open for 3% of the time, Pallas kernels for 45%

profile of v5, /device:TPU:1, one launch (start us, length us, event | category | flops | bytes accessed | tf_op | source)
XLA Modules:
  0.0 186.8 jit_solution(11789054028028304216)
XLA Ops:
  0.7 1.3 dynamic-slice_bitcast_fusion.1
  1.9 1.5 collective-permute-start
  3.4 1.5 collective-permute-done
  5.0 0.5 maximum_select_fusion.1.refs_0_
  5.5 0.5 collective-permute-start.4
  5.9 0.1 collective-permute-start.5
  6.1 3.8 %collective-permute-start.3 = (bf16[512,1024]{1,0:T(8,128)(2,1)S(1)}, bf16[512,1024]{1,0:T(8,128)(2,1)S(1)}, u32[]{:S(2)}, u32[]{:S(2)}) collective-permute-start(bf16[512,1024]{1,0:T(8,128)(2,1)S(1)} %maximum_select_fusion.1.refs_0_), channel_id=1, source_target_pairs={{0,12},{1,13},{2,14},{3,15},{4,0},{5,1},{6,2},{7,3},{8,4},{9,5},{1... | collective-permute-start | bytes 3145736 | tf_op jit(solution)/shard_map/ppermute | solution.py:33
  9.9 2.9 %collective-permute-start.1 = (bf16[512,1024]{1,0:T(8,128)(2,1)S(1)}, bf16[512,1024]{1,0:T(8,128)(2,1)}, u32[]{:S(2)}, u32[]{:S(2)}) collective-permute-start(bf16[512,1024]{1,0:T(8,128)(2,1)S(1)} %maximum_select_fusion.1.refs_0_), channel_id=1, source_target_pairs={{0,2},{1,3},{2,0},{3,1},{4,6},{5,7},{6,4},{7,5},{8,10},{9,11},{10,... | collective-permute-start | bytes 3145736 | tf_op jit(solution)/shard_map/ppermute | solution.py:37
  12.8 0.7 stack.55.off_ref.pos_ref.blk_ref.s_ref
  13.5 6.8 %decode.1 = (bf16[256,1024]{1,0:T(8,128)(2,1)}, bf16[256,1024]{1,0:T(8,128)(2,1)}, bf16[256,1024]{1,0:T(8,128)(2,1)}, bf16[256,1024]{1,0:T(8,128)(2,1)}) custom-call(s32[19]{0:T(128)} %stack.55.off_ref.pos_ref.blk_ref.s_ref, f32[256,4096]{1,0:T(8,128)} %outer_ref, f32[1,256,4096]{2,1,0:T(8,128)} %inner_ref.1), custom_call_target="tpu_custom_call" | custom-call | flops 3145728 | bytes 3145728 | tf_op jit(solution)/shard_map/decode/pallas_call | solution.py:124
  20.4 1.3 collective-permute-start.6
  21.6 10.4 %collective-permute-done.3.refs_2_ = bf16[512,1024]{1,0:T(8,128)(2,1)S(1)} collective-permute-done((bf16[512,1024]{1,0:T(8,128)(2,1)S(1)}, bf16[512,1024]{1,0:T(8,128)(2,1)S(1)}, u32[]{:S(2)}, u32[]{:S(2)}) %collective-permute-start.3) | collective-permute-done | bytes 1048608 | tf_op jit(solution)/shard_map/ppermute | solution.py:33
  32.1 3.5 %collective-permute-done.1.refs_3_ = bf16[512,1024]{1,0:T(8,128)(2,1)} collective-permute-done((bf16[512,1024]{1,0:T(8,128)(2,1)S(1)}, bf16[512,1024]{1,0:T(8,128)(2,1)}, u32[]{:S(2)}, u32[]{:S(2)}) %collective-permute-start.1) | collective-permute-done | bytes 1048608 | tf_op jit(solution)/shard_map/ppermute | solution.py:37
  35.6 0.8 copy-done.13
  36.4 1.3 collective-permute-start.9
  37.7 0.0 collective-permute-done.2.refs_1_
  37.8 0.3 collective-permute-start.7
  38.0 2.7 %collective-permute-start.13 = (bf16[256,1024]{1,0:T(8,128)(2,1)}, bf16[256,1024]{1,0:T(8,128)(2,1)}, u32[]{:S(2)}, u32[]{:S(2)}) collective-permute-start(bf16[256,1024]{1,0:T(8,128)(2,1)} %get-tuple-element.79), channel_id=1, source_target_pairs={{0,64},{16,80},{32,96},{48,112},{64,0},{80,16},{96,32},{112,48},{1... | collective-permute-start | bytes 1572872 | tf_op jit(solution)/shard_map/ppermute | solution.py:50
  40.8 9.6 %pre.2 = (f32[512,1024]{1,0:T(8,128)}, f32[512,1024]{1,0:T(8,128)}) custom-call(s32[19]{0:T(128)} %stack.55.off_ref.pos_ref.blk_ref.s_ref, bf16[512,1024]{1,0:T(8,128)(2,1)} %copy-done, bf16[512,1024]{1,0:T(8,128)(2,1)} %copy-done.2, bf16[512,1024]{1,0:T(8,128)(2,1)} %copy-done.1, bf16[512,1024]{1,0:T(8,128)(2,1)} %collective-permute-done.1.refs_3_, ...), custom_call_target="tpu_custom_call" | custom-call | flops 1288490240 | bytes 3774873 | tf_op jit(solution)/shard_map/pre/pallas_call | solution.py:261
  50.4 0.2 collective-permute-start.8
  50.5 2.6 %collective-permute-start.10 = (bf16[512,1024]{1,0:T(8,128)(2,1)}, bf16[512,1024]{1,0:T(8,128)(2,1)S(1)}, u32[]{:S(2)}, u32[]{:S(2)}) collective-permute-start(bf16[512,1024]{1,0:T(8,128)(2,1)} %collective-permute-done.1.refs_3_), channel_id=1, source_target_pairs={{0,12},{1,13},{2,14},{3,15},{4,0},{5,1},{6,2},{7,3},{8,4},{9,5},{1... | collective-permute-start | bytes 3145736 | tf_op jit(solution)/shard_map/ppermute | solution.py:33
  53.1 2.8 %collective-permute-start.14 = (bf16[256,1024]{1,0:T(8,128)(2,1)}, bf16[256,1024]{1,0:T(8,128)(2,1)}, u32[]{:S(2)}, u32[]{:S(2)}) collective-permute-start(bf16[256,1024]{1,0:T(8,128)(2,1)} %get-tuple-element.81), channel_id=1, source_target_pairs={{0,96},{16,112},{32,0},{48,16},{64,32},{80,48},{96,64},{112,80},{1... | collective-permute-start | bytes 1572872 | tf_op jit(solution)/shard_map/ppermute | solution.py:50
  55.9 2.1 %collective-permute-start.11 = (bf16[256,1024]{1,0:T(8,128)(2,1)}, bf16[256,1024]{1,0:T(8,128)(2,1)S(1)}, u32[]{:S(2)}, u32[]{:S(2)}) collective-permute-start(bf16[256,1024]{1,0:T(8,128)(2,1)} %collective-permute-done.7.refs_0_.refs_4_), channel_id=1, source_target_pairs={{0,2},{1,3},{2,0},{3,1},{4,6},{5,7},{6,4},{7,5},{8,10},{9,11},{10,... | collective-permute-start | bytes 1572872 | tf_op jit(solution)/shard_map/ppermute | solution.py:37
  58.0 0.9 collective-permute-start.12
  58.9 1.1 constant_dynamic-slice_fusion
  60.0 5.5 %pre.3 = (f32[512,1024]{1,0:T(8,128)}, f32[512,1024]{1,0:T(8,128)}) custom-call(s32[19]{0:T(128)} %stack.55.off_ref.pos_ref.blk_ref.s_ref, bf16[256,1024]{1,0:T(8,128)(2,1)} %collective-permute-done.7.refs_0_.refs_4_, bf16[256,1024]{1,0:T(8,128)(2,1)} %collective-permute-done.9.refs_1_.refs_5_, bf16[512,4096]{1,0:T(8,128)(2,1)} %xo_ref.5, ...), custom_call_target="tpu_custom_call" | custom-call | flops 322122560 | bytes 1887436 | tf_op jit(solution)/shard_map/pre/pallas_call | solution.py:261
  65.5 2.7 %add_convert_fusion = (bf16[256,512]{1,0:T(8,128)(2,1)}, f32[256,512]{1,0:T(8,128)}) fusion(bf16[256,1024]{1,0:T(8,128)(2,1)} %collective-permute-done.14, s32[]{:T(128)S(6)} %select_n.152, bf16[256,1024]{1,0:T(8,128)(2,1)} %collective-permute-done.13, bf16[256,1024]{1,0:T(8,128)(2,1)} %copy-done.13, bf16[256,1024]{1,0:T(8,128)(2,1)} %get-tuple-element.77, ...), kind=kLoop, calls=%fused_computation.9 | loop fusion | flops 1966080 | bytes 2883592 | tf_op jit(solution)/shard_map/convert_element_type | solution.py:496
  68.2 10.5 %collective-permute-done.12.refs_3_.refs_9_ = bf16[256,1024]{1,0:T(8,128)(2,1)S(1)} collective-permute-done((bf16[256,1024]{1,0:T(8,128)(2,1)}, bf16[256,1024]{1,0:T(8,128)(2,1)S(1)}, u32[]{:S(2)}, u32[]{:S(2)}) %collective-permute-start.12) | collective-permute-done | bytes 524320 | tf_op jit(solution)/shard_map/ppermute | solution.py:37
  78.7 0.0 copy-start.4
  78.7 0.7 collective-permute-start.15
  79.3 0.1 copy-done.6
  79.5 0.3 copy-done.3
  79.8 0.3 copy-done.4
  80.1 10.0 %slope.1 = (bf16[512,1024]{1,0:T(8,128)(2,1)}, bf16[512,1024]{1,0:T(8,128)(2,1)}) custom-call(s32[19]{0:T(128)} %stack.55.off_ref.pos_ref.blk_ref.s_ref, bf16[512,1024]{1,0:T(8,128)(2,1)} %copy-done.3, bf16[512,1024]{1,0:T(8,128)(2,1)} %copy-done.4, bf16[256,1024]{1,0:T(8,128)(2,1)} %copy-done.5, bf16[256,1024]{1,0:T(8,128)(2,1)} %copy-done.6, ...), custom_call_target="tpu_custom_call" | custom-call | flops 966367616 | bytes 3145728 | tf_op jit(solution)/shard_map/slope/pallas_call | solution.py:261
  90.2 2.4 %fusion = (bf16[256,512]{1,0:T(8,128)(2,1)S(1)}, f32[256,512]{1,0:T(8,128)}, f32[256,512]{1,0:T(8,128)}) fusion(f32[256,512]{1,0:T(8,128)S(1)} %constant_dynamic-slice_fusion, f32[256,512]{1,0:T(8,128)} %get-tuple-element.117, bf16[256,512]{1,0:T(8,128)(2,1)S(1)} %collective-permute-done.15, f32[256,512]{1,0:T(8,128)} %param.11), kind=kLoop, calls=%fused_computation.14 | loop fusion | flops 1310720 | bytes 3145728 | tf_op jit(solution)/shard_map/convert_element_type | solution.py:506
  92.6 0.4 collective-permute-start.16
  93.0 8.4 %wgrad.2 = (bf16[512,1024]{1,0:T(8,128)(2,1)}, bf16[512,1024]{1,0:T(8,128)(2,1)}, bf16[512,1024]{1,0:T(8,128)(2,1)}) custom-call(s32[19]{0:T(128)} %stack.55.off_ref.pos_ref.blk_ref.s_ref, bf16[512,4096]{1,0:T(8,128)(2,1)} %xo_ref.5, bf16[512,4096]{1,0:T(8,128)(2,1)} %collective-permute-done.4.refs_8_.refs_9_.refs_10_.refs_11_.refs_4_.refs_5_.xp_ref, ...), custom_call_target="tpu_custom_call" | custom-call | flops 966367616 | bytes 1887436 | tf_op jit(solution)/shard_map/wgrad/pallas_call | solution.py:302
  101.4 2.9 %collective-permute-start.17 = (bf16[512,1024]{1,0:T(8,128)(2,1)}, bf16[512,1024]{1,0:T(8,128)(2,1)}, u32[]{:S(2)}, u32[]{:S(2)}) collective-permute-start(bf16[512,1024]{1,0:T(8,128)(2,1)} %get-tuple-element.90), channel_id=1, source_target_pairs={{0,2},{1,3},{2,0},{3,1},{4,6},{5,7},{6,4},{7,5},{8,10},{9,11},{10,... | collective-permute-start | bytes 3145736 | tf_op jit(solution)/shard_map/ppermute | solution.py:37
  104.3 2.6 %collective-permute-start.18 = (bf16[512,1024]{1,0:T(8,128)(2,1)}, bf16[512,1024]{1,0:T(8,128)(2,1)S(1)}, u32[]{:S(2)}, u32[]{:S(2)}) collective-permute-start(bf16[512,1024]{1,0:T(8,128)(2,1)} %get-tuple-element.92), channel_id=1, source_target_pairs={{0,12},{1,13},{2,14},{3,15},{4,0},{5,1},{6,2},{7,3},{8,4},{9,5},{1... | collective-permute-start | bytes 3145736 | tf_op jit(solution)/shard_map/ppermute | solution.py:33
  106.9 0.1 maximum_select_fusion.2.refs_0_
  107.0 0.6 collective-permute-start.20
  107.6 16.6 %late.1 = (bf16[512,1024]{1,0:T(8,128)(2,1)}, bf16[512,1024]{1,0:T(8,128)(2,1)}, bf16[512,1024]{1,0:T(8,128)(2,1)}, bf16[512,4096]{1,0:T(8,128)(2,1)}) custom-call(s32[19]{0:T(128)} %stack.55.off_ref.pos_ref.blk_ref.s_ref, bf16[512,4096]{1,0:T(8,128)(2,1)} %xo_ref.5, ...), custom_call_target="tpu_custom_call" | custom-call | flops 2254857728 | bytes 7549747 | tf_op jit(solution)/shard_map/late/pallas_call | solution.py:355
  124.3 3.7 %halves.1 = (bf16[256,1024]{1,0:T(8,128)(2,1)}, bf16[256,1024]{1,0:T(8,128)(2,1)}) custom-call(bf16[512,1024]{1,0:T(8,128)(2,1)} %get-tuple-element.89.a_ref, bf16[512,1024]{1,0:T(8,128)(2,1)} %collective-permute-done.17.b_ref), custom_call_target="tpu_custom_call" | custom-call | flops 157286 | bytes 943718 | tf_op jit(solution)/shard_map/halves/pallas_call | solution.py:208
  128.0 6.5 %collective-permute-start.23 = (bf16[512,4096]{1,0:T(8,128)(2,1)}, bf16[512,4096]{1,0:T(8,128)(2,1)}, u32[]{:S(2)}, u32[]{:S(2)}) collective-permute-start(bf16[512,4096]{1,0:T(8,128)(2,1)} %get-tuple-element.107), channel_id=1, source_target_pairs={{0,1},{1,0},{2,3},{3,2},{4,5},{5,4},{6,7},{7,6},{8,9},{9,8},{10,11... | collective-permute-start | bytes 12582920 | tf_op jit(solution)/shard_map/ppermute | solution.py:41
  134.5 2.7 %collective-permute-start.21 = (bf16[256,1024]{1,0:T(8,128)(2,1)}, bf16[256,1024]{1,0:T(8,128)(2,1)}, u32[]{:S(2)}, u32[]{:S(2)}) collective-permute-start(bf16[256,1024]{1,0:T(8,128)(2,1)} %get-tuple-element.96), channel_id=1, source_target_pairs={{0,12},{1,13},{2,14},{3,15},{4,0},{5,1},{6,2},{7,3},{8,4},{9,5},{1... | collective-permute-start | bytes 1572872 | tf_op jit(solution)/shard_map/ppermute | solution.py:33
  137.2 3.5 %sum.1 = bf16[512,1024]{1,0:T(8,128)(2,1)} custom-call(s32[19]{0:T(128)} %stack.55.off_ref.pos_ref.blk_ref.s_ref, bf16[512,1024]{1,0:T(8,128)(2,1)} %get-tuple-element.98.refs_0_, bf16[512,1024]{1,0:T(8,128)(2,1)} %copy-done.9, bf16[512,1024]{1,0:T(8,128)(2,1)} %copy-done.8), custom_call_target="tpu_custom_call" | custom-call | flops 471859 | bytes 1258291 | tf_op jit(solution)/shard_map/sum/pallas_call | solution.py:156
  140.7 0.3 collective-permute-start.28
  141.0 6.7 %wgrad.3 = (bf16[512,1024]{1,0:T(8,128)(2,1)}, bf16[512,1024]{1,0:T(8,128)(2,1)}) custom-call(s32[19]{0:T(128)} %stack.55.off_ref.pos_ref.blk_ref.s_ref, bf16[512,4096]{1,0:T(8,128)(2,1)} %xo_ref.5, bf16[512,4096]{1,0:T(8,128)(2,1)} %collective-permute-done.4.refs_8_.refs_9_.refs_10_.refs_11_.refs_4_.refs_5_.xp_ref, ...), custom_call_target="tpu_custom_call" | custom-call | flops 644245120 | bytes 1258291 | tf_op jit(solution)/shard_map/wgrad/pallas_call | solution.py:302
  147.7 1.8 collective-permute-done.22.b_ref
  149.5 0.8 copy-done.14
  150.3 2.4 %fold.1 = (bf16[512,1024]{1,0:T(8,128)(2,1)}, bf16[512,1024]{1,0:T(8,128)(2,1)}) custom-call(bf16[512,1024]{1,0:T(8,128)(2,1)} %get-tuple-element.101.up_ref, bf16[256,1024]{1,0:T(8,128)(2,1)} %collective-permute-done.21.a_ref, bf16[512,1024]{1,0:T(8,128)(2,1)} %get-tuple-element.102.low_ref, ...), custom_call_target="tpu_custom_call", output_to_operand_aliasing={{0}: (0, {}), {1}: (2, {})} | custom-call | flops 157286 | bytes 943718 | tf_op jit(solution)/shard_map/fold/pallas_call | solution.py:180
  152.7 0.0 collective-permute-start.27
  152.7 2.7 %collective-permute-start.26 = (bf16[512,1024]{1,0:T(8,128)(2,1)}, bf16[512,1024]{1,0:T(8,128)(2,1)}, u32[]{:S(2)}, u32[]{:S(2)}) collective-permute-start(bf16[512,1024]{1,0:T(8,128)(2,1)} %get-tuple-element.103), channel_id=1, source_target_pairs={{0,12},{1,13},{2,14},{3,15},{4,0},{5,1},{6,2},{7,3},{8,4},{9,5},{1... | collective-permute-start | bytes 3145736 | tf_op jit(solution)/shard_map/ppermute | solution.py:33
  155.4 1.7 collective-permute-start.25
  157.1 11.1 %igrad.1 = bf16[512,4096]{1,0:T(8,128)(2,1)} custom-call(s32[19]{0:T(128)} %stack.55.off_ref.pos_ref.blk_ref.s_ref, bf16[512,1024]{1,0:T(8,128)(2,1)} %get-tuple-element.105.so_ref.s_ref, bf16[512,1024]{1,0:T(8,128)(2,1)} %copy-done, bf16[512,1024]{1,0:T(8,128)(2,1)} %copy-done.2, bf16[512,1024]{1,0:T(8,128)(2,1)} %copy-done.1, ...), custom_call_target="tpu_custom_call" | custom-call | flops 1288490240 | bytes 3774873 | tf_op jit(solution)/shard_map/igrad/pallas_call | solution.py:395
  168.2 2.0 %collective-permute-done.24.refs_1_ = bf16[256,1024]{1,0:T(8,128)(2,1)} collective-permute-done((bf16[256,1024]{1,0:T(8,128)(2,1)S(1)}, bf16[256,1024]{1,0:T(8,128)(2,1)}, u32[]{:S(2)}, u32[]{:S(2)}) %collective-permute-start.24) | collective-permute-done | bytes 524320 | tf_op jit(solution)/shard_map/ppermute | solution.py:50
  170.2 4.1 %place.1 = bf16[256,4096]{1,0:T(8,128)(2,1)} custom-call(s32[19]{0:T(128)} %stack.55.off_ref.pos_ref.blk_ref.s_ref, bf16[256,1024]{1,0:T(8,128)(2,1)} %copy-done.7, bf16[256,1024]{1,0:T(8,128)(2,1)} %collective-permute-done.24.refs_1_, bf16[256,1024]{1,0:T(8,128)(2,1)} %copy-done.11, bf16[256,1024]{1,0:T(8,128)(2,1)} %copy-done.12), custom_call_target="tpu_custom_call" | custom-call | bytes 1258291 | tf_op jit(solution)/shard_map/place/pallas_call | solution.py:432
  174.3 3.8 %collective-permute-done.27 = bf16[512,1024]{1,0:T(8,128)(2,1)} collective-permute-done((bf16[512,1024]{1,0:T(8,128)(2,1)}, bf16[512,1024]{1,0:T(8,128)(2,1)}, u32[]{:S(2)}, u32[]{:S(2)}) %collective-permute-start.27) | collective-permute-done | bytes 1048608 | tf_op jit(solution)/shard_map/ppermute | solution.py:29
  178.1 2.4 %add_multiply_fusion = bf16[256,1024]{1,0:T(8,128)(2,1)} fusion(bf16[512,1024]{1,0:T(8,128)(2,1)S(1)} %collective-permute-done.28, s32[]{:T(128)S(6)} %select_n.155, bf16[512,1024]{1,0:T(8,128)(2,1)} %collective-permute-done.27, bf16[512,1024]{1,0:T(8,128)(2,1)} %collective-permute-done.26, bf16[512,1024]{1,0:T(8,128)(2,1)S(1)} %copy-done.10), kind=kLoop, calls=%fused_computation.3 | loop fusion | flops 2359296 | bytes 2621444 | tf_op jit(solution)/shard_map/mul | solution.py:540
  180.5 1.7 collective-permute-start.29
  182.1 1.5 multiply_bitcast_fusion
  183.7 0.3 collective-permute-done.29
  184.0 1.1 bitcast_convert_fusion
  185.2 1.6 maximum_select_fusion
  (51 shorter events, 0.2 us)
Async XLA Ops:
  1.9 3.0 %collective-permute-start = (bf16[256,1024]{1,0:T(8,128)(2,1)S(1)}, bf16[256,1024]{1,0:T(8,128)(2,1)S(1)}, u32[]{:S(2)}, u32[]{:S(2)}) collective-permute-start(bf16[256,1024]{1,0:T(8,128)(2,1)S(1)} %get-tuple-element.119), channel_id=1, source_target_pairs={{0,1},{1,0},{2,3},{3,2},{4,5},{5,4},{6,7},{7,6},{8,9},{9,8},{10,11... | collective-permute-start | bytes 1572872 | tf_op jit(solution)/shard_map/ppermute | solution.py:41
  5.5 14.9 %copy-start = (bf16[512,1024]{1,0:T(8,128)(2,1)}, bf16[512,1024]{1,0:T(8,128)(2,1)S(1)}, u32[]{:S(2)}) copy-start(bf16[512,1024]{1,0:T(8,128)(2,1)S(1)} %maximum_select_fusion.1.refs_0_) | copy-start | bytes 3145732
  5.5 14.9 %collective-permute-start.4 = (bf16[512,4096]{1,0:T(8,128)(2,1)}, bf16[512,4096]{1,0:T(8,128)(2,1)}, u32[]{:S(2)}, u32[]{:S(2)}) collective-permute-start(bf16[512,4096]{1,0:T(8,128)(2,1)} %xo_ref.5), channel_id=1, source_target_pairs={{0,1},{1,0},{2,3},{3,2},{4,5},{5,4},{6,7},{7,6},{8,9},{9,8},{10,11... | collective-permute-start | bytes 12582920 | tf_op jit(solution)/shard_map/ppermute | solution.py:41
  5.9 14.4 %collective-permute-start.5 = (bf16[512,2048]{1,0:T(8,128)(2,1)}, bf16[512,2048]{1,0:T(8,128)(2,1)}, u32[]{:S(2)}, u32[]{:S(2)}) collective-permute-start(bf16[512,2048]{1,0:T(8,128)(2,1)} %refs_14_.1), channel_id=1, source_target_pairs={{0,1},{1,0},{2,3},{3,2},{4,5},{5,4},{6,7},{7,6},{8,9},{9,8},{10,11... | collective-permute-start | bytes 6291464 | tf_op jit(solution)/shard_map/ppermute | solution.py:41
  6.1 26.0 %collective-permute-start.3 = (bf16[512,1024]{1,0:T(8,128)(2,1)S(1)}, bf16[512,1024]{1,0:T(8,128)(2,1)S(1)}, u32[]{:S(2)}, u32[]{:S(2)}) collective-permute-start(bf16[512,1024]{1,0:T(8,128)(2,1)S(1)} %maximum_select_fusion.1.refs_0_), channel_id=1, source_target_pairs={{0,12},{1,13},{2,14},{3,15},{4,0},{5,1},{6,2},{7,3},{8,4},{9,5},{1... | collective-permute-start | bytes 3145736 | tf_op jit(solution)/shard_map/ppermute | solution.py:33
  9.9 25.7 %collective-permute-start.1 = (bf16[512,1024]{1,0:T(8,128)(2,1)S(1)}, bf16[512,1024]{1,0:T(8,128)(2,1)}, u32[]{:S(2)}, u32[]{:S(2)}) collective-permute-start(bf16[512,1024]{1,0:T(8,128)(2,1)S(1)} %maximum_select_fusion.1.refs_0_), channel_id=1, source_target_pairs={{0,2},{1,3},{2,0},{3,1},{4,6},{5,7},{6,4},{7,5},{8,10},{9,11},{10,... | collective-permute-start | bytes 3145736 | tf_op jit(solution)/shard_map/ppermute | solution.py:37
  12.8 24.9 %collective-permute-start.2 = (bf16[512,1024]{1,0:T(8,128)(2,1)S(1)}, bf16[512,1024]{1,0:T(8,128)(2,1)S(1)}, u32[]{:S(2)}, u32[]{:S(2)}) collective-permute-start(bf16[512,1024]{1,0:T(8,128)(2,1)S(1)} %maximum_select_fusion.1.refs_0_), channel_id=1, source_target_pairs={{0,4},{1,5},{2,6},{3,7},{4,8},{5,9},{6,10},{7,11},{8,12},{9,13},{1... | collective-permute-start | bytes 3145736 | tf_op jit(solution)/shard_map/ppermute | solution.py:29
  20.4 15.2 %collective-permute-start.6 = (bf16[256,1024]{1,0:T(8,128)(2,1)}, bf16[256,1024]{1,0:T(8,128)(2,1)S(1)}, u32[]{:S(2)}, u32[]{:S(2)}) collective-permute-start(bf16[256,1024]{1,0:T(8,128)(2,1)} %get-tuple-element.65), channel_id=1, source_target_pairs={{0,32},{16,48},{32,64},{48,80},{64,96},{80,112},{96,0},{112,16},{1... | collective-permute-start | bytes 1572872 | tf_op jit(solution)/shard_map/ppermute | solution.py:50
  32.1 8.7 %copy-start.1 = (bf16[512,1024]{1,0:T(8,128)(2,1)}, bf16[512,1024]{1,0:T(8,128)(2,1)S(1)}, u32[]{:S(2)}) copy-start(bf16[512,1024]{1,0:T(8,128)(2,1)S(1)} %collective-permute-done.3.refs_2_) | copy-start | bytes 3145732
  35.6 0.8 copy-start.13
  36.4 14.0 %collective-permute-start.9 = (bf16[256,1024]{1,0:T(8,128)(2,1)S(1)}, bf16[256,1024]{1,0:T(8,128)(2,1)}, u32[]{:S(2)}, u32[]{:S(2)}) collective-permute-start(bf16[256,1024]{1,0:T(8,128)(2,1)S(1)} %slice.7), channel_id=1, source_target_pairs={{0,12},{1,13},{2,14},{3,15},{4,0},{5,1},{6,2},{7,3},{8,4},{9,5},{1... | collective-permute-start | bytes 1572872 | tf_op jit(solution)/shard_map/ppermute | solution.py:33
  37.7 3.0 %copy-start.2 = (bf16[512,1024]{1,0:T(8,128)(2,1)}, bf16[512,1024]{1,0:T(8,128)(2,1)S(1)}, u32[]{:S(2)}) copy-start(bf16[512,1024]{1,0:T(8,128)(2,1)S(1)} %collective-permute-done.2.refs_1_) | copy-start | bytes 3145732
  37.8 12.6 %collective-permute-start.7 = (bf16[256,1024]{1,0:T(8,128)(2,1)S(1)}, bf16[256,1024]{1,0:T(8,128)(2,1)}, u32[]{:S(2)}, u32[]{:S(2)}) collective-permute-start(bf16[256,1024]{1,0:T(8,128)(2,1)S(1)} %slice.6), channel_id=1, source_target_pairs={{0,4},{1,5},{2,6},{3,7},{4,8},{5,9},{6,10},{7,11},{8,12},{9,13},{1... | collective-permute-start | bytes 1572872 | tf_op jit(solution)/shard_map/ppermute | solution.py:29
  38.0 19.9 %collective-permute-start.13 = (bf16[256,1024]{1,0:T(8,128)(2,1)}, bf16[256,1024]{1,0:T(8,128)(2,1)}, u32[]{:S(2)}, u32[]{:S(2)}) collective-permute-start(bf16[256,1024]{1,0:T(8,128)(2,1)} %get-tuple-element.79), channel_id=1, source_target_pairs={{0,64},{16,80},{32,96},{48,112},{64,0},{80,16},{96,32},{112,48},{1... | collective-permute-start | bytes 1572872 | tf_op jit(solution)/shard_map/ppermute | solution.py:50
  50.4 28.3 %collective-permute-start.8 = (bf16[512,1024]{1,0:T(8,128)(2,1)}, bf16[512,1024]{1,0:T(8,128)(2,1)S(1)}, u32[]{:S(2)}, u32[]{:S(2)}) collective-permute-start(bf16[512,1024]{1,0:T(8,128)(2,1)} %collective-permute-done.1.refs_3_), channel_id=1, source_target_pairs={{0,4},{1,5},{2,6},{3,7},{4,8},{5,9},{6,10},{7,11},{8,12},{9,13},{1... | collective-permute-start | bytes 3145736 | tf_op jit(solution)/shard_map/ppermute | solution.py:29
  50.5 28.1 %collective-permute-start.10 = (bf16[512,1024]{1,0:T(8,128)(2,1)}, bf16[512,1024]{1,0:T(8,128)(2,1)S(1)}, u32[]{:S(2)}, u32[]{:S(2)}) collective-permute-start(bf16[512,1024]{1,0:T(8,128)(2,1)} %collective-permute-done.1.refs_3_), channel_id=1, source_target_pairs={{0,12},{1,13},{2,14},{3,15},{4,0},{5,1},{6,2},{7,3},{8,4},{9,5},{1... | collective-permute-start | bytes 3145736 | tf_op jit(solution)/shard_map/ppermute | solution.py:33
  53.1 12.4 %collective-permute-start.14 = (bf16[256,1024]{1,0:T(8,128)(2,1)}, bf16[256,1024]{1,0:T(8,128)(2,1)}, u32[]{:S(2)}, u32[]{:S(2)}) collective-permute-start(bf16[256,1024]{1,0:T(8,128)(2,1)} %get-tuple-element.81), channel_id=1, source_target_pairs={{0,96},{16,112},{32,0},{48,16},{64,32},{80,48},{96,64},{112,80},{1... | collective-permute-start | bytes 1572872 | tf_op jit(solution)/shard_map/ppermute | solution.py:50
  55.9 12.3 %collective-permute-start.11 = (bf16[256,1024]{1,0:T(8,128)(2,1)}, bf16[256,1024]{1,0:T(8,128)(2,1)S(1)}, u32[]{:S(2)}, u32[]{:S(2)}) collective-permute-start(bf16[256,1024]{1,0:T(8,128)(2,1)} %collective-permute-done.7.refs_0_.refs_4_), channel_id=1, source_target_pairs={{0,2},{1,3},{2,0},{3,1},{4,6},{5,7},{6,4},{7,5},{8,10},{9,11},{10,... | collective-permute-start | bytes 1572872 | tf_op jit(solution)/shard_map/ppermute | solution.py:37
  58.0 20.7 %collective-permute-start.12 = (bf16[256,1024]{1,0:T(8,128)(2,1)}, bf16[256,1024]{1,0:T(8,128)(2,1)S(1)}, u32[]{:S(2)}, u32[]{:S(2)}) collective-permute-start(bf16[256,1024]{1,0:T(8,128)(2,1)} %collective-permute-done.9.refs_1_.refs_5_), channel_id=1, source_target_pairs={{0,2},{1,3},{2,0},{3,1},{4,6},{5,7},{6,4},{7,5},{8,10},{9,11},{10,... | collective-permute-start | bytes 1572872 | tf_op jit(solution)/shard_map/ppermute | solution.py:37
  68.2 11.2 %copy-start.5 = (bf16[256,1024]{1,0:T(8,128)(2,1)}, bf16[256,1024]{1,0:T(8,128)(2,1)S(1)}, u32[]{:S(2)}) copy-start(bf16[256,1024]{1,0:T(8,128)(2,1)S(1)} %collective-permute-done.11.refs_2_.refs_8_) | copy-start | bytes 1572868
  78.7 0.8 copy-start.6
  78.7 1.1 copy-start.3
  78.7 1.5 copy-start.4
  78.7 11.5 %collective-permute-start.15 = (bf16[256,512]{1,0:T(8,128)(2,1)}, bf16[256,512]{1,0:T(8,128)(2,1)S(1)}, u32[]{:S(2)}, u32[]{:S(2)}) collective-permute-start(bf16[256,512]{1,0:T(8,128)(2,1)} %get-tuple-element.82), channel_id=1, source_target_pairs={{0,16},{16,0},{32,48},{48,32},{64,80},{80,64},{96,112},{112,96},{1... | collective-permute-start | bytes 786440 | tf_op jit(solution)/shard_map/ppermute | solution.py:54
  92.6 8.8 %collective-permute-start.16 = (bf16[256,512]{1,0:T(8,128)(2,1)S(1)}, bf16[256,512]{1,0:T(8,128)(2,1)S(1)}, u32[]{:S(2)}, u32[]{:S(2)}) collective-permute-start(bf16[256,512]{1,0:T(8,128)(2,1)S(1)} %get-tuple-element.113), channel_id=1, source_target_pairs={{0,16},{16,0},{32,48},{48,32},{64,80},{80,64},{96,112},{112,96},{1... | collective-permute-start | bytes 786440 | tf_op jit(solution)/shard_map/ppermute | solution.py:54
  101.4 22.9 %collective-permute-start.19 = (bf16[512,1024]{1,0:T(8,128)(2,1)}, bf16[512,1024]{1,0:T(8,128)(2,1)S(1)}, u32[]{:S(2)}, u32[]{:S(2)}) collective-permute-start(bf16[512,1024]{1,0:T(8,128)(2,1)} %get-tuple-element.94), channel_id=1, source_target_pairs={{0,4},{1,5},{2,6},{3,7},{4,8},{5,9},{6,10},{7,11},{8,12},{9,13},{1... | collective-permute-start | bytes 3145736 | tf_op jit(solution)/shard_map/ppermute | solution.py:29
  101.4 22.9 %collective-permute-start.17 = (bf16[512,1024]{1,0:T(8,128)(2,1)}, bf16[512,1024]{1,0:T(8,128)(2,1)}, u32[]{:S(2)}, u32[]{:S(2)}) collective-permute-start(bf16[512,1024]{1,0:T(8,128)(2,1)} %get-tuple-element.90), channel_id=1, source_target_pairs={{0,2},{1,3},{2,0},{3,1},{4,6},{5,7},{6,4},{7,5},{8,10},{9,11},{10,... | collective-permute-start | bytes 3145736 | tf_op jit(solution)/shard_map/ppermute | solution.py:37
  104.3 20.0 %collective-permute-start.18 = (bf16[512,1024]{1,0:T(8,128)(2,1)}, bf16[512,1024]{1,0:T(8,128)(2,1)S(1)}, u32[]{:S(2)}, u32[]{:S(2)}) collective-permute-start(bf16[512,1024]{1,0:T(8,128)(2,1)} %get-tuple-element.92), channel_id=1, source_target_pairs={{0,12},{1,13},{2,14},{3,15},{4,0},{5,1},{6,2},{7,3},{8,4},{9,5},{1... | collective-permute-start | bytes 3145736 | tf_op jit(solution)/shard_map/ppermute | solution.py:33
  107.0 50.1 %copy-start.7 = (bf16[256,1024]{1,0:T(8,128)(2,1)}, bf16[256,1024]{1,0:T(8,128)(2,1)S(1)}, u32[]{:S(2)}) copy-start(bf16[256,1024]{1,0:T(8,128)(2,1)S(1)} %maximum_select_fusion.2.refs_0_) | copy-start | bytes 1572868
  107.0 17.2 %collective-permute-start.20 = (bf16[256,1024]{1,0:T(8,128)(2,1)S(1)}, bf16[256,1024]{1,0:T(8,128)(2,1)S(1)}, u32[]{:S(2)}, u32[]{:S(2)}) collective-permute-start(bf16[256,1024]{1,0:T(8,128)(2,1)S(1)} %maximum_select_fusion.2.refs_0_), channel_id=1, source_target_pairs={{0,64},{16,80},{32,96},{48,112},{64,0},{80,16},{96,32},{112,48},{1... | collective-permute-start | bytes 1572872 | tf_op jit(solution)/shard_map/ppermute | solution.py:50
  124.3 23.4 %copy-start.11 = (bf16[256,1024]{1,0:T(8,128)(2,1)}, bf16[256,1024]{1,0:T(8,128)(2,1)S(1)}, u32[]{:S(2)}) copy-start(bf16[256,1024]{1,0:T(8,128)(2,1)S(1)} %collective-permute-done.20.refs_2_) | copy-start | bytes 1572868
  124.3 12.9 %copy-start.8 = (bf16[512,1024]{1,0:T(8,128)(2,1)}, bf16[512,1024]{1,0:T(8,128)(2,1)S(1)}, u32[]{:S(2)}) copy-start(bf16[512,1024]{1,0:T(8,128)(2,1)S(1)} %collective-permute-done.19.refs_2_) | copy-start | bytes 3145732
  124.3 12.9 %copy-start.9 = (bf16[512,1024]{1,0:T(8,128)(2,1)}, bf16[512,1024]{1,0:T(8,128)(2,1)S(1)}, u32[]{:S(2)}) copy-start(bf16[512,1024]{1,0:T(8,128)(2,1)S(1)} %collective-permute-done.18.refs_1_) | copy-start | bytes 3145732
  128.0 29.1 %collective-permute-start.23 = (bf16[512,4096]{1,0:T(8,128)(2,1)}, bf16[512,4096]{1,0:T(8,128)(2,1)}, u32[]{:S(2)}, u32[]{:S(2)}) collective-permute-start(bf16[512,4096]{1,0:T(8,128)(2,1)} %get-tuple-element.107), channel_id=1, source_target_pairs={{0,1},{1,0},{2,3},{3,2},{4,5},{5,4},{6,7},{7,6},{8,9},{9,8},{10,11... | collective-permute-start | bytes 12582920 | tf_op jit(solution)/shard_map/ppermute | solution.py:41
  134.5 15.0 %collective-permute-start.22 = (bf16[256,1024]{1,0:T(8,128)(2,1)}, bf16[256,1024]{1,0:T(8,128)(2,1)S(1)}, u32[]{:S(2)}, u32[]{:S(2)}) collective-permute-start(bf16[256,1024]{1,0:T(8,128)(2,1)} %get-tuple-element.97), channel_id=1, source_target_pairs={{0,4},{1,5},{2,6},{3,7},{4,8},{5,9},{6,10},{7,11},{8,12},{9,13},{1... | collective-permute-start | bytes 1572872 | tf_op jit(solution)/shard_map/ppermute | solution.py:29
  134.5 15.0 %collective-permute-start.21 = (bf16[256,1024]{1,0:T(8,128)(2,1)}, bf16[256,1024]{1,0:T(8,128)(2,1)}, u32[]{:S(2)}, u32[]{:S(2)}) collective-permute-start(bf16[256,1024]{1,0:T(8,128)(2,1)} %get-tuple-element.96), channel_id=1, source_target_pairs={{0,12},{1,13},{2,14},{3,15},{4,0},{5,1},{6,2},{7,3},{8,4},{9,5},{1... | collective-permute-start | bytes 1572872 | tf_op jit(solution)/shard_map/ppermute | solution.py:33
  140.7 33.6 %collective-permute-start.28 = (bf16[512,1024]{1,0:T(8,128)(2,1)}, bf16[512,1024]{1,0:T(8,128)(2,1)S(1)}, u32[]{:S(2)}, u32[]{:S(2)}) collective-permute-start(bf16[512,1024]{1,0:T(8,128)(2,1)} %sum.1), channel_id=1, source_target_pairs={{0,2},{1,3},{2,0},{3,1},{4,6},{5,7},{6,4},{7,5},{8,10},{9,11},{10,... | collective-permute-start | bytes 3145736 | tf_op jit(solution)/shard_map/ppermute | solution.py:37
  149.5 0.8 copy-start.14
  152.7 25.4 %collective-permute-start.27 = (bf16[512,1024]{1,0:T(8,128)(2,1)}, bf16[512,1024]{1,0:T(8,128)(2,1)}, u32[]{:S(2)}, u32[]{:S(2)}) collective-permute-start(bf16[512,1024]{1,0:T(8,128)(2,1)} %get-tuple-element.104), channel_id=1, source_target_pairs={{0,4},{1,5},{2,6},{3,7},{4,8},{5,9},{6,10},{7,11},{8,12},{9,13},{1... | collective-permute-start | bytes 3145736 | tf_op jit(solution)/shard_map/ppermute | solution.py:29
  152.7 25.4 %collective-permute-start.26 = (bf16[512,1024]{1,0:T(8,128)(2,1)}, bf16[512,1024]{1,0:T(8,128)(2,1)}, u32[]{:S(2)}, u32[]{:S(2)}) collective-permute-start(bf16[512,1024]{1,0:T(8,128)(2,1)} %get-tuple-element.103), channel_id=1, source_target_pairs={{0,12},{1,13},{2,14},{3,15},{4,0},{5,1},{6,2},{7,3},{8,4},{9,5},{1... | collective-permute-start | bytes 3145736 | tf_op jit(solution)/shard_map/ppermute | solution.py:33
  155.4 12.9 %collective-permute-start.25 = (bf16[256,1024]{1,0:T(8,128)(2,1)S(1)}, bf16[256,1024]{1,0:T(8,128)(2,1)S(1)}, u32[]{:S(2)}, u32[]{:S(2)}) collective-permute-start(bf16[256,1024]{1,0:T(8,128)(2,1)S(1)} %maximum_select_fusion.2.refs_0_), channel_id=1, source_target_pairs={{0,96},{16,112},{32,0},{48,16},{64,32},{80,48},{96,64},{112,80},{1... | collective-permute-start | bytes 1572872 | tf_op jit(solution)/shard_map/ppermute | solution.py:50
  157.1 13.1 %collective-permute-start.24 = (bf16[256,1024]{1,0:T(8,128)(2,1)S(1)}, bf16[256,1024]{1,0:T(8,128)(2,1)}, u32[]{:S(2)}, u32[]{:S(2)}) collective-permute-start(bf16[256,1024]{1,0:T(8,128)(2,1)S(1)} %maximum_select_fusion.2.refs_0_), channel_id=1, source_target_pairs={{0,32},{16,48},{32,64},{48,80},{64,96},{80,112},{96,0},{112,16},{1... | collective-permute-start | bytes 1572872 | tf_op jit(solution)/shard_map/ppermute | solution.py:50
  168.2 9.9 %copy-start.10 = (bf16[512,1024]{1,0:T(8,128)(2,1)S(1)}, bf16[512,1024]{1,0:T(8,128)(2,1)}, u32[]{:S(2)}) copy-start(bf16[512,1024]{1,0:T(8,128)(2,1)} %get-tuple-element.112) | copy-start | bytes 3145732
  168.2 2.0 %copy-start.12 = (bf16[256,1024]{1,0:T(8,128)(2,1)}, bf16[256,1024]{1,0:T(8,128)(2,1)S(1)}, u32[]{:S(2)}) copy-start(bf16[256,1024]{1,0:T(8,128)(2,1)S(1)} %collective-permute-done.25.refs_3_) | copy-start | bytes 1572868
  180.5 3.6 %collective-permute-start.29 = (bf16[256,1024]{1,0:T(8,128)(2,1)}, bf16[256,1024]{1,0:T(8,128)(2,1)}, u32[]{:S(2)}, u32[]{:S(2)}) collective-permute-start(bf16[256,1024]{1,0:T(8,128)(2,1)} %add_multiply_fusion), channel_id=1, source_target_pairs={{0,1},{1,0},{2,3},{3,2},{4,5},{5,4},{6,7},{7,6},{8,9},{9,8},{10,11... | collective-permute-start | bytes 1572872 | tf_op jit(solution)/shard_map/ppermute | solution.py:41
